TPU v7x, 512 devices: a whole 4x4x16 slice. The times are simulated.
512 devices in a mesh: seq: 64 (over z, x_hi, core), dp: 8 (over y, x_lo).
Axes of the slice: x: 4 (x_hi: 2, x_lo: 2; x = x_hi * 2 + x_lo), y: 4, z: 16, core: 2. Of those that a mesh axis runs over, the one named last changes fastest.
Arguments:
- inputs: bfloat16 [8, 65536, 512], P('dp', 'seq'), may hold values from -16 to 16
- out_grad: bfloat16 [8, 65536, 512], P('dp', 'seq'), may hold values from -6 to 6
- first_factor: bfloat16 [128, 512, 512], P('seq', 'dp'), may hold values from -0.25 to 0.25
- second_factor: bfloat16 [512, 128, 128], P('seq', 'dp'), may hold values from -0.5 to 0.5
- gate_weight: bfloat16 [512, 512], P('seq', 'dp'), may hold values from -0.25 to 0.25
Outputs:
- grad_inputs: bfloat16 [8, 65536, 512], P('dp', 'seq')
- grad_first: float32 [128, 512, 512], P('seq', 'dp')
- grad_second: float32 [512, 128, 128], P('seq', 'dp')
- grad_gate: float32 [512, 512], P('seq', 'dp')
All inputs are finite; a program needn't handle non-finite values.
Results may differ from a plain program's by a relative error of at most 0.006.
Values may be sent and summed in bfloat16 or wider, within the bound.
No kernel may reach another device: no remote copies, remote signals or barrier semaphores. Data moves between devices by JAX's collectives and lax.ppermute only.
A program may use at most 64 MiB of HBM per device.

v0:
```python
import jax
import jax.numpy as jnp
from jax import lax
from jax.sharding import PartitionSpec as P


def mix_columns(factor, column_one, column_grad):
    column_two = jnp.einsum(
        "jpq,sqjd->spjd", factor, column_one, preferred_element_type=jnp.float32
    ).astype(jnp.bfloat16)
    column_back = jnp.einsum(
        "jpq,spjd->sqjd", factor, column_grad, preferred_element_type=jnp.float32
    ).astype(jnp.bfloat16)
    second_part = jnp.einsum(
        "spjd,sqjd->jpq", column_grad, column_one, preferred_element_type=jnp.float32
    )
    return (column_two, column_back, second_part)


def per_device(inputs, out_grad, first_factor, second_factor, gate_weight):
    count, rows, width = inputs.shape
    first_full, second_full, gate_half = (
        lax.all_gather(first_factor, "dp", axis=1, tiled=True),
        lax.all_gather(second_factor, "dp", axis=1, tiled=True),
        lax.all_gather(gate_weight, "dp", axis=1, tiled=True),
    )
    gate_full = lax.all_gather(gate_half, "seq", axis=0, tiled=True)
    blocks = first_full.shape[0]
    length = first_full.shape[1]
    blocked = inputs.reshape(count, blocks, length, width)
    cotangent = out_grad.reshape(count, blocks, length, width)
    mixed_one = jnp.einsum(
        "bjk,sbkd->sbjd", first_full, blocked, preferred_element_type=jnp.float32
    ).astype(jnp.bfloat16)
    flat_inputs = inputs.reshape(-1, width)
    gate = jax.nn.sigmoid(
        jnp.dot(flat_inputs, gate_full, preferred_element_type=jnp.float32)
    ).reshape(blocked.shape)
    mixed_grad = (cotangent.astype(jnp.float32) * gate).astype(jnp.bfloat16)
    column_one, column_grad = (
        lax.all_to_all(mixed_one, "seq", split_axis=2, concat_axis=1, tiled=True),
        lax.all_to_all(mixed_grad, "seq", split_axis=2, concat_axis=1, tiled=True),
    )
    column_two, column_back, second_part = mix_columns(second_full, column_one, column_grad)
    mixed_two, back_one = (
        lax.all_to_all(column_two, "seq", split_axis=1, concat_axis=2, tiled=True),
        lax.all_to_all(column_back, "seq", split_axis=1, concat_axis=2, tiled=True),
    )
    gate_delta = (
        cotangent.astype(jnp.float32) * mixed_two.astype(jnp.float32) * gate * (1.0 - gate)
    ).astype(jnp.bfloat16)
    flat_delta = gate_delta.reshape(-1, width)
    gate_part = jnp.dot(flat_inputs.T, flat_delta, preferred_element_type=jnp.float32)
    gate_input = (
        jnp.dot(flat_delta, gate_full.T, preferred_element_type=jnp.float32)
        .astype(jnp.bfloat16)
        .reshape(blocked.shape)
    )
    first_part = jnp.einsum("sbjd,sbkd->bjk", back_one, blocked, preferred_element_type=jnp.float32)
    through = jnp.einsum("bjk,sbjd->sbkd", first_full, back_one, preferred_element_type=jnp.float32)
    grad_inputs = (
        (through + gate_input.astype(jnp.float32)).astype(jnp.bfloat16).reshape(count, rows, width)
    )
    grad_first, grad_second, grad_gate = (
        lax.psum_scatter(first_part, "dp", scatter_dimension=1, tiled=True),
        lax.psum_scatter(second_part, "dp", scatter_dimension=1, tiled=True),
        lax.psum_scatter(gate_part, "dp", scatter_dimension=1, tiled=True),
    )
    grad_gate = lax.psum_scatter(grad_gate, "seq", scatter_dimension=0, tiled=True)
    return (grad_inputs, grad_first, grad_second, grad_gate)


def solution(mesh):
    return jax.shard_map(
        per_device,
        mesh=mesh,
        in_specs=(
            P("dp", "seq", None),
            P("dp", "seq", None),
            P("seq", "dp", None),
            P("seq", "dp", None),
            P("seq", "dp"),
        ),
        out_specs=(
            P("dp", "seq", None),
            P("seq", "dp", None),
            P("seq", "dp", None),
            P("seq", "dp"),
        ),
        check_vma=False,
    )
```

profile of v0, /device:TPU:1, one launch (start us, length us, event | category | flops | bytes accessed | tf_op | source)
XLA Modules:
  0.0 986.5 jit_solution(11484518269084112097)
XLA Ops:
  7.9 50.7 %all-gather.3.cloned.1.call-done = bf16[2,512,512]{2,1,0:T(8,128)(2,1)} async-done(((bf16[2,64,512]{2,1,0:T(8,128)(2,1)}), bf16[2,512,512]{2,1,0:T(8,128)(2,1)}) %all-gather.3.cloned.1.call-update) | async-done | bytes 1048592 | tf_op jit(solution)/shard_map/all_gather | solution.py:23
  58.6 2.1 fusion.5
  60.7 2.1 copy.71
  62.8 20.4 %all-to-all-start.2 = ((bf16[1,2,512,512]{3,1,0,2:T(2,128)(2,1)}), bf16[1,2,512,512]{3,1,0,2:T(2,128)(2,1)S(1)}, u32[]{:S(2)}, u32[]{:S(2)}) async-start(bf16[1,2,512,512]{3,1,0,2:T(2,128)(2,1)} %copy.71), calls=%async_computation.2 | async-start | bytes 2097152 | tf_op jit(solution)/shard_map/all_to_all | solution.py:41
  83.3 24.9 %all_gather.14 = bf16[8,128,128]{2,1,0:T(8,128)(2,1)S(1)} all-gather(bf16[8,16,128]{2,1,0:T(8,128)(2,1)S(1)} %copy-done.5), channel_id=1, replica_groups=mesh['seq'=64,'dp'=8] {'dp'}, dimensions={1}, use_global_device_ids=true | all-gather | bytes 294912 | tf_op jit(solution)/shard_map/all_gather | solution.py:24
  108.2 29.2 %all-to-all-done.2 = bf16[1,2,512,512]{3,1,0,2:T(2,128)(2,1)S(1)} async-done(((bf16[1,2,512,512]{3,1,0,2:T(2,128)(2,1)}), bf16[1,2,512,512]{3,1,0,2:T(2,128)(2,1)S(1)}, u32[]{:S(2)}, u32[]{:S(2)}) %all-to-all-start.2) | async-done | bytes 1048608 | tf_op jit(solution)/shard_map/all_to_all | solution.py:41
  138.3 1.7 copy.75
  140.0 7.4 all-to-all-start.3
  147.4 20.7 %all-gather = bf16[8,64,8]{1,2,0:T(8,128)(2,1)S(1)} all-gather(bf16[1,64,8]{1,2,0:T(8,128)(2,1)S(1)} %bitcast.99), channel_id=1, replica_groups=mesh['seq'=64,'dp'=8] {'dp'}, dimensions={0}, use_global_device_ids=true | all-gather | bytes 9216 | tf_op jit(solution)/shard_map/all_gather | solution.py:25
  168.2 99.1 %all_gather.13 = bf16[512,512]{1,0:T(8,128)(2,1)} all-gather(bf16[8,512]{1,0:T(8,128)(2,1)S(1)} %bitcast.98), channel_id=1, replica_groups=mesh['seq'=64,'dp'=8] {'seq'}, dimensions={0}, use_global_device_ids=true | all-gather | bytes 532480 | tf_op jit(solution)/shard_map/all_gather | solution.py:27
  269.0 2.1 fusion.3
  272.5 68.3 %all_to_all.54 = bf16[1,2,512,512]{3,1,0,2:T(2,128)(2,1)S(1)} all-to-all(bf16[1,2,512,512]{3,1,0,2:T(2,128)(2,1)S(1)} %copy.64), channel_id=1, replica_groups=mesh['seq'=64,'dp'=8] {'seq'}, dimensions={2} | all-to-all | bytes 2097152 | tf_op jit(solution)/shard_map/all_to_all | solution.py:42
  341.2 1.6 fusion.4
  342.8 2.7 copy.68
  345.5 7.6 all-to-all-start.1
  353.3 3.0 convolution_bitcast_fusion
  356.4 46.7 %reduce-scatter.9.cloned.1.call-done = f32[512,64]{0,1:T(8,128)} async-done(((f32[512,512]{0,1:T(8,128)}), f32[512,64]{0,1:T(8,128)}) %reduce-scatter.9.cloned.1.call-update) | async-done | bytes 131088 | tf_op jit(solution)/shard_map/reduce_scatter | solution.py:67
  404.7 2.4 all-to-all-done.1
  407.1 3.3 fusion.7
  412.5 2.9 convolution_convert_fusion.3
  415.4 456.4 %all-reduce.3.cloned.1.call-done = f32[512,64]{0,1:T(8,128)} async-done(((f32[512,64]{0,1:T(8,128)}), f32[512,64]{0,1:T(8,128)}) %all-reduce.3.cloned.1.call-update) | async-done | bytes 131088
  873.3 3.3 fusion
  876.7 36.7 %reduce-scatter.7.cloned.1.call-done = f32[8,16,128]{2,1,0:T(8,128)} async-done(((f32[8,128,128]{2,1,0:T(8,128)}), f32[8,16,128]{2,1,0:T(8,128)}) %reduce-scatter.7.cloned.1.call-update) | async-done | bytes 65552 | tf_op jit(solution)/shard_map/reduce_scatter | solution.py:66
  913.3 66.6 %reduce-scatter.5.cloned.1.call-done = f32[2,64,512]{2,1,0:T(8,128)} async-done(((f32[2,512,512]{2,1,0:T(8,128)}), f32[2,64,512]{2,1,0:T(8,128)}) %reduce-scatter.5.cloned.1.call-update) | async-done | bytes 262160 | tf_op jit(solution)/shard_map/reduce_scatter | solution.py:65
  (40 shorter events, 10.0 us)
Async XLA Ops:
  7.2 51.4 %copy-start = (bf16[1,1024,512]{2,1,0:T(8,128)(2,1)S(1)}, bf16[1,1024,512]{2,1,0:T(8,128)(2,1)}, u32[]{:S(2)}) copy-start(bf16[1,1024,512]{2,1,0:T(8,128)(2,1)} %param.5) | copy-start | bytes 3145732
  7.2 51.4 %all-gather.3.cloned.1.call-start = ((), (), s32[]{:S(2)}) async-start(), calls=%async_computation.7 | async-start | bytes 1179648 | tf_op jit(solution)/shard_map/all_gather | solution.py:23
  60.7 22.6 %copy-start.5 = (bf16[8,16,128]{2,1,0:T(8,128)(2,1)S(1)}, bf16[8,16,128]{2,1,0:T(8,128)(2,1)}, u32[]{:S(2)}) copy-start(bf16[8,16,128]{2,1,0:T(8,128)(2,1)} %param.8) | copy-start | bytes 98308
  62.8 74.5 %all-to-all-start.2 = ((bf16[1,2,512,512]{3,1,0,2:T(2,128)(2,1)}), bf16[1,2,512,512]{3,1,0,2:T(2,128)(2,1)S(1)}, u32[]{:S(2)}, u32[]{:S(2)}) async-start(bf16[1,2,512,512]{3,1,0,2:T(2,128)(2,1)} %copy.71), calls=%async_computation.2 | async-start | bytes 2097152 | tf_op jit(solution)/shard_map/all_to_all | solution.py:41
  138.3 9.1 copy-start.6
  140.0 127.3 %all-to-all-start.3 = ((bf16[1,128,8,512]{3,2,0,1:T(8,128)(2,1)}), bf16[1,128,8,512]{3,2,0,1:T(8,128)(2,1)S(1)}, u32[]{:S(2)}, u32[]{:S(2)}) async-start(bf16[1,128,8,512]{3,2,0,1:T(8,128)(2,1)} %copy.75), calls=%async_computation.3 | async-start | bytes 2097152 | tf_op jit(solution)/shard_map/all_to_all | solution.py:46
  267.6 1.2 copy-start.2
  267.7 1.4 copy-start.3
  345.5 61.5 %all-to-all-start.1 = ((bf16[1,128,8,512]{3,2,0,1:T(8,128)(2,1)}), bf16[1,128,8,512]{3,2,0,1:T(8,128)(2,1)}, u32[]{:S(2)}, u32[]{:S(2)}) async-start(bf16[1,128,8,512]{3,2,0,1:T(8,128)(2,1)} %copy.68), calls=%async_computation.1 | async-start | bytes 2097152 | tf_op jit(solution)/shard_map/all_to_all | solution.py:47
  353.1 49.9 %reduce-scatter.9.cloned.1.call-start = ((), (), s32[]{:S(2)}) async-start(), calls=%async_computation.10 | async-start | bytes 1179648 | tf_op jit(solution)/shard_map/reduce_scatter | solution.py:67
  356.3 515.5 %all-reduce.3.cloned.1.call-start = ((), (), s32[]{:S(2)}) async-start(), calls=%async_computation.11 | async-start | bytes 262144
  403.1 510.3 %reduce-scatter.7.cloned.1.call-start = ((), (), s32[]{:S(2)}) async-start(), calls=%async_computation.9 | async-start | bytes 589824 | tf_op jit(solution)/shard_map/reduce_scatter | solution.py:66
  404.7 575.3 %reduce-scatter.5.cloned.1.call-start = ((), (), s32[]{:S(2)}) async-start(), calls=%async_computation.8 | async-start | bytes 2359296 | tf_op jit(solution)/shard_map/reduce_scatter | solution.py:65
  410.4 2.1 copy-start.4
  410.4 463.0 %copy-start.1 = (bf16[2,512,512]{2,1,0:T(8,128)(2,1)S(1)}, bf16[2,512,512]{2,1,0:T(8,128)(2,1)}, u32[]{:S(2)}) copy-start(bf16[2,512,512]{2,1,0:T(8,128)(2,1)} %all-gather.3.cloned.1.call-done) | copy-start | bytes 3145732
Sparse Core Ops, SparseCore 0:
  10.1 48.4 all-gather.2
  356.8 46.2 reduce-scatter.8
  406.0 465.8 all-reduce.2
  875.3 37.9 reduce-scatter.6
  916.6 63.3 reduce-scatter.4
where the time goes:
time: 987 us
  waiting for transfers between devices  689 us (70%)
  blocking collectives  213 us (22%)
  starting transfers between devices  35.8 us (4%)
  matrix products  20.5 us (2%)
  between operations  14.6 us (1%)
  local copies, waits for them, and re-layouts  12.5 us (1%)
    unnamed x6, waiting for transfers between devices  457 us
    all_gather x1, blocking collectives, per_device(): gate_full = lax.all_gather(gate_half, 'seq', axis=0, tiled=True)  99.1 us
    all_to_all x1, blocking collectives, per_device(): lax.all_to_all(mixed_grad, 'seq', split_axis=2, concat_axis=1, tiled=True)  68.3 us
    reduce_scatter x1, waiting for transfers between devices, per_device(): lax.psum_scatter(first_part, 'dp', scatter_dimension=1, tiled=True)  66.6 us
    all_gather x1, waiting for transfers between devices, per_device(): lax.all_gather(first_factor, 'dp', axis=1, tiled=True)  50.7 us
    reduce_scatter x1, waiting for transfers between devices, per_device(): lax.psum_scatter(gate_part, 'dp', scatter_dimension=1, tiled=True)  46.7 us
    reduce_scatter x1, waiting for transfers between devices, per_device(): lax.psum_scatter(second_part, 'dp', scatter_dimension=1, tiled=True)  36.7 us
    all_to_all x1, waiting for transfers between devices, per_device(): lax.all_to_all(mixed_one, 'seq', split_axis=2, concat_axis=1, tiled=True)  29.2 us
  transfers between devices with their start and end apart: 8, of which 7 were waited for; matrix products, arithmetic and copies ran while one was open for 2% of the time, Pallas kernels for 0%

commit v1 on v0

v1 whole, which is shorter than its diff:
```python
import jax
import jax.numpy as jnp
from jax import lax
from jax.sharding import PartitionSpec as P

BF16 = jnp.bfloat16
F32 = jnp.float32


def exchange(x, axis):
    return lax.all_to_all(x, axis, split_axis=0, concat_axis=0, tiled=True)


def gather(x, axis):
    n = lax.axis_size(axis)
    return exchange(jnp.broadcast_to(x[None], (n,) + x.shape), axis)


def per_device(inputs, out_grad, first_factor, second_factor, gate_weight):
    nd = lax.axis_size("dp")
    ns = lax.axis_size("seq")
    _, rows, width = inputs.shape
    blocks, part, length = first_factor.shape
    cols, part2, size2 = second_factor.shape
    crows, cpart = gate_weight.shape
    flat = inputs.reshape(rows, width)
    blocked = inputs.reshape(blocks, length, width)
    cot = out_grad.reshape(rows, width).astype(F32)

    first = gather(first_factor, "dp").transpose(1, 0, 2, 3).reshape(blocks, length, length)
    one = jnp.einsum("bjk,bkd->bjd", first, blocked, preferred_element_type=F32).astype(BF16)
    one = one.reshape(blocks, ns, cols, width).transpose(1, 0, 2, 3)
    col_one = exchange(one, "seq").reshape(size2, cols, width)

    gate_full = gather(gate_weight, "seq").reshape(width, cpart)
    gate_full = gather(gate_full, "dp").transpose(1, 0, 2).reshape(width, width)
    second = gather(second_factor, "dp").transpose(1, 0, 2, 3).reshape(cols, size2, size2)

    gate = jax.nn.sigmoid(jnp.dot(flat, gate_full, preferred_element_type=F32))
    mgrad = (cot * gate).astype(BF16)
    mgrad = mgrad.reshape(blocks, ns, cols, width).transpose(1, 0, 2, 3)

    col_two = jnp.einsum("jpq,qjd->pjd", second, col_one, preferred_element_type=F32).astype(BF16)
    col_two = col_two.reshape(ns, blocks, cols, width)
    both = exchange(jnp.concatenate([mgrad, col_two], axis=1), "seq")
    col_grad = both[:, :blocks].reshape(size2, cols, width)
    two = both[:, blocks:].transpose(1, 0, 2, 3).reshape(rows, width)

    col_back = jnp.einsum("jpq,pjd->qjd", second, col_grad, preferred_element_type=F32).astype(BF16)
    back = exchange(col_back.reshape(ns, blocks, cols, width), "seq")
    back = back.transpose(1, 0, 2, 3).reshape(blocks, length, width)

    delta = (cot * two.astype(F32) * gate * (1.0 - gate)).astype(BF16)
    gpart = jnp.dot(flat.T, delta, preferred_element_type=F32)
    gpart = gpart.reshape(width, nd, cpart).transpose(1, 0, 2)
    gsum = exchange(gpart, "dp").sum(0)
    grad_gate = exchange(gsum.reshape(ns, crows, cpart), "seq").sum(0)

    spart = jnp.einsum("pjd,qjd->jpq", col_grad, col_one, preferred_element_type=F32)
    spart = spart.reshape(cols, nd, part2, size2).transpose(1, 0, 2, 3)
    grad_second = exchange(spart, "dp").sum(0)

    gate_input = jnp.dot(delta, gate_full.T, preferred_element_type=F32).astype(BF16)

    fpart = jnp.einsum("bjd,bkd->bjk", back, blocked, preferred_element_type=F32).astype(BF16)
    fpart = fpart.reshape(blocks, nd, part, length).transpose(1, 0, 2, 3)
    grad_first = exchange(fpart, "dp").astype(F32).sum(0)
    through = jnp.einsum("bjk,bjd->bkd", first, back, preferred_element_type=F32)
    grad_inputs = (through + gate_input.reshape(through.shape).astype(F32)).astype(BF16)
    return (grad_inputs.reshape(inputs.shape), grad_first, grad_second, grad_gate)


def solution(mesh):
    specs = (P("seq", "dp", None), P("seq", "dp", None), P("seq", "dp"))
    return jax.shard_map(
        per_device,
        mesh=mesh,
        in_specs=(P("dp", "seq", None), P("dp", "seq", None)) + specs,
        out_specs=(P("dp", "seq", None),) + specs,
        check_vma=False,
    )
```

time: 987 us -> 399 us (0.40)
  waiting for transfers between devices: 689 us -> 160 us
  blocking collectives: 213 us -> 141 us
  starting transfers between devices: 35.8 us -> 53.5 us
  between operations: 14.6 us -> 0.92 us
    unnamed x6 -> x0, waiting for transfers between devices: 457 us -> none
    reduce_scatter x3 -> x0, waiting for transfers between devices: 150 us -> none  [the longest x1 66.6 us: per_device(): lax.psum_scatter(first_part, 'dp', scatter_dimension=1, tiled=True)]
    all_gather x3 -> x0, blocking collectives: 145 us -> none  [the longest x1 99.1 us: per_device(): gate_full = lax.all_gather(gate_half, 'seq', axis=0, tiled=True)]
    all_to_all x3 -> x9, waiting for transfers between devices: 31.5 us -> 160 us  [exchange(): return lax.all_to_all(x, axis, split_axis=0, concat_axis=0, tiled=True)]
    all_to_all x1 -> x2, blocking collectives: 68.3 us -> 141 us  [exchange(): return lax.all_to_all(x, axis, split_axis=0, concat_axis=0, tiled=True)]
    all_gather x1 -> x0, waiting for transfers between devices: 50.7 us -> none  [per_device(): lax.all_gather(first_factor, 'dp', axis=1, tiled=True)]
    all_to_all x3 -> x9, starting transfers between devices: 35.4 us -> 53.5 us  [exchange(): return lax.all_to_all(x, axis, split_axis=0, concat_axis=0, tiled=True)]
  transfers between devices with their start and end apart: 8 -> 9, of which waited for: 7 -> 9; matrix products, arithmetic and copies ran while one was open for 2% -> 7% of each run, Pallas kernels for 0% -> 0%
where the time goes in v1:
time: 399 us; the launch traced here: 398 us
  waiting for transfers between devices  160 us (40%)
  blocking collectives  141 us (35%)
  starting transfers between devices  53.5 us (13%)
  local copies, waits for them, and re-layouts  18.7 us (5%)
  matrix products  16.6 us (4%)
  other arithmetic  7.12 us (2%)
    all_to_all x9, waiting for transfers between devices, exchange(): return lax.all_to_all(x, axis, split_axis=0, concat_axis=0, tiled=True)  160 us
    all_to_all x2, blocking collectives, exchange(): return lax.all_to_all(x, axis, split_axis=0, concat_axis=0, tiled=True)  141 us
    all_to_all x9, starting transfers between devices, exchange(): return lax.all_to_all(x, axis, split_axis=0, concat_axis=0, tiled=True)  53.5 us
  transfers between devices with their start and end apart: 9, of which 9 were waited for; matrix products, arithmetic and copies ran while one was open for 7% of the time, Pallas kernels for 0%

profile of v1, /device:TPU:1, one launch (start us, length us, event | category | flops | bytes accessed | tf_op | source)
XLA Modules:
  0.0 398.0 jit_solution(5858168330793625563)
XLA Ops:
  2.2 5.9 %all-to-all-start.4 = ((bf16[8,8,16,128]{3,2,1,0:T(8,128)(2,1)}), bf16[8,8,16,128]{3,2,1,0:T(8,128)(2,1)S(1)}, u32[]{:S(2)}, u32[]{:S(2)}) async-start(bf16[8,8,16,128]{3,2,1,0:T(8,128)(2,1)} %broadcast_in_dim.14), calls=%async_computation.4 | async-start | bytes 524288 | tf_op jit(solution)/shard_map/all_to_all | solution.py:11
  9.0 5.3 %all-to-all-done.4 = bf16[8,8,16,128]{3,2,1,0:T(8,128)(2,1)S(1)} async-done(((bf16[8,8,16,128]{3,2,1,0:T(8,128)(2,1)}), bf16[8,8,16,128]{3,2,1,0:T(8,128)(2,1)S(1)}, u32[]{:S(2)}, u32[]{:S(2)}) %all-to-all-start.4) | async-done | bytes 262176 | tf_op jit(solution)/shard_map/all_to_all | solution.py:11
  14.3 35.6 %all_to_all.55 = bf16[64,2,256]{2,1,0:T(2,128)(2,1)S(1)} all-to-all(bf16[64,2,256]{2,1,0:T(2,128)(2,1)S(1)} %reshape.92), channel_id=1, replica_groups=mesh['seq'=64,'dp'=8] {'seq'}, dimensions={0} | all-to-all | bytes 131072 | tf_op jit(solution)/shard_map/all_to_all | solution.py:11
  51.9 3.6 all-to-all-start.2
  55.7 15.2 %all-to-all-done.2 = bf16[8,2,64,512]{3,2,1,0:T(8,128)(2,1)S(1)} async-done(((bf16[8,2,64,512]{3,2,1,0:T(8,128)(2,1)}), bf16[8,2,64,512]{3,2,1,0:T(8,128)(2,1)S(1)}, u32[]{:S(2)}, u32[]{:S(2)}) %all-to-all-start.2) | async-done | bytes 1048608 | tf_op jit(solution)/shard_map/all_to_all | solution.py:11
  71.7 3.5 all-to-all-start.1
  78.1 6.0 %all-to-all-done.1 = bf16[8,512,64]{1,2,0:T(8,128)(2,1)S(1)} async-done(((bf16[8,512,64]{1,2,0:T(8,128)(2,1)}), bf16[8,512,64]{1,2,0:T(8,128)(2,1)S(1)}, u32[]{:S(2)}, u32[]{:S(2)}) %all-to-all-start.1) | async-done | bytes 524320 | tf_op jit(solution)/shard_map/all_to_all | solution.py:11
  84.1 6.2 %all-to-all-start.3 = ((bf16[64,2,8,512]{3,2,1,0:T(8,128)(2,1)}), bf16[64,2,8,512]{3,2,1,0:T(8,128)(2,1)S(1)}, u32[]{:S(2)}, u32[]{:S(2)}) async-start(bf16[64,2,8,512]{3,2,1,0:T(8,128)(2,1)} %bitcast.74), calls=%async_computation.3 | async-start | bytes 2097152 | tf_op jit(solution)/shard_map/all_to_all | solution.py:11
  90.3 3.6 fusion
  94.0 50.3 %all-to-all-done.3 = bf16[64,2,8,512]{3,2,1,0:T(8,128)(2,1)S(1)} async-done(((bf16[64,2,8,512]{3,2,1,0:T(8,128)(2,1)}), bf16[64,2,8,512]{3,2,1,0:T(8,128)(2,1)S(1)}, u32[]{:S(2)}, u32[]{:S(2)}) %all-to-all-start.3) | async-done | bytes 1048608 | tf_op jit(solution)/shard_map/all_to_all | solution.py:11
  145.9 105.7 %all_to_all.56 = bf16[64,4,8,512]{3,2,1,0:T(8,128)(2,1)S(1)} all-to-all(bf16[64,4,8,512]{3,2,1,0:T(8,128)(2,1)S(1)} %pad_maximum_fusion), channel_id=1, replica_groups=mesh['seq'=64,'dp'=8] {'seq'}, dimensions={0} | all-to-all | bytes 4194304 | tf_op jit(solution)/shard_map/all_to_all | solution.py:11
  255.2 4.1 %all-to-all-start.8 = ((f32[8,8,16,128]{3,2,1,0:T(8,128)}), f32[8,8,16,128]{3,2,1,0:T(8,128)}, u32[]{:S(2)}, u32[]{:S(2)}) async-start(f32[8,8,16,128]{3,2,1,0:T(8,128)} %bitcast.90), calls=%async_computation.8 | async-start | bytes 1048576 | tf_op jit(solution)/shard_map/all_to_all | solution.py:11
  259.3 2.3 fusion.3
  264.3 2.5 all-to-all-done.8
  266.9 3.6 all-to-all-start.9
  276.0 5.9 %all-to-all-done.9 = f32[8,512,64]{1,2,0:T(8,128)S(1)} async-done(((f32[8,512,64]{1,2,0:T(8,128)}), f32[8,512,64]{1,2,0:T(8,128)S(1)}, u32[]{:S(2)}, u32[]{:S(2)}) %all-to-all-start.9) | async-done | bytes 1048608 | tf_op jit(solution)/shard_map/all_to_all | solution.py:11
  281.8 15.7 %all-to-all-start.6 = ((bf16[64,2,8,512]{3,1,2,0:T(2,128)(2,1)}), bf16[64,2,8,512]{3,1,2,0:T(2,128)(2,1)S(1)}, u32[]{:S(2)}, u32[]{:S(2)}) async-start(bf16[64,2,8,512]{3,1,2,0:T(2,128)(2,1)} %copy.53), calls=%async_computation.6 | async-start | bytes 2097152 | tf_op jit(solution)/shard_map/all_to_all | solution.py:11
  298.6 53.0 %all-to-all-done.6 = bf16[64,2,8,512]{3,1,2,0:T(2,128)(2,1)S(1)} async-done(((bf16[64,2,8,512]{3,1,2,0:T(2,128)(2,1)}), bf16[64,2,8,512]{3,1,2,0:T(2,128)(2,1)S(1)}, u32[]{:S(2)}, u32[]{:S(2)}) %all-to-all-start.6) | async-done | bytes 1048608 | tf_op jit(solution)/shard_map/all_to_all | solution.py:11
  351.6 7.4 %all-to-all-start.10 = ((f32[64,1,512]{2,1,0:T(1,128)}), f32[64,1,512]{2,1,0:T(1,128)S(1)}, u32[]{:S(2)}, u32[]{:S(2)}) async-start(f32[64,1,512]{2,1,0:T(1,128)} %reshape.94), calls=%async_computation.10 | async-start | bytes 262144 | tf_op jit(solution)/shard_map/all_to_all | solution.py:11
  360.8 16.8 %all-to-all-done.10 = f32[64,1,512]{2,1,0:T(1,128)S(1)} async-done(((f32[64,1,512]{2,1,0:T(1,128)}), f32[64,1,512]{2,1,0:T(1,128)S(1)}, u32[]{:S(2)}, u32[]{:S(2)}) %all-to-all-start.10) | async-done | bytes 131104 | tf_op jit(solution)/shard_map/all_to_all | solution.py:11
  378.2 3.6 all-to-all-start.7
  381.8 3.2 convolution_convert_fusion.4
  388.9 3.3 fusion.4
  392.2 5.0 %all-to-all-done.7 = bf16[8,2,64,512]{3,2,1,0:T(8,128)(2,1)S(1)} async-done(((bf16[8,2,64,512]{3,2,1,0:T(8,128)(2,1)}), bf16[8,2,64,512]{3,2,1,0:T(8,128)(2,1)S(1)}, u32[]{:S(2)}, u32[]{:S(2)}) %all-to-all-start.7) | async-done | bytes 1048608 | tf_op jit(solution)/shard_map/all_to_all | solution.py:11
  (58 shorter events, 30.1 us)
Async XLA Ops:
  0.6 74.7 %copy-start = (bf16[1,1024,512]{2,1,0:T(8,128)(2,1)S(1)}, bf16[1,1024,512]{2,1,0:T(8,128)(2,1)}, u32[]{:S(2)}) copy-start(bf16[1,1024,512]{2,1,0:T(8,128)(2,1)} %param.5) | copy-start | bytes 3145732
  2.2 12.1 %all-to-all-start.4 = ((bf16[8,8,16,128]{3,2,1,0:T(8,128)(2,1)}), bf16[8,8,16,128]{3,2,1,0:T(8,128)(2,1)S(1)}, u32[]{:S(2)}, u32[]{:S(2)}) async-start(bf16[8,8,16,128]{3,2,1,0:T(8,128)(2,1)} %broadcast_in_dim.14), calls=%async_computation.4 | async-start | bytes 524288 | tf_op jit(solution)/shard_map/all_to_all | solution.py:11
  51.9 19.0 %all-to-all-start.2 = ((bf16[8,2,64,512]{3,2,1,0:T(8,128)(2,1)}), bf16[8,2,64,512]{3,2,1,0:T(8,128)(2,1)S(1)}, u32[]{:S(2)}, u32[]{:S(2)}) async-start(bf16[8,2,64,512]{3,2,1,0:T(8,128)(2,1)} %broadcast_in_dim.13), calls=%async_computation.2 | async-start | bytes 2097152 | tf_op jit(solution)/shard_map/all_to_all | solution.py:11
  71.7 12.3 %all-to-all-start.1 = ((bf16[8,512,64]{1,2,0:T(8,128)(2,1)}), bf16[8,512,64]{1,2,0:T(8,128)(2,1)S(1)}, u32[]{:S(2)}, u32[]{:S(2)}) async-start(bf16[8,512,64]{1,2,0:T(8,128)(2,1)} %broadcast_in_dim.12), calls=%async_computation.1 | async-start | bytes 1048576 | tf_op jit(solution)/shard_map/all_to_all | solution.py:11
  75.3 1.0 copy-start.1
  84.1 9.9 %copy-start.9 = (bf16[8,512,64]{1,2,0:T(8,128)(2,1)}, bf16[8,512,64]{1,2,0:T(8,128)(2,1)S(1)}, u32[]{:S(2)}) copy-start(bf16[8,512,64]{1,2,0:T(8,128)(2,1)S(1)} %all-to-all-done.1) | copy-start | bytes 1572868
  84.1 60.2 %all-to-all-start.3 = ((bf16[64,2,8,512]{3,2,1,0:T(8,128)(2,1)}), bf16[64,2,8,512]{3,2,1,0:T(8,128)(2,1)S(1)}, u32[]{:S(2)}, u32[]{:S(2)}) async-start(bf16[64,2,8,512]{3,2,1,0:T(8,128)(2,1)} %bitcast.74), calls=%async_computation.3 | async-start | bytes 2097152 | tf_op jit(solution)/shard_map/all_to_all | solution.py:11
  144.3 1.4 copy-start.5
  252.0 1.0 copy-start.3
  252.0 1.6 copy-start.6
  255.2 11.7 %all-to-all-start.8 = ((f32[8,8,16,128]{3,2,1,0:T(8,128)}), f32[8,8,16,128]{3,2,1,0:T(8,128)}, u32[]{:S(2)}, u32[]{:S(2)}) async-start(f32[8,8,16,128]{3,2,1,0:T(8,128)} %bitcast.90), calls=%async_computation.8 | async-start | bytes 1048576 | tf_op jit(solution)/shard_map/all_to_all | solution.py:11
  261.6 1.0 copy-start.8
  264.3 6.1 %copy-start.4 = (bf16[64,2,8,512]{3,2,1,0:T(8,128)(2,1)S(1)}, bf16[64,2,8,512]{3,2,1,0:T(8,128)(2,1)}, u32[]{:S(2)}) copy-start(bf16[64,2,8,512]{3,2,1,0:T(8,128)(2,1)} %copy-done.3) | copy-start | bytes 3145732
  266.9 15.0 %all-to-all-start.9 = ((f32[8,512,64]{1,2,0:T(8,128)}), f32[8,512,64]{1,2,0:T(8,128)S(1)}, u32[]{:S(2)}, u32[]{:S(2)}) async-start(f32[8,512,64]{1,2,0:T(8,128)} %bitcast.94), calls=%async_computation.9 | async-start | bytes 2097152 | tf_op jit(solution)/shard_map/all_to_all | solution.py:11
  281.8 69.7 %all-to-all-start.6 = ((bf16[64,2,8,512]{3,1,2,0:T(2,128)(2,1)}), bf16[64,2,8,512]{3,1,2,0:T(2,128)(2,1)S(1)}, u32[]{:S(2)}, u32[]{:S(2)}) async-start(bf16[64,2,8,512]{3,1,2,0:T(2,128)(2,1)} %copy.53), calls=%async_computation.6 | async-start | bytes 2097152 | tf_op jit(solution)/shard_map/all_to_all | solution.py:11
  351.6 9.2 %copy-start.7 = (bf16[64,2,8,512]{3,1,2,0:T(2,128)(2,1)}, bf16[64,2,8,512]{3,1,2,0:T(2,128)(2,1)S(1)}, u32[]{:S(2)}) copy-start(bf16[64,2,8,512]{3,1,2,0:T(2,128)(2,1)S(1)} %all-to-all-done.6) | copy-start | bytes 3145732
  351.6 26.0 %all-to-all-start.10 = ((f32[64,1,512]{2,1,0:T(1,128)}), f32[64,1,512]{2,1,0:T(1,128)S(1)}, u32[]{:S(2)}, u32[]{:S(2)}) async-start(f32[64,1,512]{2,1,0:T(1,128)} %reshape.94), calls=%async_computation.10 | async-start | bytes 262144 | tf_op jit(solution)/shard_map/all_to_all | solution.py:11
  377.6 0.7 copy-start.10
  378.2 19.0 %all-to-all-start.7 = ((bf16[8,2,64,512]{3,2,1,0:T(8,128)(2,1)}), bf16[8,2,64,512]{3,2,1,0:T(8,128)(2,1)S(1)}, u32[]{:S(2)}, u32[]{:S(2)}) async-start(bf16[8,2,64,512]{3,2,1,0:T(8,128)(2,1)} %bitcast.73), calls=%async_computation.7 | async-start | bytes 2097152 | tf_op jit(solution)/shard_map/all_to_all | solution.py:11
  381.8 5.4 %copy-start.11 = (f32[64,1,512]{2,1,0:T(1,128)S(1)}, f32[64,1,512]{2,1,0:T(1,128)}, u32[]{:S(2)}) copy-start(f32[64,1,512]{2,1,0:T(1,128)} %copy-done.10) | copy-start | bytes 393220
  381.8 7.1 %copy-start.2 = (bf16[2,8,64,512]{3,2,1,0:T(8,128)(2,1)S(1)}, bf16[2,8,64,512]{3,2,1,0:T(8,128)(2,1)}, u32[]{:S(2)}) copy-start(bf16[2,8,64,512]{3,2,1,0:T(8,128)(2,1)} %copy-done.1) | copy-start | bytes 3145732

commit v2 on v1

v2 whole, which is shorter than its diff:
```python
import jax
import jax.numpy as jnp
from jax import lax
from jax.sharding import Mesh, PartitionSpec as P

BF16 = jnp.bfloat16
F32 = jnp.float32
SEQ = ("z", "xh", "co")
DP = ("y", "xl")


def exchange(x, axis):
    return lax.all_to_all(x, axis, split_axis=0, concat_axis=0, tiled=True)


def spread(x, axis):
    n = lax.axis_size(axis)
    return exchange(jnp.broadcast_to(x[None], (n,) + x.shape), axis)


def gather(x, axes):
    out = x[None]
    for axis in reversed(axes):
        out = lax.all_gather(out, axis, axis=0, tiled=True)
    return out


def halve(x, axis, bit):
    n = lax.axis_size(axis)
    low = lax.axis_index(axis) & bit == 0
    keep = jnp.where(low, x[0], x[1])
    give = jnp.where(low, x[1], x[0])
    return keep + lax.ppermute(give, axis, [(i, i ^ bit) for i in range(n)])


def per_device(inputs, out_grad, first_factor, second_factor, gate_weight):
    nd = lax.axis_size(DP)
    ns = lax.axis_size(SEQ)
    nz = lax.axis_size("z")
    _, rows, width = inputs.shape
    blocks, part, length = first_factor.shape
    cols, part2, size2 = second_factor.shape
    crows, cpart = gate_weight.shape
    flat = inputs.reshape(rows, width)
    blocked = inputs.reshape(blocks, length, width)
    cot = out_grad.reshape(rows, width).astype(F32)

    first = spread(first_factor, DP).transpose(1, 0, 2, 3).reshape(blocks, length, length)
    second = gather(second_factor, DP).transpose(1, 0, 2, 3).reshape(cols, size2, size2)
    gate_full = gather(gate_weight, SEQ).reshape(width, cpart)
    gate_full = gather(gate_full, DP).transpose(1, 0, 2).reshape(width, width)

    one = jnp.einsum("bjk,bkd->bjd", first, blocked, preferred_element_type=F32).astype(BF16)
    one = one.reshape(blocks, ns, cols, width).transpose(1, 0, 2, 3)
    col_one = exchange(one, SEQ).reshape(size2, cols, width)

    gate = jax.nn.sigmoid(jnp.dot(flat, gate_full, preferred_element_type=F32))
    mgrad = (cot * gate).astype(BF16)
    mgrad = mgrad.reshape(blocks, ns, cols, width).transpose(1, 0, 2, 3)

    col_two = jnp.einsum("jpq,qjd->pjd", second, col_one, preferred_element_type=F32).astype(BF16)
    col_two = col_two.reshape(ns, blocks, cols, width)
    both = exchange(jnp.concatenate([mgrad, col_two], axis=1), SEQ)
    col_grad = both[:, :blocks].reshape(size2, cols, width)
    two = both[:, blocks:].transpose(1, 0, 2, 3).reshape(rows, width)

    col_back = jnp.einsum("jpq,pjd->qjd", second, col_grad, preferred_element_type=F32).astype(BF16)
    spart = jnp.einsum("pjd,qjd->jpq", col_grad, col_one, preferred_element_type=F32)
    two, col_back, spart = lax.optimization_barrier((two, col_back, spart))
    back = exchange(col_back.reshape(ns, blocks, cols, width), SEQ)
    back = back.transpose(1, 0, 2, 3).reshape(blocks, length, width)
    grad_second = lax.psum_scatter(spart, DP, scatter_dimension=1, tiled=True)

    delta = (cot * two.astype(F32) * gate * (1.0 - gate)).astype(BF16)
    gpart = jnp.dot(delta.T, flat, preferred_element_type=F32)
    gsum = gpart.reshape(lax.axis_size("y"), 2, cpart, width)
    gsum = halve(gsum.transpose(1, 0, 2, 3), "xl", 1)
    gsum = halve(gsum.reshape(2, 2, cpart, width), "y", 2)
    gsum = halve(gsum, "y", 1)
    gsum = gsum.T.reshape(ns // 2, 2, crows, cpart).transpose(1, 0, 2, 3)
    gsum = halve(gsum, "co", 1)
    gsum = halve(gsum.reshape(nz, 2, crows, cpart).transpose(1, 0, 2, 3), "xh", 1)
    while nz > 1:
        nz //= 2
        gsum = halve(gsum.reshape(2, nz, crows, cpart), "z", nz)
    grad_gate = gsum.reshape(crows, cpart)

    gate_input = jnp.dot(delta, gate_full.T, preferred_element_type=F32).astype(BF16)

    fpart = jnp.einsum("bjd,bkd->bjk", back, blocked, preferred_element_type=F32).astype(BF16)
    fpart = fpart.reshape(blocks, nd, part, length).transpose(1, 0, 2, 3)
    grad_first = exchange(fpart, DP).astype(F32).sum(0)
    through = jnp.einsum("bjk,bjd->bkd", first, back, preferred_element_type=F32)
    grad_inputs = (through + gate_input.reshape(through.shape).astype(F32)).astype(BF16)
    return (grad_inputs.reshape(inputs.shape), grad_first, grad_second, grad_gate)


def solution(mesh):
    fine = Mesh(mesh.devices.reshape(16, 2, 2, 4, 2), SEQ + DP)
    specs = (P(SEQ, DP, None), P(SEQ, DP, None), P(SEQ, DP))
    return jax.shard_map(
        per_device,
        mesh=fine,
        in_specs=(P(DP, SEQ, None), P(DP, SEQ, None)) + specs,
        out_specs=(P(DP, SEQ, None),) + specs,
        check_vma=False,
    )
```

time: 399 us -> 418 us (1.048)
  starting transfers between devices: 53.5 us -> 99.1 us
  blocking collectives: 141 us -> 111 us
  between operations: 0.92 us -> 14.4 us
  local copies, waits for them, and re-layouts: 18.7 us -> 10.6 us
  waiting for transfers between devices: 160 us -> 154 us
    all_to_all x2 -> x1, blocking collectives: 141 us -> 17.7 us  [exchange(): return lax.all_to_all(x, axis, split_axis=0, concat_axis=0, tiled=True)]
    all_gather x0 -> x7, blocking collectives: none -> 92.9 us  [gather(): out = lax.all_gather(out, axis, axis=0, tiled=True)]
    all_to_all x9 -> x4, waiting for transfers between devices: 160 us -> 108 us  [exchange(): return lax.all_to_all(x, axis, split_axis=0, concat_axis=0, tiled=True)]
    ppermute x0 -> x9, waiting for transfers between devices: none -> 36.7 us  [halve(): return keep + lax.ppermute(give, axis, [(i, i ^ bit) for i in range(n)])]
    ppermute x0 -> x9, starting transfers between devices: none -> 35.9 us  [halve(): return keep + lax.ppermute(give, axis, [(i, i ^ bit) for i in range(n)])]
    all_to_all x9 -> x4, starting transfers between devices: 53.5 us -> 63.1 us  [exchange(): return lax.all_to_all(x, axis, split_axis=0, concat_axis=0, tiled=True)]
    reduce_scatter x0 -> x1, waiting for transfers between devices: none -> 9.33 us  [per_device(): grad_second = lax.psum_scatter(spart, DP, scatter_dimension=1, tiled=True)]
    reshape x3 -> x0, local copies, waits for them, and re-layouts: 4.51 us -> none  [the longest x2 3.63 us: per_device(): back = exchange(col_back.reshape(ns, blocks, cols, width), 'seq')]
  transfers between devices with their start and end apart: 9 -> 14, of which waited for: 9 -> 11; matrix products, arithmetic and copies ran while one was open for 7% -> 4% of each run, Pallas kernels for 0% -> 0%
where the time goes in v2:
time: 418 us; the launch traced here: 414 us
  waiting for transfers between devices  154 us (37%)
  blocking collectives  111 us (27%)
  starting transfers between devices  99.1 us (24%)
  matrix products  15.6 us (4%)
  between operations  14.4 us (3%)
  local copies, waits for them, and re-layouts  10.6 us (3%)
  other arithmetic  9.77 us (2%)
    all_to_all x4, waiting for transfers between devices, exchange(): return lax.all_to_all(x, axis, split_axis=0, concat_axis=0, tiled=True)  108 us
    all_gather x7, blocking collectives, gather(): out = lax.all_gather(out, axis, axis=0, tiled=True)  92.9 us
    all_to_all x4, starting transfers between devices, exchange(): return lax.all_to_all(x, axis, split_axis=0, concat_axis=0, tiled=True)  63.1 us
    ppermute x9, waiting for transfers between devices, halve(): return keep + lax.ppermute(give, axis, [(i, i ^ bit) for i in range(n)])  36.7 us
    ppermute x9, starting transfers between devices, halve(): return keep + lax.ppermute(give, axis, [(i, i ^ bit) for i in range(n)])  35.9 us
    all_to_all x1, blocking collectives, exchange(): return lax.all_to_all(x, axis, split_axis=0, concat_axis=0, tiled=True)  17.7 us
    reduce_scatter x1, waiting for transfers between devices, per_device(): grad_second = lax.psum_scatter(spart, DP, scatter_dimension=1, tiled=True)  9.33 us
  transfers between devices with their start and end apart: 14, of which 11 were waited for; matrix products, arithmetic and copies ran while one was open for 4% of the time, Pallas kernels for 0%

profile of v2, /device:TPU:1, one launch (start us, length us, event | category | flops | bytes accessed | tf_op | source)
XLA Modules:
  0.0 413.8 jit_solution(10903925884755456122)
XLA Ops:
  8.3 17.7 %all_to_all.25 = bf16[8,2,64,512]{3,2,1,0:T(8,128)(2,1)S(1)} all-to-all(bf16[8,2,64,512]{3,2,1,0:T(8,128)(2,1)S(1)} %broadcast_in_dim.13), channel_id=1, replica_groups=mesh['z'=16,'xh'=2,'co'=2,'y'=4,'xl'=2] {'y','xl'}, dimensions={0} | all-to-all | bytes 2097152 | tf_op jit(solution)/shard_map/all_to_all | solution.py:13
  27.9 22.8 %all-to-all-start.1 = ((bf16[64,2,8,512]{3,2,1,0:T(8,128)(2,1)}), bf16[64,2,8,512]{3,2,1,0:T(8,128)(2,1)S(1)}, u32[]{:S(2)}, u32[]{:S(2)}) async-start(bf16[64,2,8,512]{3,2,1,0:T(8,128)(2,1)} %bitcast.150), calls=%async_computation.1 | async-start | bytes 2097152 | tf_op jit(solution)/shard_map/all_to_all | solution.py:13
  52.6 4.9 %all_gather.22 = bf16[4,8,64]{2,1,0:T(8,128)(2,1)S(1)} all-gather(bf16[2,8,64]{2,1,0:T(8,128)(2,1)S(1)} %bitcast.179), channel_id=1, replica_groups=mesh['z'=16,'xh'=2,'co'=2,'y'=4,'xl'=2] {'xh'}, dimensions={0}, use_global_device_ids=true | all-gather | bytes 6144 | tf_op jit(solution)/shard_map/all_gather | solution.py:24
  57.5 58.7 %all_gather.23 = bf16[64,8,64]{2,1,0:T(8,128)(2,1)S(1)} all-gather(bf16[4,8,64]{2,1,0:T(8,128)(2,1)S(1)} %all_gather.22), channel_id=1, replica_groups=mesh['z'=16,'xh'=2,'co'=2,'y'=4,'xl'=2] {'z'}, dimensions={0}, use_global_device_ids=true | all-gather | bytes 69632 | tf_op jit(solution)/shard_map/all_gather | solution.py:24
  116.3 3.4 all-gather.1
  119.8 3.8 all_gather.24
  123.5 9.9 %all_gather.25 = bf16[8,512,64]{1,2,0:T(8,128)(2,1)S(1)} all-gather(bf16[2,512,64]{1,2,0:T(8,128)(2,1)S(1)} %all_gather.24), channel_id=1, replica_groups=mesh['z'=16,'xh'=2,'co'=2,'y'=4,'xl'=2] {'y'}, dimensions={0}, use_global_device_ids=true | all-gather | bytes 655360 | tf_op jit(solution)/shard_map/all_gather | solution.py:24
  135.9 10.3 %all_gather.27 = bf16[8,8,16,128]{3,2,0,1:T(8,128)(2,1)S(1)} all-gather(bf16[2,8,16,128]{3,2,0,1:T(8,128)(2,1)S(1)} %copy.80), channel_id=1, replica_groups=mesh['z'=16,'xh'=2,'co'=2,'y'=4,'xl'=2] {'y'}, dimensions={0}, use_global_device_ids=true | all-gather | bytes 327680 | tf_op jit(solution)/shard_map/all_gather | solution.py:24
  149.2 27.0 %all-to-all-start.2 = ((bf16[64,4,8,512]{3,2,1,0:T(8,128)(2,1)}), bf16[64,4,8,512]{3,2,1,0:T(8,128)(2,1)S(1)}, u32[]{:S(2)}, u32[]{:S(2)}) async-start(bf16[64,4,8,512]{3,2,1,0:T(8,128)(2,1)} %pad_maximum_fusion), calls=%async_computation.2 | async-start | bytes 4194304 | tf_op jit(solution)/shard_map/all_to_all | solution.py:13
  176.2 98.3 %all-to-all-done.2 = bf16[64,4,8,512]{3,2,1,0:T(8,128)(2,1)S(1)} async-done(((bf16[64,4,8,512]{3,2,1,0:T(8,128)(2,1)}), bf16[64,4,8,512]{3,2,1,0:T(8,128)(2,1)S(1)}, u32[]{:S(2)}, u32[]{:S(2)}) %all-to-all-start.2) | async-done | bytes 2097184 | tf_op jit(solution)/shard_map/all_to_all | solution.py:13
  291.7 8.9 %all-to-all-start.3 = ((bf16[64,2,8,512]{3,2,1,0:T(8,128)(2,1)}), bf16[64,2,8,512]{3,2,1,0:T(8,128)(2,1)}, u32[]{:S(2)}, u32[]{:S(2)}) async-start(bf16[64,2,8,512]{3,2,1,0:T(8,128)(2,1)} %bitcast.24), calls=%async_computation.3 | async-start | bytes 2097152 | tf_op jit(solution)/shard_map/all_to_all | solution.py:13
  302.2 3.1 collective-permute-start.1
  305.3 5.9 %collective-permute-done.1 = f32[2,64,512]{2,1,0:T(8,128)S(1)} collective-permute-done((f32[2,64,512]{2,1,0:T(8,128)S(1)}, f32[2,64,512]{2,1,0:T(8,128)S(1)}, u32[]{:S(2)}, u32[]{:S(2)}) %collective-permute-start.1) | collective-permute-done | bytes 262176 | tf_op jit(solution)/shard_map/ppermute | solution.py:33
  313.3 4.2 %collective-permute-done.2 = f32[64,512]{1,0:T(8,128)S(1)} collective-permute-done((f32[64,512]{1,0:T(8,128)S(1)}, f32[64,512]{1,0:T(8,128)S(1)}, u32[]{:S(2)}, u32[]{:S(2)}) %collective-permute-start.2) | collective-permute-done | bytes 131104 | tf_op jit(solution)/shard_map/ppermute | solution.py:33
  317.6 7.7 %collective-permute-start.3 = (f32[32,8,64]{2,1,0:T(8,128)S(1)}, f32[32,8,64]{2,1,0:T(8,128)S(1)}, u32[]{:S(2)}, u32[]{:S(2)}) collective-permute-start(f32[32,8,64]{2,1,0:T(8,128)S(1)} %select_bitcast_fusion.1), channel_id=1, source_target_pairs={{0,8},{8,0},{1,9},{9,1},{2,10},{10,2},{3,11},{11,3},{4,12},{12,4},... | collective-permute-start | bytes 196616 | tf_op jit(solution)/shard_map/ppermute | solution.py:33
  326.3 6.5 %collective-permute-start.4 = (f32[16,8,64]{2,1,0:T(8,128)S(1)}, f32[16,8,64]{2,1,0:T(8,128)S(1)}, u32[]{:S(2)}, u32[]{:S(2)}) collective-permute-start(f32[16,8,64]{2,1,0:T(8,128)S(1)} %select_bitcast_fusion.3), channel_id=1, source_target_pairs={{0,16},{16,0},{1,17},{17,1},{2,18},{18,2},{3,19},{19,3},{4,20},{20... | collective-permute-start | bytes 98312 | tf_op jit(solution)/shard_map/ppermute | solution.py:33
  335.6 8.0 %collective-permute-start.5 = (f32[8,8,64]{2,1,0:T(8,128)S(1)}, f32[8,8,64]{2,1,0:T(8,128)S(1)}, u32[]{:S(2)}, u32[]{:S(2)}) collective-permute-start(f32[8,8,64]{2,1,0:T(8,128)S(1)} %slice_select_fusion.1), channel_id=1, source_target_pairs={{0,256},{32,288},{64,320},{96,352},{128,384},{160,416},{192,448},{... | collective-permute-start | bytes 49160 | tf_op jit(solution)/shard_map/ppermute | solution.py:33
  343.7 12.8 %collective-permute-done.5 = f32[8,8,64]{2,1,0:T(8,128)S(1)} collective-permute-done((f32[8,8,64]{2,1,0:T(8,128)S(1)}, f32[8,8,64]{2,1,0:T(8,128)S(1)}, u32[]{:S(2)}, u32[]{:S(2)}) %collective-permute-start.5) | collective-permute-done | bytes 16416 | tf_op jit(solution)/shard_map/ppermute | solution.py:33
  358.5 6.6 %collective-permute-done.6 = f32[4,8,64]{2,1,0:T(8,128)S(1)} collective-permute-done((f32[4,8,64]{2,1,0:T(8,128)S(1)}, f32[4,8,64]{2,1,0:T(8,128)S(1)}, u32[]{:S(2)}, u32[]{:S(2)}) %collective-permute-start.6) | collective-permute-done | bytes 8224 | tf_op jit(solution)/shard_map/ppermute | solution.py:33
  367.1 3.3 collective-permute-done.7
  373.5 4.4 %all-to-all-start.4 = ((bf16[8,2,64,512]{3,2,1,0:T(8,128)(2,1)}), bf16[8,2,64,512]{3,2,1,0:T(8,128)(2,1)}, u32[]{:S(2)}, u32[]{:S(2)}) async-start(bf16[8,2,64,512]{3,2,1,0:T(8,128)(2,1)} %bitcast.160), calls=%async_computation.4 | async-start | bytes 2097152 | tf_op jit(solution)/shard_map/all_to_all | solution.py:13
  383.2 3.0 fusion.4
  386.2 9.3 %all-to-all-done.4 = bf16[8,2,64,512]{3,2,1,0:T(8,128)(2,1)} async-done(((bf16[8,2,64,512]{3,2,1,0:T(8,128)(2,1)}), bf16[8,2,64,512]{3,2,1,0:T(8,128)(2,1)}, u32[]{:S(2)}, u32[]{:S(2)}) %all-to-all-start.4) | async-done | bytes 1048608 | tf_op jit(solution)/shard_map/all_to_all | solution.py:13
  397.6 9.3 %reduce-scatter.2.cloned.1.call-done = f32[8,16,128]{2,1,0:T(8,128)} async-done(((f32[8,128,128]{2,1,0:T(8,128)}), f32[8,16,128]{2,1,0:T(8,128)}) %reduce-scatter.2.cloned.1.call-update) | async-done | bytes 65552 | tf_op jit(solution)/shard_map/reduce_scatter | solution.py:72
  (78 shorter events, 49.4 us)
Async XLA Ops:
  7.2 18.9 %copy-start = (bf16[1,1024,512]{2,1,0:T(8,128)(2,1)S(1)}, bf16[1,1024,512]{2,1,0:T(8,128)(2,1)}, u32[]{:S(2)}) copy-start(bf16[1,1024,512]{2,1,0:T(8,128)(2,1)} %param.5) | copy-start | bytes 3145732
  26.0 1.9 copy-start.1
  26.8 23.9 %copy-start.10 = (bf16[8,64]{1,0:T(8,128)(2,1)S(1)}, bf16[8,64]{1,0:T(8,128)(2,1)}, u32[]{:S(2)}) copy-start(bf16[8,64]{1,0:T(8,128)(2,1)} %param.9) | copy-start | bytes 3076
  26.8 89.5 %copy-start.9 = (bf16[8,16,128]{2,1,0:T(8,128)(2,1)S(1)}, bf16[8,16,128]{2,1,0:T(8,128)(2,1)}, u32[]{:S(2)}) copy-start(bf16[8,16,128]{2,1,0:T(8,128)(2,1)} %param.8) | copy-start | bytes 98308
  27.9 105.5 %copy-start.7 = (bf16[1,1024,512]{2,1,0:T(8,128)(2,1)S(1)}, bf16[1,1024,512]{2,1,0:T(8,128)(2,1)}, u32[]{:S(2)}) copy-start(bf16[1,1024,512]{2,1,0:T(8,128)(2,1)} %param.6) | copy-start | bytes 3145732
  27.9 118.3 %all-to-all-start.1 = ((bf16[64,2,8,512]{3,2,1,0:T(8,128)(2,1)}), bf16[64,2,8,512]{3,2,1,0:T(8,128)(2,1)S(1)}, u32[]{:S(2)}, u32[]{:S(2)}) async-start(bf16[64,2,8,512]{3,2,1,0:T(8,128)(2,1)} %bitcast.150), calls=%async_computation.1 | async-start | bytes 2097152 | tf_op jit(solution)/shard_map/all_to_all | solution.py:13
  133.4 2.4 copy-start.8
  146.2 1.4 copy-start.3
  149.2 125.4 %all-to-all-start.2 = ((bf16[64,4,8,512]{3,2,1,0:T(8,128)(2,1)}), bf16[64,4,8,512]{3,2,1,0:T(8,128)(2,1)S(1)}, u32[]{:S(2)}, u32[]{:S(2)}) async-start(bf16[64,4,8,512]{3,2,1,0:T(8,128)(2,1)} %pad_maximum_fusion), calls=%async_computation.2 | async-start | bytes 4194304 | tf_op jit(solution)/shard_map/all_to_all | solution.py:13
  277.0 1.5 copy-start.5
  278.4 1.6 copy-start.6
  288.1 12.6 %collective-permute-start = (f32[4,64,512]{2,1,0:T(8,128)}, f32[4,64,512]{2,1,0:T(8,128)}, u32[]{:S(2)}, u32[]{:S(2)}) collective-permute-start(f32[4,64,512]{2,1,0:T(8,128)} %select_bitcast_fusion), channel_id=1, source_target_pairs={{0,1},{1,0},{2,3},{3,2},{4,5},{5,4},{6,7},{7,6},{8,9},{9,8},{10,11... | collective-permute-start | bytes 1572872 | tf_op jit(solution)/shard_map/ppermute | solution.py:33
  291.7 78.8 %all-to-all-start.3 = ((bf16[64,2,8,512]{3,2,1,0:T(8,128)(2,1)}), bf16[64,2,8,512]{3,2,1,0:T(8,128)(2,1)}, u32[]{:S(2)}, u32[]{:S(2)}) async-start(bf16[64,2,8,512]{3,2,1,0:T(8,128)(2,1)} %bitcast.24), calls=%async_computation.3 | async-start | bytes 2097152 | tf_op jit(solution)/shard_map/all_to_all | solution.py:13
  300.6 106.4 %reduce-scatter.2.cloned.1.call-start = ((), (), s32[]{:S(2)}) async-start(), calls=%async_computation.6 | async-start | bytes 589824 | tf_op jit(solution)/shard_map/reduce_scatter | solution.py:72
  302.2 9.0 %collective-permute-start.1 = (f32[2,64,512]{2,1,0:T(8,128)S(1)}, f32[2,64,512]{2,1,0:T(8,128)S(1)}, u32[]{:S(2)}, u32[]{:S(2)}) collective-permute-start(f32[2,64,512]{2,1,0:T(8,128)S(1)} %slice_select_fusion), channel_id=1, source_target_pairs={{0,4},{2,6},{4,0},{6,2},{1,5},{3,7},{5,1},{7,3},{8,12},{10,14},{12... | collective-permute-start | bytes 786440 | tf_op jit(solution)/shard_map/ppermute | solution.py:33
  311.3 6.1 %collective-permute-start.2 = (f32[64,512]{1,0:T(8,128)S(1)}, f32[64,512]{1,0:T(8,128)S(1)}, u32[]{:S(2)}, u32[]{:S(2)}) collective-permute-start(f32[64,512]{1,0:T(8,128)S(1)} %select_bitcast_fusion.2), channel_id=1, source_target_pairs={{0,2},{2,0},{4,6},{6,4},{1,3},{3,1},{5,7},{7,5},{8,10},{10,8},{12,... | collective-permute-start | bytes 393224 | tf_op jit(solution)/shard_map/ppermute | solution.py:33
  317.6 8.7 %collective-permute-start.3 = (f32[32,8,64]{2,1,0:T(8,128)S(1)}, f32[32,8,64]{2,1,0:T(8,128)S(1)}, u32[]{:S(2)}, u32[]{:S(2)}) collective-permute-start(f32[32,8,64]{2,1,0:T(8,128)S(1)} %select_bitcast_fusion.1), channel_id=1, source_target_pairs={{0,8},{8,0},{1,9},{9,1},{2,10},{10,2},{3,11},{11,3},{4,12},{12,4},... | collective-permute-start | bytes 196616 | tf_op jit(solution)/shard_map/ppermute | solution.py:33
  326.3 9.3 %collective-permute-start.4 = (f32[16,8,64]{2,1,0:T(8,128)S(1)}, f32[16,8,64]{2,1,0:T(8,128)S(1)}, u32[]{:S(2)}, u32[]{:S(2)}) collective-permute-start(f32[16,8,64]{2,1,0:T(8,128)S(1)} %select_bitcast_fusion.3), channel_id=1, source_target_pairs={{0,16},{16,0},{1,17},{17,1},{2,18},{18,2},{3,19},{19,3},{4,20},{20... | collective-permute-start | bytes 98312 | tf_op jit(solution)/shard_map/ppermute | solution.py:33
  335.6 20.9 %collective-permute-start.5 = (f32[8,8,64]{2,1,0:T(8,128)S(1)}, f32[8,8,64]{2,1,0:T(8,128)S(1)}, u32[]{:S(2)}, u32[]{:S(2)}) collective-permute-start(f32[8,8,64]{2,1,0:T(8,128)S(1)} %slice_select_fusion.1), channel_id=1, source_target_pairs={{0,256},{32,288},{64,320},{96,352},{128,384},{160,416},{192,448},{... | collective-permute-start | bytes 49160 | tf_op jit(solution)/shard_map/ppermute | solution.py:33
  356.5 8.6 %collective-permute-start.6 = (f32[4,8,64]{2,1,0:T(8,128)S(1)}, f32[4,8,64]{2,1,0:T(8,128)S(1)}, u32[]{:S(2)}, u32[]{:S(2)}) collective-permute-start(f32[4,8,64]{2,1,0:T(8,128)S(1)} %slice_select_fusion.2), channel_id=1, source_target_pairs={{0,128},{32,160},{64,192},{96,224},{128,0},{160,32},{192,64},{224,... | collective-permute-start | bytes 24584 | tf_op jit(solution)/shard_map/ppermute | solution.py:33
  365.1 5.3 %collective-permute-start.7 = (f32[2,8,64]{2,1,0:T(8,128)S(1)}, f32[2,8,64]{2,1,0:T(8,128)S(1)}, u32[]{:S(2)}, u32[]{:S(2)}) collective-permute-start(f32[2,8,64]{2,1,0:T(8,128)S(1)} %slice_select_fusion.3), channel_id=1, source_target_pairs={{0,64},{32,96},{64,0},{96,32},{128,192},{160,224},{192,128},{224,1... | collective-permute-start | bytes 12296 | tf_op jit(solution)/shard_map/ppermute | solution.py:33
  373.5 9.7 %copy-start.2 = (bf16[2,8,64,512]{3,2,1,0:T(8,128)(2,1)S(1)}, bf16[2,8,64,512]{3,2,1,0:T(8,128)(2,1)}, u32[]{:S(2)}) copy-start(bf16[2,8,64,512]{3,2,1,0:T(8,128)(2,1)} %copy-done.1) | copy-start | bytes 3145732
  373.5 22.1 %all-to-all-start.4 = ((bf16[8,2,64,512]{3,2,1,0:T(8,128)(2,1)}), bf16[8,2,64,512]{3,2,1,0:T(8,128)(2,1)}, u32[]{:S(2)}, u32[]{:S(2)}) async-start(bf16[8,2,64,512]{3,2,1,0:T(8,128)(2,1)} %bitcast.160), calls=%async_computation.4 | async-start | bytes 2097152 | tf_op jit(solution)/shard_map/all_to_all | solution.py:13
  377.9 4.8 %collective-permute-start.8 = (f32[1,8,64]{2,1,0:T(8,128)S(1)}, f32[1,8,64]{2,1,0:T(8,128)S(1)}, u32[]{:S(2)}, u32[]{:S(2)}) collective-permute-start(f32[1,8,64]{2,1,0:T(8,128)S(1)} %slice_select_fusion.4), channel_id=1, source_target_pairs={{0,32},{32,0},{64,96},{96,64},{128,160},{160,128},{192,224},{224,1... | collective-permute-start | bytes 6152 | tf_op jit(solution)/shard_map/ppermute | solution.py:33
  (1 other events, 1.2 us)
Sparse Core Ops, SparseCore 0:
  367.2 39.7 reduce-scatter.1

commit v3 on v2

v3 whole, which is shorter than its diff:
```python
import functools

import jax
import jax.numpy as jnp
from jax import lax
from jax.experimental import pallas as pl
from jax.experimental.pallas import tpu as pltpu
from jax.sharding import Mesh, PartitionSpec as P

BF16 = jnp.bfloat16
F32 = jnp.float32
SEQ = ("z", "xh", "co")
DP = ("y", "xl")
VMEM = pl.BlockSpec(memory_space=pltpu.VMEM)
SMEM = pl.BlockSpec(memory_space=pltpu.SMEM)


def exchange(x, axis):
    return lax.all_to_all(x, axis, split_axis=0, concat_axis=0, tiled=True)


def spread(x, axis):
    n = lax.axis_size(axis)
    return exchange(jnp.broadcast_to(x[None], (n,) + x.shape), axis)


def gather(x, axes):
    out = x[None]
    for axis in reversed(axes):
        out = lax.all_gather(out, axis, axis=0, tiled=True)
    return out


def swap(x, axis, bits):
    n = lax.axis_size(axis)
    return lax.ppermute(x, axis, [(i, i ^ bits) for i in range(n)])


def local(body, out_shape, operands, in_specs=None, flops=0, scratch=()):
    outs = jax.tree.leaves(out_shape)
    moved = sum(a.size * a.dtype.itemsize for a in list(operands) + outs)
    return pl.pallas_call(
        body,
        grid=(1,),
        out_shape=out_shape,
        in_specs=in_specs or [VMEM] * len(operands),
        out_specs=jax.tree.map(lambda _: VMEM, out_shape),
        scratch_shapes=list(scratch),
        cost_estimate=pl.CostEstimate(flops=flops, bytes_accessed=moved, transcendentals=0),
        compiler_params=pltpu.CompilerParams(vmem_limit_bytes=40 << 20),
    )(*operands)


def shape(dims, dtype):
    return jax.ShapeDtypeStruct(dims, dtype)


def order_kernel(me_ref, *refs):
    out_ref = refs[-1]
    for far, ref in enumerate(refs[:-1]):
        for near in range(ref.shape[0]):
            out_ref[me_ref[0] ^ (far * ref.shape[0] + near)] = ref[near]


def gather_near(x, axis):
    n = lax.axis_size(axis)
    near = jnp.stack([x] + [swap(x, axis, k) for k in range(1, 4)])
    parts = [near] + [swap(near, axis, k) for k in range(4, n, 4)]
    return local(
        order_kernel,
        shape((n,) + x.shape, x.dtype),
        [lax.axis_index(axis)[None]] + parts,
        [SMEM] + [VMEM] * len(parts),
    )


def halve(x, axis, bit):
    low = lax.axis_index(axis) & bit == 0
    keep = jnp.where(low, x[0], x[1])
    give = jnp.where(low, x[1], x[0])
    return keep + swap(give, axis, bit)


def dot(a, b, ca=1, cb=0):
    return lax.dot_general(a, b, (((ca,), (cb,)), ((), ())), preferred_element_type=F32)


STEP = 32


def pack(tops, cols):
    return jnp.concatenate([t.reshape(-1, cols, t.shape[-1]) for t in tops], axis=1)


def rows_kernel(cols, first_ref, x_ref, out_ref):
    _, blocks, part, length = first_ref.shape
    per = STEP * cols // part
    for c in range(out_ref.shape[0] // STEP):
        tops = [
            dot(first_ref[c * per : (c + 1) * per, b].reshape(per * part, length), x_ref[b])
            for b in range(blocks)
        ]
        out_ref[c * STEP : (c + 1) * STEP] = pack(tops, cols).astype(BF16)


def gate_kernel(cols, x_ref, weight_ref, cot_ref, out_ref, slope_ref):
    blocks = x_ref.shape[0]
    for c in range(out_ref.shape[0] // STEP):
        rows = pl.ds(c * STEP * cols, STEP * cols)
        tops = []
        for b in range(blocks):
            gate = jax.nn.sigmoid(dot(x_ref[b, rows], weight_ref[...]))
            grad = cot_ref[b, rows].astype(F32) * gate
            slope_ref[b, rows] = grad * (1.0 - gate)
            tops.append(grad)
        out_ref[c * STEP : (c + 1) * STEP] = pack(tops, cols).astype(BF16)


LANES = 128


def unfold(src_ref, tmp_ref):
    tall = src_ref.shape[1]
    for c in range(0, src_ref.shape[0], STEP):
        piece = src_ref[c : c + STEP].astype(F32).reshape(STEP * tall, src_ref.shape[2])
        for k in range(tmp_ref.shape[0]):
            tmp_ref[k, pl.ds(c * tall, STEP * tall)] = piece[:, k * LANES : (k + 1) * LANES]


def fold(tmp_ref, dst_ref, first):
    tall = tmp_ref.shape[1] // dst_ref.shape[0]
    for c in range(0, dst_ref.shape[0], STEP):
        for k in range(tmp_ref.shape[0]):
            piece = tmp_ref[k, pl.ds(c * tall, STEP * tall)].reshape(STEP, tall, LANES)
            dst_ref[c : c + STEP, first : first + tall, k * LANES : (k + 1) * LANES] = piece.astype(BF16)


def column(tmp_ref, j, cols):
    rows = pl.ds(j, tmp_ref.shape[1] // cols, stride=cols)
    return jnp.concatenate([tmp_ref[k, rows] for k in range(tmp_ref.shape[0])], axis=1)


def set_column(tmp_ref, j, cols, value):
    rows = pl.ds(j, tmp_ref.shape[1] // cols, stride=cols)
    for k in range(tmp_ref.shape[0]):
        tmp_ref[k, rows] = value[:, k * LANES : (k + 1) * LANES]


def forward_kernel(second_ref, one_ref, grad_ref, both_ref, by_ref, tmp_ref, res_ref):
    _, cols, _, size = second_ref.shape
    rows = grad_ref.shape[1]
    for c in range(0, grad_ref.shape[0], STEP):
        both_ref[c : c + STEP, :rows] = grad_ref[c : c + STEP]
    unfold(one_ref, tmp_ref)
    for j in range(cols):
        mine = column(tmp_ref, j, cols).astype(BF16)
        by_ref[j] = mine
        set_column(res_ref, j, cols, dot(second_ref[:, j].reshape(size, size), mine))
    fold(res_ref, both_ref, rows)


def backward_kernel(second_ref, both_ref, by_ref, back_ref, part_ref, tmp_ref, res_ref):
    nd, cols, part, size = second_ref.shape
    unfold(both_ref, tmp_ref)
    for j in range(cols):
        mine = column(tmp_ref, j, cols).astype(BF16)
        weight = second_ref[:, j].reshape(size, size)
        set_column(res_ref, j, cols, dot(weight, mine, 0, 0))
        part_ref[j] = dot(mine, by_ref[j], 1, 1)
    fold(res_ref, back_ref, 0)


def delta_kernel(cols, both_ref, slope_ref, x_ref, weight_ref, input_ref, part_ref, delta_ref):
    blocks, length, _ = x_ref.shape
    n = STEP * cols
    for c in range(both_ref.shape[0] // STEP):
        two = both_ref[c * STEP : (c + 1) * STEP].astype(F32)
        for b in range(blocks):
            rows = pl.ds(c * n, n)
            mine = two[:, b * cols : (b + 1) * cols].reshape(n, two.shape[2])
            delta_ref[b, rows] = (mine * slope_ref[b, rows]).astype(BF16)
    for b in range(blocks):
        add = dot(delta_ref[b], x_ref[b], 0, 0)
        part_ref[...] = add if b == 0 else part_ref[...] + add
        input_ref[b] = dot(delta_ref[b], weight_ref[...], 1, 1).astype(BF16)


def unpack(src_ref, cols, b):
    piece = src_ref[...].astype(F32)[:, b * cols : (b + 1) * cols]
    return piece.reshape(-1, piece.shape[2]).astype(BF16)


def outer_kernel(cols, back_ref, x_ref, part_ref, by_ref):
    nd, blocks, part, length = part_ref.shape
    for b in range(blocks):
        by_ref[b] = unpack(back_ref, cols, b)
        part_ref[:, b] = dot(by_ref[b], x_ref[b], 1, 1).astype(BF16).reshape(nd, part, length)


def inputs_kernel(first_ref, by_ref, input_ref, out_ref):
    nd, blocks, part, length = first_ref.shape
    for b in range(blocks):
        through = dot(first_ref[:, b].reshape(nd * part, length), by_ref[b], 0, 0)
        out_ref[b] = (through + input_ref[b].astype(F32)).astype(BF16)


def per_device(inputs, out_grad, first_factor, second_factor, gate_weight):
    nd = lax.axis_size(DP)
    ns = lax.axis_size(SEQ)
    nz = lax.axis_size("z")
    _, rows, width = inputs.shape
    blocks, part, length = first_factor.shape
    cols, part2, size2 = second_factor.shape
    crows, cpart = gate_weight.shape
    x = inputs.reshape(blocks, length, width)
    cot = out_grad.reshape(blocks, length, width)
    tall = blocks * cols
    wide = 2 * rows * width * width
    cells = pltpu.VMEM((width // LANES, ns * tall, LANES), F32)

    first = spread(first_factor, DP)
    gate_part = gather_near(gate_weight, "z")
    one = local(
        functools.partial(rows_kernel, cols), shape((ns, tall, width), BF16), [first, x], flops=wide
    )
    one, gate_part, second_factor = lax.optimization_barrier((one, gate_part, second_factor))
    gate_part = gather(gate_part, SEQ[1:]).transpose(1, 0, 2, 3).reshape(width, cpart)
    second = gather(second_factor, DP)
    gate_full = gather(gate_part, DP).transpose(1, 0, 2).reshape(width, width)

    mixed_grad, slope = local(
        functools.partial(gate_kernel, cols),
        (shape((ns, tall, width), BF16), shape(x.shape, F32)),
        [x, gate_full, cot],
        flops=wide,
    )
    col_one = exchange(one, SEQ)
    both, by_col = local(
        forward_kernel,
        (shape((ns, 2 * tall, width), BF16), shape((cols, size2, width), BF16)),
        [second, col_one, mixed_grad],
        flops=wide // 4,
        scratch=[cells, cells],
    )
    both = exchange(both, SEQ)
    half = [
        pl.BlockSpec((ns, tall, width), functools.partial(lambda k, i: (0, k, 0), k))
        for k in range(2)
    ]
    col_back, spart = local(
        backward_kernel,
        (shape((ns, tall, width), BF16), shape((cols, size2, size2), F32)),
        [second, both, by_col],
        [VMEM, half[0], VMEM],
        flops=wide // 2,
        scratch=[cells, cells],
    )
    both, col_back, spart = lax.optimization_barrier((both, col_back, spart))
    back = exchange(col_back, SEQ)
    grad_second = lax.psum_scatter(spart, DP, scatter_dimension=1, tiled=True)

    gate_input, gsum = local(
        functools.partial(delta_kernel, cols),
        (shape(x.shape, BF16), shape((width, width), F32)),
        [both, slope, x, gate_full],
        [half[1], VMEM, VMEM, VMEM],
        flops=2 * wide,
        scratch=[pltpu.VMEM(x.shape, BF16)],
    )
    gsum = gsum.reshape(lax.axis_size("y"), 2, cpart, width)
    gsum = halve(gsum.transpose(1, 0, 2, 3), "xl", 1)
    gsum = halve(gsum.reshape(2, 2, cpart, width), "y", 2)
    gsum = halve(gsum, "y", 1)
    gsum, grad_second = lax.optimization_barrier((gsum, grad_second))
    gsum = gsum.T.reshape(ns // 2, 2, crows, cpart).transpose(1, 0, 2, 3)
    gsum = halve(gsum, "co", 1)
    gsum = halve(gsum.reshape(nz, 2, crows, cpart).transpose(1, 0, 2, 3), "xh", 1)
    fpart, by_row = local(
        functools.partial(outer_kernel, cols),
        (shape(first.shape, BF16), shape(x.shape, BF16)),
        [back, x],
        flops=wide,
    )
    gsum, fpart = lax.optimization_barrier((gsum, fpart))
    while nz > 1:
        nz //= 2
        gsum = halve(gsum.reshape(2, nz, crows, cpart), "z", nz)
    grad_gate = gsum.reshape(crows, cpart)
    grad_first = exchange(fpart, DP).astype(F32).sum(0)
    grad_inputs = local(inputs_kernel, shape(x.shape, BF16), [first, by_row, gate_input], flops=wide)
    return (grad_inputs.reshape(inputs.shape), grad_first, grad_second, grad_gate)


def solution(mesh):
    fine = Mesh(mesh.devices.reshape(16, 2, 2, 4, 2), SEQ + DP)
    specs = (P(SEQ, DP, None), P(SEQ, DP, None), P(SEQ, DP))
    return jax.shard_map(
        per_device,
        mesh=fine,
        in_specs=(P(DP, SEQ, None), P(DP, SEQ, None)) + specs,
        out_specs=(P(DP, SEQ, None),) + specs,
        check_vma=False,
    )
```

time: 418 us -> 398 us (0.952)
  waiting for transfers between devices: 154 us -> 85.4 us
  blocking collectives: 111 us -> 146 us
  matrix products: 15.6 us -> 0 us
  Pallas kernels: 0 us -> 11.8 us
  local copies, waits for them, and re-layouts: 10.6 us -> 21.3 us
  starting transfers between devices: 99.1 us -> 108 us
    all_to_all x4, waiting for transfers between devices: 108 us -> 13.6 us  [exchange(): return lax.all_to_all(x, axis, split_axis=0, concat_axis=0, tiled=True)]
    all_to_all x1, blocking collectives: 17.7 us -> 108 us  [exchange(): return lax.all_to_all(x, axis, split_axis=0, concat_axis=0, tiled=True)]
    all_gather x7 -> x6, blocking collectives: 92.9 us -> 38 us  [gather(): out = lax.all_gather(out, axis, axis=0, tiled=True)]
    ppermute x9 -> x15, starting transfers between devices: 35.9 us -> 77 us  [swap(): return lax.ppermute(x, axis, [(i, i ^ bits) for i in range(n)])]
    all_to_all x4, starting transfers between devices: 63.1 us -> 31.2 us  [exchange(): return lax.all_to_all(x, axis, split_axis=0, concat_axis=0, tiled=True)]
    dot_general x9 -> x0, matrix products: 15.6 us -> none  [the longest x1 2.99 us: per_device(): jnp.einsum('bjk,bjd->bkd', first, back, preferred_element_type=F32)]
    ppermute x9 -> x15, waiting for transfers between devices: 36.7 us -> 52 us  [swap(): return lax.ppermute(x, axis, [(i, i ^ bits) for i in range(n)])]
    pallas_call x0 -> x8, Pallas kernels: none -> 11.8 us  [local(): pl.pallas_call(body, grid=(1,), out_shape=out_shape, in_specs=in_specs or...]
  transfers between devices with their start and end apart: 14 -> 20, of which waited for: 11 -> 14; matrix products, arithmetic and copies ran while one was open for 4% -> 3% of each run, Pallas kernels for 0% -> 1%
where the time goes in v3:
time: 398 us; the launch traced here: 394 us
  blocking collectives  146 us (37%)
  starting transfers between devices  108 us (27%)
  waiting for transfers between devices  85.4 us (21%)
  local copies, waits for them, and re-layouts  21.3 us (5%)
  between operations  14.5 us (4%)
  Pallas kernels  11.8 us (3%)
  other arithmetic  6.66 us (2%)
    all_to_all x1, blocking collectives, exchange(): return lax.all_to_all(x, axis, split_axis=0, concat_axis=0, tiled=True)  108 us
    ppermute x15, starting transfers between devices, swap(): return lax.ppermute(x, axis, [(i, i ^ bits) for i in range(n)])  77 us
    ppermute x15, waiting for transfers between devices, swap(): return lax.ppermute(x, axis, [(i, i ^ bits) for i in range(n)])  52 us
    all_gather x6, blocking collectives, gather(): out = lax.all_gather(out, axis, axis=0, tiled=True)  38 us
    all_to_all x4, starting transfers between devices, exchange(): return lax.all_to_all(x, axis, split_axis=0, concat_axis=0, tiled=True)  31.2 us
    reduce_scatter x1, waiting for transfers between devices, per_device(): grad_second = lax.psum_scatter(spart, DP, scatter_dimension=1, tiled=True)  19.8 us
    all_to_all x4, waiting for transfers between devices, exchange(): return lax.all_to_all(x, axis, split_axis=0, concat_axis=0, tiled=True)  13.6 us
    unnamed x38, local copies, waits for them, and re-layouts  12.3 us
  transfers between devices with their start and end apart: 20, of which 14 were waited for; matrix products, arithmetic and copies ran while one was open for 3% of the time, Pallas kernels for 1%

profile of v3, /device:TPU:1, one launch (start us, length us, event | category | flops | bytes accessed | tf_op | source)
XLA Modules:
  0.0 394.3 jit_solution(8373082132028634656)
XLA Ops:
  9.2 5.9 %all-to-all-start = ((bf16[8,2,64,512]{3,2,1,0:T(8,128)(2,1)}), bf16[8,2,64,512]{3,2,1,0:T(8,128)(2,1)S(1)}, u32[]{:S(2)}, u32[]{:S(2)}) async-start(bf16[8,2,64,512]{3,2,1,0:T(8,128)(2,1)} %broadcast_in_dim.15), calls=%async_computation | async-start | bytes 2097152 | tf_op jit(solution)/shard_map/all_to_all | solution.py:19
  18.8 4.9 %collective-permute-start.1 = (bf16[8,64]{1,0:T(8,128)(2,1)S(1)}, bf16[8,64]{1,0:T(8,128)(2,1)S(1)}, u32[]{:S(2)}, u32[]{:S(2)}) collective-permute-start(bf16[8,64]{1,0:T(8,128)(2,1)S(1)} %copy-done.18), channel_id=1, source_target_pairs={{0,64},{32,96},{64,0},{96,32},{128,192},{160,224},{192,128},{224,1... | collective-permute-start | bytes 3080 | tf_op jit(solution)/shard_map/ppermute | solution.py:36
  25.6 4.5 %collective-permute-done.2 = bf16[8,64]{1,0:T(8,128)(2,1)S(1)} collective-permute-done((bf16[8,64]{1,0:T(8,128)(2,1)S(1)}, bf16[8,64]{1,0:T(8,128)(2,1)S(1)}, u32[]{:S(2)}, u32[]{:S(2)}) %collective-permute-start.2) | collective-permute-done | bytes 1056 | tf_op jit(solution)/shard_map/ppermute | solution.py:36
  30.1 8.8 %collective-permute-start.3 = (bf16[4,8,64]{2,1,0:T(8,128)(2,1)S(1)}, bf16[4,8,64]{2,1,0:T(8,128)(2,1)S(1)}, u32[]{:S(2)}, u32[]{:S(2)}) collective-permute-start(bf16[4,8,64]{2,1,0:T(8,128)(2,1)S(1)} %pad_maximum_fusion.refs_0_), channel_id=1, source_target_pairs={{0,128},{32,160},{64,192},{96,224},{128,0},{160,32},{192,64},{224,... | collective-permute-start | bytes 12296 | tf_op jit(solution)/shard_map/ppermute | solution.py:36
  38.9 7.9 %collective-permute-start.4 = (bf16[4,8,64]{2,1,0:T(8,128)(2,1)S(1)}, bf16[4,8,64]{2,1,0:T(8,128)(2,1)S(1)}, u32[]{:S(2)}, u32[]{:S(2)}) collective-permute-start(bf16[4,8,64]{2,1,0:T(8,128)(2,1)S(1)} %pad_maximum_fusion.refs_0_), channel_id=1, source_target_pairs={{0,256},{32,288},{64,320},{96,352},{128,384},{160,416},{192,448},{... | collective-permute-start | bytes 12296 | tf_op jit(solution)/shard_map/ppermute | solution.py:36
  57.2 12.8 %all-to-all-start.1 = ((bf16[64,16,512]{2,1,0:T(8,128)(2,1)}), bf16[64,16,512]{2,1,0:T(8,128)(2,1)S(1)}, u32[]{:S(2)}, u32[]{:S(2)}) async-start(bf16[64,16,512]{2,1,0:T(8,128)(2,1)} %shard_map.84), calls=%async_computation.1 | async-start | bytes 2097152 | tf_op jit(solution)/shard_map/all_to_all | solution.py:19
  72.0 5.6 %all_gather.21 = bf16[4,16,8,64]{3,2,0,1:T(8,128)(2,1)S(1)} all-gather(bf16[2,16,8,64]{3,2,0,1:T(8,128)(2,1)S(1)} %copy.31), channel_id=1, replica_groups=mesh['z'=16,'xh'=2,'co'=2,'y'=4,'xl'=2] {'xh'}, dimensions={0}, use_global_device_ids=true | all-gather | bytes 98304 | tf_op jit(solution)/shard_map/all_gather | solution.py:30
  77.7 4.2 %all_gather.22 = bf16[2,512,64]{1,2,0:T(8,128)(2,1)S(1)} all-gather(bf16[1,512,64]{1,2,0:T(8,128)(2,1)S(1)} %copy.32), channel_id=1, replica_groups=mesh['z'=16,'xh'=2,'co'=2,'y'=4,'xl'=2] {'xl'}, dimensions={0}, use_global_device_ids=true | all-gather | bytes 196608 | tf_op jit(solution)/shard_map/all_gather | solution.py:30
  81.9 11.8 %all_gather.23 = bf16[8,512,64]{1,2,0:T(8,128)(2,1)S(1)} all-gather(bf16[2,512,64]{1,2,0:T(8,128)(2,1)S(1)} %all_gather.22), channel_id=1, replica_groups=mesh['z'=16,'xh'=2,'co'=2,'y'=4,'xl'=2] {'y'}, dimensions={0}, use_global_device_ids=true | all-gather | bytes 655360 | tf_op jit(solution)/shard_map/all_gather | solution.py:30
  94.0 4.0 %all-gather = bf16[16,16,128]{2,1,0:T(8,128)(2,1)S(1)} all-gather(bf16[8,16,128]{2,1,0:T(8,128)(2,1)S(1)} %copy-done.17), channel_id=2, replica_groups=mesh['z'=16,'xh'=2,'co'=2,'y'=4,'xl'=2] {'xl'}, dimensions={0}, use_global_device_ids=true | all-gather | bytes 98304 | tf_op jit(solution)/shard_map/all_gather | solution.py:30
  102.3 10.5 %all_gather.19.second_ref = bf16[8,8,16,128]{3,2,1,0:T(8,128)(2,1)S(1)} all-gather(bf16[2,8,16,128]{3,2,1,0:T(8,128)(2,1)S(1)} %bitcast.87), channel_id=1, replica_groups=mesh['z'=16,'xh'=2,'co'=2,'y'=4,'xl'=2] {'y'}, dimensions={0}, use_global_device_ids=true | all-gather | bytes 327680 | tf_op jit(solution)/shard_map/all_gather | solution.py:30
  112.7 11.3 %all-to-all-done.1.one_ref = bf16[64,16,512]{2,1,0:T(8,128)(2,1)S(1)} async-done(((bf16[64,16,512]{2,1,0:T(8,128)(2,1)}), bf16[64,16,512]{2,1,0:T(8,128)(2,1)S(1)}, u32[]{:S(2)}, u32[]{:S(2)}) %all-to-all-start.1) | async-done | bytes 1048608 | tf_op jit(solution)/shard_map/all_to_all | solution.py:19
  126.6 108.3 %all_to_all.25.both_ref = bf16[64,32,512]{2,1,0:T(8,128)(2,1)S(1)} all-to-all(bf16[64,32,512]{2,1,0:T(8,128)(2,1)S(1)} %get-tuple-element.28), channel_id=1, replica_groups=mesh['z'=16,'xh'=2,'co'=2,'y'=4,'xl'=2] {'z','xh','co'}, dimensions={0} | all-to-all | bytes 4194304 | tf_op jit(solution)/shard_map/all_to_all | solution.py:19
  237.9 8.2 %all-to-all-start.3 = ((bf16[64,16,512]{2,1,0:T(8,128)(2,1)}), bf16[64,16,512]{2,1,0:T(8,128)(2,1)}, u32[]{:S(2)}, u32[]{:S(2)}) async-start(bf16[64,16,512]{2,1,0:T(8,128)(2,1)} %copy-done.9), calls=%async_computation.3 | async-start | bytes 2097152 | tf_op jit(solution)/shard_map/all_to_all | solution.py:19
  260.3 17.0 %collective-permute-done.6 = f32[4,64,512]{2,1,0:T(8,128)} collective-permute-done((f32[4,64,512]{2,1,0:T(8,128)}, f32[4,64,512]{2,1,0:T(8,128)}, u32[]{:S(2)}, u32[]{:S(2)}) %collective-permute-start.6) | collective-permute-done | bytes 524320 | tf_op jit(solution)/shard_map/ppermute | solution.py:36
  285.2 12.5 %collective-permute-done.7 = f32[2,64,512]{1,2,0:T(8,128)S(1)} collective-permute-done((f32[2,64,512]{1,2,0:T(8,128)S(1)}, f32[2,64,512]{1,2,0:T(8,128)S(1)}, u32[]{:S(2)}, u32[]{:S(2)}) %collective-permute-start.7) | collective-permute-done | bytes 262176 | tf_op jit(solution)/shard_map/ppermute | solution.py:36
  302.6 5.1 %collective-permute-done.8 = f32[64,512]{0,1:T(8,128)S(1)} collective-permute-done((f32[64,512]{0,1:T(8,128)S(1)}, f32[64,512]{0,1:T(8,128)S(1)}, u32[]{:S(2)}, u32[]{:S(2)}) %collective-permute-start.8) | collective-permute-done | bytes 131104 | tf_op jit(solution)/shard_map/ppermute | solution.py:36
  307.8 19.8 %reduce-scatter.2.cloned.1.call-done = f32[8,16,128]{2,1,0:T(8,128)} async-done(((f32[8,128,128]{2,1,0:T(8,128)}), f32[8,16,128]{2,1,0:T(8,128)}) %reduce-scatter.2.cloned.1.call-update) | async-done | bytes 65552 | tf_op jit(solution)/shard_map/reduce_scatter | solution.py:260
  327.6 7.3 %collective-permute-start.9 = (f32[32,8,64]{2,1,0:T(8,128)S(1)}, f32[32,8,64]{2,1,0:T(8,128)S(1)}, u32[]{:S(2)}, u32[]{:S(2)}) collective-permute-start(f32[32,8,64]{2,1,0:T(8,128)S(1)} %select_bitcast_fusion.2), channel_id=1, source_target_pairs={{0,8},{8,0},{1,9},{9,1},{2,10},{10,2},{3,11},{11,3},{4,12},{12,4},... | collective-permute-start | bytes 196616 | tf_op jit(solution)/shard_map/ppermute | solution.py:36
  336.0 4.2 %collective-permute-start.10 = (f32[16,8,64]{2,1,0:T(8,128)S(1)}, f32[16,8,64]{2,1,0:T(8,128)S(1)}, u32[]{:S(2)}, u32[]{:S(2)}) collective-permute-start(f32[16,8,64]{2,1,0:T(8,128)S(1)} %select_bitcast_fusion.3), channel_id=1, source_target_pairs={{0,16},{16,0},{1,17},{17,1},{2,18},{18,2},{3,19},{19,3},{4,20},{20... | collective-permute-start | bytes 98312 | tf_op jit(solution)/shard_map/ppermute | solution.py:36
  346.6 12.6 %collective-permute-start.11 = (f32[8,8,64]{2,1,0:T(8,128)S(1)}, f32[8,8,64]{2,1,0:T(8,128)S(1)}, u32[]{:S(2)}, u32[]{:S(2)}) collective-permute-start(f32[8,8,64]{2,1,0:T(8,128)S(1)} %slice_select_fusion.1), channel_id=1, source_target_pairs={{0,256},{32,288},{64,320},{96,352},{128,384},{160,416},{192,448},{... | collective-permute-start | bytes 49160 | tf_op jit(solution)/shard_map/ppermute | solution.py:36
  360.7 7.5 %collective-permute-start.12 = (f32[4,8,64]{2,1,0:T(8,128)S(1)}, f32[4,8,64]{2,1,0:T(8,128)S(1)}, u32[]{:S(2)}, u32[]{:S(2)}) collective-permute-start(f32[4,8,64]{2,1,0:T(8,128)S(1)} %slice_select_fusion.2), channel_id=1, source_target_pairs={{0,128},{32,160},{64,192},{96,224},{128,0},{160,32},{192,64},{224,... | collective-permute-start | bytes 24584 | tf_op jit(solution)/shard_map/ppermute | solution.py:36
  368.1 4.3 %all-to-all-start.4 = ((bf16[8,2,64,512]{3,2,1,0:T(8,128)(2,1)}), bf16[8,2,64,512]{3,2,1,0:T(8,128)(2,1)}, u32[]{:S(2)}, u32[]{:S(2)}) async-start(bf16[8,2,64,512]{3,2,1,0:T(8,128)(2,1)} %get-tuple-element.41), calls=%async_computation.5 | async-start | bytes 2097152 | tf_op jit(solution)/shard_map/all_to_all | solution.py:19
  372.4 4.3 %collective-permute-start.13 = (f32[2,8,64]{2,1,0:T(8,128)S(1)}, f32[2,8,64]{2,1,0:T(8,128)S(1)}, u32[]{:S(2)}, u32[]{:S(2)}) collective-permute-start(f32[2,8,64]{2,1,0:T(8,128)S(1)} %slice_select_fusion.3), channel_id=1, source_target_pairs={{0,64},{32,96},{64,0},{96,32},{128,192},{160,224},{192,128},{224,1... | collective-permute-start | bytes 12296 | tf_op jit(solution)/shard_map/ppermute | solution.py:36
  (97 shorter events, 76.3 us)
Async XLA Ops:
  7.2 48.4 %copy-start = (bf16[1,1024,512]{2,1,0:T(8,128)(2,1)S(1)}, bf16[1,1024,512]{2,1,0:T(8,128)(2,1)}, u32[]{:S(2)}) copy-start(bf16[1,1024,512]{2,1,0:T(8,128)(2,1)} %param.5) | copy-start | bytes 3145732
  9.2 46.3 %all-to-all-start = ((bf16[8,2,64,512]{3,2,1,0:T(8,128)(2,1)}), bf16[8,2,64,512]{3,2,1,0:T(8,128)(2,1)S(1)}, u32[]{:S(2)}, u32[]{:S(2)}) async-start(bf16[8,2,64,512]{3,2,1,0:T(8,128)(2,1)} %broadcast_in_dim.15), calls=%async_computation | async-start | bytes 2097152 | tf_op jit(solution)/shard_map/all_to_all | solution.py:19
  15.2 10.4 %collective-permute-start = (bf16[8,64]{1,0:T(8,128)(2,1)S(1)}, bf16[8,64]{1,0:T(8,128)(2,1)S(1)}, u32[]{:S(2)}, u32[]{:S(2)}) collective-permute-start(bf16[8,64]{1,0:T(8,128)(2,1)S(1)} %copy-done.18), channel_id=1, source_target_pairs={{0,32},{32,0},{64,96},{96,64},{128,160},{160,128},{192,224},{224,1... | collective-permute-start | bytes 3080 | tf_op jit(solution)/shard_map/ppermute | solution.py:36
  18.8 6.8 %collective-permute-start.1 = (bf16[8,64]{1,0:T(8,128)(2,1)S(1)}, bf16[8,64]{1,0:T(8,128)(2,1)S(1)}, u32[]{:S(2)}, u32[]{:S(2)}) collective-permute-start(bf16[8,64]{1,0:T(8,128)(2,1)S(1)} %copy-done.18), channel_id=1, source_target_pairs={{0,64},{32,96},{64,0},{96,32},{128,192},{160,224},{192,128},{224,1... | collective-permute-start | bytes 3080 | tf_op jit(solution)/shard_map/ppermute | solution.py:36
  23.7 6.4 %collective-permute-start.2 = (bf16[8,64]{1,0:T(8,128)(2,1)S(1)}, bf16[8,64]{1,0:T(8,128)(2,1)S(1)}, u32[]{:S(2)}, u32[]{:S(2)}) collective-permute-start(bf16[8,64]{1,0:T(8,128)(2,1)S(1)} %copy-done.18), channel_id=1, source_target_pairs={{0,96},{32,64},{64,32},{96,0},{128,224},{160,192},{192,160},{224,1... | collective-permute-start | bytes 3080 | tf_op jit(solution)/shard_map/ppermute | solution.py:36
  30.1 18.7 %collective-permute-start.3 = (bf16[4,8,64]{2,1,0:T(8,128)(2,1)S(1)}, bf16[4,8,64]{2,1,0:T(8,128)(2,1)S(1)}, u32[]{:S(2)}, u32[]{:S(2)}) collective-permute-start(bf16[4,8,64]{2,1,0:T(8,128)(2,1)S(1)} %pad_maximum_fusion.refs_0_), channel_id=1, source_target_pairs={{0,128},{32,160},{64,192},{96,224},{128,0},{160,32},{192,64},{224,... | collective-permute-start | bytes 12296 | tf_op jit(solution)/shard_map/ppermute | solution.py:36
  38.9 13.1 %collective-permute-start.4 = (bf16[4,8,64]{2,1,0:T(8,128)(2,1)S(1)}, bf16[4,8,64]{2,1,0:T(8,128)(2,1)S(1)}, u32[]{:S(2)}, u32[]{:S(2)}) collective-permute-start(bf16[4,8,64]{2,1,0:T(8,128)(2,1)S(1)} %pad_maximum_fusion.refs_0_), channel_id=1, source_target_pairs={{0,256},{32,288},{64,320},{96,352},{128,384},{160,416},{192,448},{... | collective-permute-start | bytes 12296 | tf_op jit(solution)/shard_map/ppermute | solution.py:36
  46.9 8.6 %collective-permute-start.5 = (bf16[4,8,64]{2,1,0:T(8,128)(2,1)S(1)}, bf16[4,8,64]{2,1,0:T(8,128)(2,1)S(1)}, u32[]{:S(2)}, u32[]{:S(2)}) collective-permute-start(bf16[4,8,64]{2,1,0:T(8,128)(2,1)S(1)} %pad_maximum_fusion.refs_0_), channel_id=1, source_target_pairs={{0,384},{32,416},{64,448},{96,480},{128,256},{160,288},{192,320},{... | collective-permute-start | bytes 12296 | tf_op jit(solution)/shard_map/ppermute | solution.py:36
  57.2 36.7 %copy-start.17 = (bf16[8,16,128]{2,1,0:T(8,128)(2,1)S(1)}, bf16[8,16,128]{2,1,0:T(8,128)(2,1)}, u32[]{:S(2)}) copy-start(bf16[8,16,128]{2,1,0:T(8,128)(2,1)} %param.8) | copy-start | bytes 98308
  57.2 66.8 %all-to-all-start.1 = ((bf16[64,16,512]{2,1,0:T(8,128)(2,1)}), bf16[64,16,512]{2,1,0:T(8,128)(2,1)S(1)}, u32[]{:S(2)}, u32[]{:S(2)}) async-start(bf16[64,16,512]{2,1,0:T(8,128)(2,1)} %shard_map.84), calls=%async_computation.1 | async-start | bytes 2097152 | tf_op jit(solution)/shard_map/all_to_all | solution.py:19
  237.9 104.6 %all-to-all-start.3 = ((bf16[64,16,512]{2,1,0:T(8,128)(2,1)}), bf16[64,16,512]{2,1,0:T(8,128)(2,1)}, u32[]{:S(2)}, u32[]{:S(2)}) async-start(bf16[64,16,512]{2,1,0:T(8,128)(2,1)} %copy-done.9), calls=%async_computation.3 | async-start | bytes 2097152 | tf_op jit(solution)/shard_map/all_to_all | solution.py:19
  246.1 81.5 %reduce-scatter.2.cloned.1.call-start = ((), (), s32[]{:S(2)}) async-start(), calls=%async_computation.6 | async-start | bytes 589824 | tf_op jit(solution)/shard_map/reduce_scatter | solution.py:260
  257.4 19.9 %collective-permute-start.6 = (f32[4,64,512]{2,1,0:T(8,128)}, f32[4,64,512]{2,1,0:T(8,128)}, u32[]{:S(2)}, u32[]{:S(2)}) collective-permute-start(f32[4,64,512]{2,1,0:T(8,128)} %copy.36), channel_id=1, source_target_pairs={{0,1},{1,0},{2,3},{3,2},{4,5},{5,4},{6,7},{7,6},{8,9},{9,8},{10,11... | collective-permute-start | bytes 1572872 | tf_op jit(solution)/shard_map/ppermute | solution.py:36
  282.0 15.7 %collective-permute-start.7 = (f32[2,64,512]{1,2,0:T(8,128)S(1)}, f32[2,64,512]{1,2,0:T(8,128)S(1)}, u32[]{:S(2)}, u32[]{:S(2)}) collective-permute-start(f32[2,64,512]{1,2,0:T(8,128)S(1)} %slice_select_fusion), channel_id=1, source_target_pairs={{0,4},{2,6},{4,0},{6,2},{1,5},{3,7},{5,1},{7,3},{8,12},{10,14},{12... | collective-permute-start | bytes 786440 | tf_op jit(solution)/shard_map/ppermute | solution.py:36
  299.0 8.7 %collective-permute-start.8 = (f32[64,512]{0,1:T(8,128)S(1)}, f32[64,512]{0,1:T(8,128)S(1)}, u32[]{:S(2)}, u32[]{:S(2)}) collective-permute-start(f32[64,512]{0,1:T(8,128)S(1)} %select_bitcast_fusion.1), channel_id=1, source_target_pairs={{0,2},{2,0},{4,6},{6,4},{1,3},{3,1},{5,7},{7,5},{8,10},{10,8},{12,... | collective-permute-start | bytes 393224 | tf_op jit(solution)/shard_map/ppermute | solution.py:36
  327.6 8.3 %collective-permute-start.9 = (f32[32,8,64]{2,1,0:T(8,128)S(1)}, f32[32,8,64]{2,1,0:T(8,128)S(1)}, u32[]{:S(2)}, u32[]{:S(2)}) collective-permute-start(f32[32,8,64]{2,1,0:T(8,128)S(1)} %select_bitcast_fusion.2), channel_id=1, source_target_pairs={{0,8},{8,0},{1,9},{9,1},{2,10},{10,2},{3,11},{11,3},{4,12},{12,4},... | collective-permute-start | bytes 196616 | tf_op jit(solution)/shard_map/ppermute | solution.py:36
  336.0 6.5 %collective-permute-start.10 = (f32[16,8,64]{2,1,0:T(8,128)S(1)}, f32[16,8,64]{2,1,0:T(8,128)S(1)}, u32[]{:S(2)}, u32[]{:S(2)}) collective-permute-start(f32[16,8,64]{2,1,0:T(8,128)S(1)} %select_bitcast_fusion.3), channel_id=1, source_target_pairs={{0,16},{16,0},{1,17},{17,1},{2,18},{18,2},{3,19},{19,3},{4,20},{20... | collective-permute-start | bytes 98312 | tf_op jit(solution)/shard_map/ppermute | solution.py:36
  342.5 37.8 %copy-start.2 = (bf16[8,2,64,512]{3,2,1,0:T(8,128)(2,1)S(1)}, bf16[8,2,64,512]{3,2,1,0:T(8,128)(2,1)}, u32[]{:S(2)}) copy-start(bf16[8,2,64,512]{3,2,1,0:T(8,128)(2,1)} %copy-done.1) | copy-start | bytes 3145732
  342.5 37.8 %copy-start.13 = (bf16[2,512,512]{2,1,0:T(8,128)(2,1)S(1)}, bf16[2,512,512]{2,1,0:T(8,128)(2,1)}, u32[]{:S(2)}) copy-start(bf16[2,512,512]{2,1,0:T(8,128)(2,1)} %copy-done.12) | copy-start | bytes 3145732
  346.6 14.1 %collective-permute-start.11 = (f32[8,8,64]{2,1,0:T(8,128)S(1)}, f32[8,8,64]{2,1,0:T(8,128)S(1)}, u32[]{:S(2)}, u32[]{:S(2)}) collective-permute-start(f32[8,8,64]{2,1,0:T(8,128)S(1)} %slice_select_fusion.1), channel_id=1, source_target_pairs={{0,256},{32,288},{64,320},{96,352},{128,384},{160,416},{192,448},{... | collective-permute-start | bytes 49160 | tf_op jit(solution)/shard_map/ppermute | solution.py:36
  360.7 11.7 %collective-permute-start.12 = (f32[4,8,64]{2,1,0:T(8,128)S(1)}, f32[4,8,64]{2,1,0:T(8,128)S(1)}, u32[]{:S(2)}, u32[]{:S(2)}) collective-permute-start(f32[4,8,64]{2,1,0:T(8,128)S(1)} %slice_select_fusion.2), channel_id=1, source_target_pairs={{0,128},{32,160},{64,192},{96,224},{128,0},{160,32},{192,64},{224,... | collective-permute-start | bytes 24584 | tf_op jit(solution)/shard_map/ppermute | solution.py:36
  368.1 17.2 %all-to-all-start.4 = ((bf16[8,2,64,512]{3,2,1,0:T(8,128)(2,1)}), bf16[8,2,64,512]{3,2,1,0:T(8,128)(2,1)}, u32[]{:S(2)}, u32[]{:S(2)}) async-start(bf16[8,2,64,512]{3,2,1,0:T(8,128)(2,1)} %get-tuple-element.41), calls=%async_computation.5 | async-start | bytes 2097152 | tf_op jit(solution)/shard_map/all_to_all | solution.py:19
  372.4 5.3 %collective-permute-start.13 = (f32[2,8,64]{2,1,0:T(8,128)S(1)}, f32[2,8,64]{2,1,0:T(8,128)S(1)}, u32[]{:S(2)}, u32[]{:S(2)}) collective-permute-start(f32[2,8,64]{2,1,0:T(8,128)S(1)} %slice_select_fusion.3), channel_id=1, source_target_pairs={{0,64},{32,96},{64,0},{96,32},{128,192},{160,224},{192,128},{224,1... | collective-permute-start | bytes 12296 | tf_op jit(solution)/shard_map/ppermute | solution.py:36
  377.8 4.7 %collective-permute-start.14 = (f32[1,8,64]{2,1,0:T(8,128)S(1)}, f32[1,8,64]{2,1,0:T(8,128)S(1)}, u32[]{:S(2)}, u32[]{:S(2)}) collective-permute-start(f32[1,8,64]{2,1,0:T(8,128)S(1)} %slice_select_fusion.4), channel_id=1, source_target_pairs={{0,32},{32,0},{64,96},{96,64},{128,160},{160,128},{192,224},{224,1... | collective-permute-start | bytes 6152 | tf_op jit(solution)/shard_map/ppermute | solution.py:36
  (15 other events, 88.4 us)
Sparse Core Ops, SparseCore 0:
  285.3 42.2 reduce-scatter.1

commit v4 on v3

v4 whole, which is shorter than its diff:
```python
import functools

import jax
import jax.numpy as jnp
from jax import lax
from jax.experimental import pallas as pl
from jax.experimental.pallas import tpu as pltpu
from jax.sharding import Mesh, PartitionSpec as P

BF16 = jnp.bfloat16
F32 = jnp.float32
SEQ = ("z", "xh", "co")
DP = ("y", "xl")
VMEM = pl.BlockSpec(memory_space=pltpu.VMEM)
ANY = pl.BlockSpec(memory_space=pl.ANY)
SMEM = pl.BlockSpec(memory_space=pltpu.SMEM)


def exchange(x, axis):
    return lax.all_to_all(x, axis, split_axis=0, concat_axis=0, tiled=True)


def gather(x, axes):
    out = x[None]
    for axis in reversed(axes):
        out = lax.all_gather(out, axis, axis=0, tiled=True)
    return out


def swap(x, axis, bits):
    n = lax.axis_size(axis)
    return lax.ppermute(x, axis, [(i, i ^ bits) for i in range(n)])


def local(body, out_shape, operands, in_specs=None, flops=0, scratch=()):
    outs = jax.tree.leaves(out_shape)
    moved = sum(a.size * a.dtype.itemsize for a in list(operands) + outs)
    return pl.pallas_call(
        body,
        grid=(1,),
        out_shape=out_shape,
        in_specs=in_specs or [VMEM] * len(operands),
        out_specs=jax.tree.map(lambda _: VMEM, out_shape),
        scratch_shapes=list(scratch),
        cost_estimate=pl.CostEstimate(flops=flops, bytes_accessed=moved, transcendentals=0),
        compiler_params=pltpu.CompilerParams(vmem_limit_bytes=28 << 20),
    )(*operands)


def shape(dims, dtype):
    return jax.ShapeDtypeStruct(dims, dtype)


def order_kernel(me_ref, low_ref, high_ref, after_ref, out_ref):
    del after_ref
    n = low_ref.shape[0]
    for k in range(n):
        out_ref[me_ref[0] ^ k] = low_ref[k]
        out_ref[me_ref[0] ^ (n + k)] = high_ref[k]


def double(x, axis):
    low, bit = x[None], 1
    while True:
        high = swap(low, axis, bit)
        bit *= 2
        if bit == lax.axis_size(axis):
            return low, high
        low = jnp.concatenate([low, high])


def halve(x, axis, bit):
    low = lax.axis_index(axis) & bit == 0
    keep = jnp.where(low, x[0], x[1])
    give = jnp.where(low, x[1], x[0])
    return keep, swap(give, axis, bit)


def dot(a, b, ca=1, cb=0):
    return lax.dot_general(a, b, (((ca,), (cb,)), ((), ())), preferred_element_type=F32)


STEP = 32
LANES = 128


def pack(tops, cols):
    return jnp.concatenate([t.reshape(-1, cols, t.shape[-1]) for t in tops], axis=1)


def beside(j, part, width):
    per = width // LANES
    return pl.ds((j // per) * part, part), pl.ds((j % per) * LANES, LANES)


def weights_kernel(first_ref, second_ref, out_ref):
    blocks, part, width = first_ref.shape
    for d in range(out_ref.shape[0]):
        for b in range(blocks):
            out_ref[d, b * part : (b + 1) * part] = first_ref[b]
        for j in range(second_ref.shape[0]):
            rows, lanes = beside(j, second_ref.shape[1], width)
            out_ref[d, pl.ds(blocks * part + rows.start, rows.size), lanes] = second_ref[j]


def second_of(second_ref, j):
    nd, _, width = second_ref.shape
    rows, lanes = beside(j, LANES // nd, width)
    return second_ref[:, rows, lanes].reshape(LANES, LANES)


def rows_kernel(cols, weights_ref, x_ref, out_ref):
    nd, (blocks, length, _) = weights_ref.shape[0], x_ref.shape
    part = length // nd
    per = STEP * cols // part
    for c in range(out_ref.shape[0] // STEP):
        tops = []
        for b in range(blocks):
            mine = weights_ref[c * per : (c + 1) * per, b * part : (b + 1) * part]
            tops.append(dot(mine.reshape(per * part, length), x_ref[b]))
        out_ref[c * STEP : (c + 1) * STEP] = pack(tops, cols).astype(BF16)


def gate_kernel(cols, x_ref, weight_ref, cot_ref, out_ref, slope_ref):
    blocks = x_ref.shape[0]
    for c in range(out_ref.shape[0] // STEP):
        rows = pl.ds(c * STEP * cols, STEP * cols)
        tops = []
        for b in range(blocks):
            gate = jax.nn.sigmoid(dot(x_ref[b, rows], weight_ref[...]))
            grad = cot_ref[b, rows].astype(F32) * gate
            slope_ref[b, rows] = grad * (1.0 - gate)
            tops.append(grad)
        out_ref[c * STEP : (c + 1) * STEP] = pack(tops, cols).astype(BF16)


def unfold(src_ref, tmp_ref):
    tall = src_ref.shape[1]
    for c in range(0, src_ref.shape[0], STEP):
        piece = src_ref[c : c + STEP].astype(F32).reshape(STEP * tall, src_ref.shape[2])
        for k in range(tmp_ref.shape[0]):
            tmp_ref[k, pl.ds(c * tall, STEP * tall)] = piece[:, k * LANES : (k + 1) * LANES]


def fold(tmp_ref, dst_ref):
    tall = dst_ref.shape[1]
    for c in range(0, dst_ref.shape[0], STEP):
        rows = pl.ds(c * tall, STEP * tall)
        piece = jnp.concatenate([tmp_ref[k, rows] for k in range(tmp_ref.shape[0])], axis=1)
        dst_ref[c : c + STEP] = piece.reshape(STEP, tall, dst_ref.shape[2]).astype(BF16)


def column(tmp_ref, j, cols):
    rows = pl.ds(j, tmp_ref.shape[1] // cols, stride=cols)
    return jnp.concatenate([tmp_ref[k, rows] for k in range(tmp_ref.shape[0])], axis=1)


def set_column(tmp_ref, j, cols, value):
    rows = pl.ds(j, tmp_ref.shape[1] // cols, stride=cols)
    for k in range(tmp_ref.shape[0]):
        tmp_ref[k, rows] = value[:, k * LANES : (k + 1) * LANES]


def forward_kernel(second_ref, one_ref, two_ref, by_ref, tmp_ref, res_ref):
    unfold(one_ref, tmp_ref)
    cols = by_ref.shape[0]
    for j in range(cols):
        mine = column(tmp_ref, j, cols).astype(BF16)
        by_ref[j] = mine
        set_column(res_ref, j, cols, dot(second_of(second_ref, j), mine))
    fold(res_ref, two_ref)


def backward_kernel(second_ref, grad_ref, by_ref, back_ref, part_ref, tmp_ref, res_ref):
    unfold(grad_ref, tmp_ref)
    cols = by_ref.shape[0]
    nd, _, width = part_ref.shape
    for j in range(cols):
        mine = column(tmp_ref, j, cols).astype(BF16)
        set_column(res_ref, j, cols, dot(second_of(second_ref, j), mine, 0, 0))
        rows, lanes = beside(j, LANES // nd, width)
        part = dot(mine, by_ref[j], 1, 1).reshape(nd, LANES // nd, LANES)
        part_ref[:, rows, lanes] = part.astype(BF16)
    fold(res_ref, back_ref)


def delta_kernel(
    cols, me_ref, two_ref, slope_ref, x_ref, weight_ref, input_ref, keep_ref, give_ref, delta_ref, sum_ref
):
    blocks, length, _ = x_ref.shape
    n = STEP * cols
    for c in range(two_ref.shape[0] // STEP):
        two = two_ref[c * STEP : (c + 1) * STEP].astype(F32)
        for b in range(blocks):
            rows = pl.ds(c * n, n)
            mine = two[:, b * cols : (b + 1) * cols].reshape(n, two.shape[2])
            delta_ref[b, rows] = (mine * slope_ref[b, rows]).astype(BF16)
    pairs, cpart, width = keep_ref.shape
    for b in range(blocks):
        add = dot(delta_ref[b], x_ref[b], 0, 0).reshape(pairs, 2, cpart, width)
        for k in range(2):
            sum_ref[k] = add[:, k] if b == 0 else sum_ref[k] + add[:, k]
        input_ref[b] = dot(delta_ref[b], weight_ref[...], 1, 1).astype(BF16)
    keep_ref[...] = sum_ref[me_ref[0]]
    give_ref[...] = sum_ref[1 - me_ref[0]].astype(BF16)


def turn_kernel(keep_ref, got_ref, after_ref, out_ref):
    del after_ref
    near, far, nz, crows, cpart = out_ref.shape
    whole = (keep_ref[...] + got_ref[...]).T.reshape(nz, far, near, crows, cpart)
    for k in range(near):
        for h in range(far):
            out_ref[k, h] = whole[:, h, k]


def outer_kernel(cols, back_ref, x_ref, second_ref, part_ref, by_ref):
    blocks, length, _ = x_ref.shape
    nd, rows, width = part_ref.shape
    part = length // nd
    for b in range(blocks):
        piece = back_ref[...].astype(F32)[:, b * cols : (b + 1) * cols]
        by_ref[b] = piece.reshape(length, width).astype(BF16)
        add = dot(by_ref[b], x_ref[b], 1, 1).astype(BF16)
        part_ref[:, b * part : (b + 1) * part] = add.reshape(nd, part, width)
    part_ref[:, blocks * part :] = second_ref[...]


def inputs_kernel(weights_ref, by_ref, input_ref, out_ref):
    nd, (blocks, length, _) = weights_ref.shape[0], by_ref.shape
    part = length // nd
    for b in range(blocks):
        mine = weights_ref[:, b * part : (b + 1) * part].reshape(length, length)
        through = dot(mine, by_ref[b], 0, 0)
        out_ref[b] = (through + input_ref[b].astype(F32)).astype(BF16)


def total_kernel(parts_ref, first_ref, second_ref):
    nd, _, width = parts_ref.shape
    blocks, part, _ = first_ref.shape
    for b in range(blocks):
        rows = pl.ds(b * part, part)
        first_ref[b] = sum(parts_ref[d, rows].astype(F32) for d in range(nd))
    for j in range(second_ref.shape[0]):
        rows, lanes = beside(j, second_ref.shape[1], width)
        rows = pl.ds(blocks * part + rows.start, rows.size)
        second_ref[j] = sum(parts_ref[d, rows, lanes].astype(F32) for d in range(nd))


def per_device(inputs, out_grad, first_factor, second_factor, gate_weight):
    nd = lax.axis_size(DP)
    ns = lax.axis_size(SEQ)
    ny = lax.axis_size("y")
    nz = lax.axis_size("z")
    _, rows, width = inputs.shape
    blocks, part, length = first_factor.shape
    cols, part2, size2 = second_factor.shape
    crows, cpart = gate_weight.shape
    x = inputs.reshape(blocks, length, width)
    cot = out_grad.reshape(blocks, length, width)
    piece = shape((ns, blocks * cols, width), BF16)
    wide = 2 * rows * width * width
    cells = pltpu.VMEM((width // LANES, rows, LANES), F32)
    tail = cols * part2 * size2 // width
    both_rows = blocks * part + tail
    by_second = pl.BlockSpec((nd, tail, width), lambda i: (0, blocks * part // tail, 0))

    weights = local(
        weights_kernel, shape((nd, both_rows, width), BF16), [first_factor, second_factor]
    )
    weights = exchange(weights, DP)
    one = local(functools.partial(rows_kernel, cols), piece, [weights, x], flops=wide)
    one, gate_weight = lax.optimization_barrier((one, gate_weight))
    gate_low, gate_high = double(gate_weight, "z")
    col_one = exchange(one, SEQ)
    col_one, gate_low, gate_high = lax.optimization_barrier((col_one, gate_low, gate_high))
    col_two, by_col = local(
        forward_kernel,
        (piece, shape((cols, size2, width), BF16)),
        [weights, col_one],
        [by_second, VMEM],
        flops=wide // 4,
        scratch=[cells, cells],
    )
    two = exchange(col_two, SEQ)

    gate_part = local(
        order_kernel,
        shape((nz, crows, cpart), BF16),
        [lax.axis_index("z")[None], gate_low, gate_high, col_two],
        [SMEM, VMEM, VMEM, ANY],
    )
    gate_part = gather(gate_part, SEQ[1:]).transpose(1, 0, 2, 3).reshape(width, cpart)
    gate_full = gather(gate_part, DP).transpose(1, 0, 2).reshape(width, width)
    mixed_grad, slope = local(
        functools.partial(gate_kernel, cols),
        (piece, shape(x.shape, F32)),
        [x, gate_full, cot],
        flops=wide,
    )
    two, mixed_grad = lax.optimization_barrier((two, mixed_grad))
    col_grad = exchange(mixed_grad, SEQ)

    gate_input, keep, give = local(
        functools.partial(delta_kernel, cols),
        (
            shape(x.shape, BF16),
            shape((ny, cpart, width), F32),
            shape((ny, cpart, width), BF16),
        ),
        [lax.axis_index("xl")[None], two, slope, x, gate_full],
        [SMEM] + [VMEM] * 4,
        flops=2 * wide,
        scratch=[pltpu.VMEM(x.shape, BF16), pltpu.VMEM((2, ny, cpart, width), F32)],
    )
    gsum = keep + swap(give, "xl", 1).astype(F32)
    keep, got = halve(gsum.reshape(2, ny // 2, cpart, width), "y", 2)
    keep, got = halve(keep + got, "y", 1)
    col_grad, keep, got = lax.optimization_barrier((col_grad, keep, got))

    col_back, spart = local(
        backward_kernel,
        (piece, shape((nd, tail, width), BF16)),
        [weights, col_grad, by_col],
        [by_second, VMEM, VMEM],
        flops=wide // 2,
        scratch=[cells, cells],
    )
    back = exchange(col_back, SEQ)
    gsum = local(
        turn_kernel,
        shape((2, 2, nz, crows, cpart), F32),
        [keep, got, col_back],
        [VMEM, VMEM, ANY],
    )
    keep, got = halve(gsum, "co", 1)
    keep, got = halve(keep + got, "xh", 1)
    bit = nz
    while bit > 4:
        bit //= 2
        keep, got = halve((keep + got).reshape(2, bit, crows, cpart), "z", bit)

    parts, by_row = local(
        functools.partial(outer_kernel, cols),
        (shape(weights.shape, BF16), shape(x.shape, BF16)),
        [back, x, spart],
        flops=wide,
    )
    keep, got, parts = lax.optimization_barrier((keep, got, parts))
    parts = exchange(parts, DP)
    while bit > 1:
        bit //= 2
        keep, got = halve((keep + got).reshape(2, bit, crows, cpart), "z", bit)
    grad_gate = (keep + got).reshape(crows, cpart)
    grad_inputs = local(inputs_kernel, shape(x.shape, BF16), [weights, by_row, gate_input], flops=wide)
    grad_first, grad_second = local(
        total_kernel, (shape(first_factor.shape, F32), shape(second_factor.shape, F32)), [parts]
    )
    return (grad_inputs.reshape(inputs.shape), grad_first, grad_second, grad_gate)


def solution(mesh):
    fine = Mesh(mesh.devices.reshape(16, 2, 2, 4, 2), SEQ + DP)
    specs = (P(SEQ, DP, None), P(SEQ, DP, None), P(SEQ, DP))
    return jax.shard_map(
        per_device,
        mesh=fine,
        in_specs=(P(DP, SEQ, None), P(DP, SEQ, None)) + specs,
        out_specs=(P(DP, SEQ, None),) + specs,
        check_vma=False,
    )
```

time: 398 us -> 360 us (0.905)
  the two profiles are of different devices: /device:TPU:1 before, /device:TPU:4 now
where the time goes in v4:
time: 360 us; the launch traced here: 359 us
  waiting for transfers between devices  159 us (44%)
  starting transfers between devices  106 us (29%)
  blocking collectives  50.8 us (14%)
  local copies, waits for them, and re-layouts  22.4 us (6%)
  Pallas kernels  12.3 us (3%)
  other arithmetic  6.96 us (2%)
    ppermute x13, waiting for transfers between devices, swap(): return lax.ppermute(x, axis, [(i, i ^ bits) for i in range(n)])  115 us
    ppermute x13, starting transfers between devices, swap(): return lax.ppermute(x, axis, [(i, i ^ bits) for i in range(n)])  56.5 us
    all_to_all x5, starting transfers between devices, exchange(): return lax.all_to_all(x, axis, split_axis=0, concat_axis=0, tiled=True)  49.4 us
    all_to_all x5, waiting for transfers between devices, exchange(): return lax.all_to_all(x, axis, split_axis=0, concat_axis=0, tiled=True)  43.9 us
    all_gather x4, blocking collectives, gather(): out = lax.all_gather(out, axis, axis=0, tiled=True)  27 us
    all_to_all x1, blocking collectives, exchange(): return lax.all_to_all(x, axis, split_axis=0, concat_axis=0, tiled=True)  23.7 us
    unnamed x52, local copies, waits for them, and re-layouts  22 us
    pallas_call x11, Pallas kernels, local(): pl.pallas_call(body, grid=(1,), out_shape=out_shape, in_specs=in_specs or...  12.3 us
  transfers between devices with their start and end apart: 18, of which 15 were waited for; matrix products, arithmetic and copies ran while one was open for 2% of the time, Pallas kernels for 2%

profile of v4, /device:TPU:4, one launch (start us, length us, event | category | flops | bytes accessed | tf_op | source)
XLA Modules:
  0.0 358.6 jit_solution(5558936890769691290)
XLA Ops:
  2.4 23.7 %all_to_all.30.weights_ref.second_ref = bf16[8,160,512]{2,1,0:T(8,128)(2,1)S(1)} all-to-all(bf16[8,160,512]{2,1,0:T(8,128)(2,1)S(1)} %shard_map.84), channel_id=1, replica_groups=mesh['z'=16,'xh'=2,'co'=2,'y'=4,'xl'=2] {'y','xl'}, dimensions={0} | all-to-all | bytes 2621440 | tf_op jit(solution)/shard_map/all_to_all | solution.py:20
  27.8 18.7 %all-to-all-start.1 = ((bf16[64,16,512]{2,1,0:T(8,128)(2,1)}), bf16[64,16,512]{2,1,0:T(8,128)(2,1)S(1)}, u32[]{:S(2)}, u32[]{:S(2)}) async-start(bf16[64,16,512]{2,1,0:T(8,128)(2,1)} %copy-done.3), calls=%async_computation.1 | async-start | bytes 2097152 | tf_op jit(solution)/shard_map/all_to_all | solution.py:20
  46.6 3.4 collective-permute-start
  50.0 42.2 %collective-permute-done = bf16[1,8,64]{2,1,0:T(8,128)(2,1)S(1)} collective-permute-done((bf16[1,8,64]{2,1,0:T(8,128)(2,1)S(1)}, bf16[1,8,64]{2,1,0:T(8,128)(2,1)S(1)}, u32[]{:S(2)}, u32[]{:S(2)}) %collective-permute-start) | collective-permute-done | bytes 1056 | tf_op jit(solution)/shard_map/ppermute | solution.py:32
  92.1 3.4 collective-permute-start.1
  98.5 7.0 %collective-permute-start.2 = (bf16[4,8,64]{2,1,0:T(8,128)(2,1)S(1)}, bf16[4,8,64]{2,1,0:T(8,128)(2,1)S(1)}, u32[]{:S(2)}, u32[]{:S(2)}) collective-permute-start(bf16[4,8,64]{2,1,0:T(8,128)(2,1)S(1)} %pad_maximum_fusion.1), channel_id=1, source_target_pairs={{0,128},{32,160},{64,192},{96,224},{128,0},{160,32},{192,64},{224,... | collective-permute-start | bytes 12296 | tf_op jit(solution)/shard_map/ppermute | solution.py:32
  108.0 12.6 %collective-permute-start.3 = (bf16[8,8,64]{2,1,0:T(8,128)(2,1)S(1)}, bf16[8,8,64]{2,1,0:T(8,128)(2,1)S(1)}, u32[]{:S(2)}, u32[]{:S(2)}) collective-permute-start(bf16[8,8,64]{2,1,0:T(8,128)(2,1)S(1)} %pad_maximum_fusion.low_ref), channel_id=1, source_target_pairs={{0,256},{32,288},{64,320},{96,352},{128,384},{160,416},{192,448},{... | collective-permute-start | bytes 24584 | tf_op jit(solution)/shard_map/ppermute | solution.py:32
  125.6 16.2 %all-to-all-start.2 = ((bf16[64,16,512]{2,1,0:T(8,128)(2,1)}), bf16[64,16,512]{2,1,0:T(8,128)(2,1)}, u32[]{:S(2)}, u32[]{:S(2)}) async-start(bf16[64,16,512]{2,1,0:T(8,128)(2,1)} %copy-done.4), calls=%async_computation.2 | async-start | bytes 2097152 | tf_op jit(solution)/shard_map/all_to_all | solution.py:20
  143.6 6.8 %all_gather.13 = bf16[4,16,8,64]{3,2,0,1:T(8,128)(2,1)S(1)} all-gather(bf16[2,16,8,64]{3,2,0,1:T(8,128)(2,1)S(1)} %copy.14), channel_id=1, replica_groups=mesh['z'=16,'xh'=2,'co'=2,'y'=4,'xl'=2] {'xh'}, dimensions={0}, use_global_device_ids=true | all-gather | bytes 98304 | tf_op jit(solution)/shard_map/all_gather | solution.py:26
  150.5 5.0 %all_gather.14 = bf16[2,512,64]{1,2,0:T(8,128)(2,1)S(1)} all-gather(bf16[1,512,64]{1,2,0:T(8,128)(2,1)S(1)} %copy.15), channel_id=1, replica_groups=mesh['z'=16,'xh'=2,'co'=2,'y'=4,'xl'=2] {'xl'}, dimensions={0}, use_global_device_ids=true | all-gather | bytes 196608 | tf_op jit(solution)/shard_map/all_gather | solution.py:26
  155.6 13.4 %all_gather.15 = bf16[8,512,64]{1,2,0:T(8,128)(2,1)S(1)} all-gather(bf16[2,512,64]{1,2,0:T(8,128)(2,1)S(1)} %all_gather.14), channel_id=1, replica_groups=mesh['z'=16,'xh'=2,'co'=2,'y'=4,'xl'=2] {'y'}, dimensions={0}, use_global_device_ids=true | all-gather | bytes 655360 | tf_op jit(solution)/shard_map/all_gather | solution.py:26
  173.5 24.2 %all-to-all-done.2.two_ref = bf16[64,16,512]{2,1,0:T(8,128)(2,1)} async-done(((bf16[64,16,512]{2,1,0:T(8,128)(2,1)}), bf16[64,16,512]{2,1,0:T(8,128)(2,1)}, u32[]{:S(2)}, u32[]{:S(2)}) %all-to-all-start.2) | async-done | bytes 1048608 | tf_op jit(solution)/shard_map/all_to_all | solution.py:20
  197.7 5.6 %all-to-all-start.3 = ((bf16[64,16,512]{2,1,0:T(8,128)(2,1)}), bf16[64,16,512]{2,1,0:T(8,128)(2,1)}, u32[]{:S(2)}, u32[]{:S(2)}) async-start(bf16[64,16,512]{2,1,0:T(8,128)(2,1)} %copy-done.16), calls=%async_computation.3 | async-start | bytes 2097152 | tf_op jit(solution)/shard_map/all_to_all | solution.py:20
  211.5 9.6 %collective-permute-done.4 = bf16[4,64,512]{2,1,0:T(8,128)(2,1)S(1)} collective-permute-done((bf16[4,64,512]{2,1,0:T(8,128)(2,1)}, bf16[4,64,512]{2,1,0:T(8,128)(2,1)S(1)}, u32[]{:S(2)}, u32[]{:S(2)}) %collective-permute-start.4) | collective-permute-done | bytes 262176 | tf_op jit(solution)/shard_map/ppermute | solution.py:32
  225.7 8.2 %collective-permute-done.5 = f32[2,64,512]{2,1,0:T(8,128)} collective-permute-done((f32[2,64,512]{2,1,0:T(8,128)}, f32[2,64,512]{2,1,0:T(8,128)}, u32[]{:S(2)}, u32[]{:S(2)}) %collective-permute-start.5) | collective-permute-done | bytes 262176 | tf_op jit(solution)/shard_map/ppermute | solution.py:32
  237.8 4.3 %collective-permute-done.6.got_ref = f32[64,512]{1,0:T(8,128)S(1)} collective-permute-done((f32[64,512]{1,0:T(8,128)S(1)}, f32[64,512]{1,0:T(8,128)S(1)}, u32[]{:S(2)}, u32[]{:S(2)}) %collective-permute-start.6) | collective-permute-done | bytes 131104 | tf_op jit(solution)/shard_map/ppermute | solution.py:32
  242.7 16.6 %all-to-all-done.3.grad_ref = bf16[64,16,512]{2,1,0:T(8,128)(2,1)} async-done(((bf16[64,16,512]{2,1,0:T(8,128)(2,1)}), bf16[64,16,512]{2,1,0:T(8,128)(2,1)}, u32[]{:S(2)}, u32[]{:S(2)}) %all-to-all-start.3) | async-done | bytes 1048608 | tf_op jit(solution)/shard_map/all_to_all | solution.py:20
  263.3 5.4 %all-to-all-start.4 = ((bf16[64,16,512]{2,1,0:T(8,128)(2,1)}), bf16[64,16,512]{2,1,0:T(8,128)(2,1)S(1)}, u32[]{:S(2)}, u32[]{:S(2)}) async-start(bf16[64,16,512]{2,1,0:T(8,128)(2,1)} %copy-done.1), calls=%async_computation.4 | async-start | bytes 2097152 | tf_op jit(solution)/shard_map/all_to_all | solution.py:20
  280.2 6.1 %collective-permute-done.8 = f32[16,8,64]{2,1,0:T(8,128)} collective-permute-done((f32[16,8,64]{2,1,0:T(8,128)}, f32[16,8,64]{2,1,0:T(8,128)}, u32[]{:S(2)}, u32[]{:S(2)}) %collective-permute-start.8) | collective-permute-done | bytes 32800 | tf_op jit(solution)/shard_map/ppermute | solution.py:32
  287.8 11.8 %collective-permute-start.9 = (f32[8,8,64]{2,1,0:T(8,128)S(1)}, f32[8,8,64]{2,1,0:T(8,128)S(1)}, u32[]{:S(2)}, u32[]{:S(2)}) collective-permute-start(f32[8,8,64]{2,1,0:T(8,128)S(1)} %slice_select_fusion.1), channel_id=1, source_target_pairs={{0,256},{32,288},{64,320},{96,352},{128,384},{160,416},{192,448},{... | collective-permute-start | bytes 49160 | tf_op jit(solution)/shard_map/ppermute | solution.py:32
  299.6 28.0 %collective-permute-done.9 = f32[8,8,64]{2,1,0:T(8,128)S(1)} collective-permute-done((f32[8,8,64]{2,1,0:T(8,128)S(1)}, f32[8,8,64]{2,1,0:T(8,128)S(1)}, u32[]{:S(2)}, u32[]{:S(2)}) %collective-permute-start.9) | collective-permute-done | bytes 16416 | tf_op jit(solution)/shard_map/ppermute | solution.py:32
  334.1 3.9 %collective-permute-done.10 = f32[4,8,64]{2,1,0:T(8,128)S(1)} collective-permute-done((f32[4,8,64]{2,1,0:T(8,128)S(1)}, f32[4,8,64]{2,1,0:T(8,128)S(1)}, u32[]{:S(2)}, u32[]{:S(2)}) %collective-permute-start.10) | collective-permute-done | bytes 8224 | tf_op jit(solution)/shard_map/ppermute | solution.py:32
  337.9 3.6 all-to-all-start.5
  343.5 4.5 %collective-permute-done.11 = f32[2,8,64]{2,1,0:T(8,128)S(1)} collective-permute-done((f32[2,8,64]{2,1,0:T(8,128)S(1)}, f32[2,8,64]{2,1,0:T(8,128)S(1)}, u32[]{:S(2)}, u32[]{:S(2)}) %collective-permute-start.11) | collective-permute-done | bytes 4128 | tf_op jit(solution)/shard_map/ppermute | solution.py:32
  (102 shorter events, 73.5 us)
Async XLA Ops:
  2.4 23.7 %copy-start = (bf16[1,1024,512]{2,1,0:T(8,128)(2,1)S(1)}, bf16[1,1024,512]{2,1,0:T(8,128)(2,1)}, u32[]{:S(2)}) copy-start(bf16[1,1024,512]{2,1,0:T(8,128)(2,1)} %param.5) | copy-start | bytes 3145732
  27.8 18.8 %copy-start.25 = (bf16[8,64]{1,0:T(8,128)(2,1)S(1)}, bf16[8,64]{1,0:T(8,128)(2,1)}, u32[]{:S(2)}) copy-start(bf16[8,64]{1,0:T(8,128)(2,1)} %param.9) | copy-start | bytes 3076
  27.8 94.6 %all-to-all-start.1 = ((bf16[64,16,512]{2,1,0:T(8,128)(2,1)}), bf16[64,16,512]{2,1,0:T(8,128)(2,1)S(1)}, u32[]{:S(2)}, u32[]{:S(2)}) async-start(bf16[64,16,512]{2,1,0:T(8,128)(2,1)} %copy-done.3), calls=%async_computation.1 | async-start | bytes 2097152 | tf_op jit(solution)/shard_map/all_to_all | solution.py:20
  46.6 45.6 %collective-permute-start = (bf16[1,8,64]{2,1,0:T(8,128)(2,1)S(1)}, bf16[1,8,64]{2,1,0:T(8,128)(2,1)S(1)}, u32[]{:S(2)}, u32[]{:S(2)}) collective-permute-start(bf16[1,8,64]{2,1,0:T(8,128)(2,1)S(1)} %bitcast.36), channel_id=1, source_target_pairs={{0,32},{32,0},{64,96},{96,64},{128,160},{160,128},{192,224},{224,1... | collective-permute-start | bytes 3080 | tf_op jit(solution)/shard_map/ppermute | solution.py:32
  92.1 6.4 %collective-permute-start.1 = (bf16[2,8,64]{2,1,0:T(8,128)(2,1)S(1)}, bf16[2,8,64]{2,1,0:T(8,128)(2,1)S(1)}, u32[]{:S(2)}, u32[]{:S(2)}) collective-permute-start(bf16[2,8,64]{2,1,0:T(8,128)(2,1)S(1)} %pad_maximum_fusion.2), channel_id=1, source_target_pairs={{0,64},{32,96},{64,0},{96,32},{128,192},{160,224},{192,128},{224,1... | collective-permute-start | bytes 6152 | tf_op jit(solution)/shard_map/ppermute | solution.py:32
  98.5 9.5 %collective-permute-start.2 = (bf16[4,8,64]{2,1,0:T(8,128)(2,1)S(1)}, bf16[4,8,64]{2,1,0:T(8,128)(2,1)S(1)}, u32[]{:S(2)}, u32[]{:S(2)}) collective-permute-start(bf16[4,8,64]{2,1,0:T(8,128)(2,1)S(1)} %pad_maximum_fusion.1), channel_id=1, source_target_pairs={{0,128},{32,160},{64,192},{96,224},{128,0},{160,32},{192,64},{224,... | collective-permute-start | bytes 12296 | tf_op jit(solution)/shard_map/ppermute | solution.py:32
  108.0 14.4 %collective-permute-start.3 = (bf16[8,8,64]{2,1,0:T(8,128)(2,1)S(1)}, bf16[8,8,64]{2,1,0:T(8,128)(2,1)S(1)}, u32[]{:S(2)}, u32[]{:S(2)}) collective-permute-start(bf16[8,8,64]{2,1,0:T(8,128)(2,1)S(1)} %pad_maximum_fusion.low_ref), channel_id=1, source_target_pairs={{0,256},{32,288},{64,320},{96,352},{128,384},{160,416},{192,448},{... | collective-permute-start | bytes 24584 | tf_op jit(solution)/shard_map/ppermute | solution.py:32
  125.6 16.2 %copy-start.5 = (bf16[64,16,512]{2,1,0:T(8,128)(2,1)S(1)}, bf16[64,16,512]{2,1,0:T(8,128)(2,1)}, u32[]{:S(2)}) copy-start(bf16[64,16,512]{2,1,0:T(8,128)(2,1)} %copy-done.4) | copy-start | bytes 3145732
  125.6 72.2 %all-to-all-start.2 = ((bf16[64,16,512]{2,1,0:T(8,128)(2,1)}), bf16[64,16,512]{2,1,0:T(8,128)(2,1)}, u32[]{:S(2)}, u32[]{:S(2)}) async-start(bf16[64,16,512]{2,1,0:T(8,128)(2,1)} %copy-done.4), calls=%async_computation.2 | async-start | bytes 2097152 | tf_op jit(solution)/shard_map/all_to_all | solution.py:20
  171.2 1.4 copy-start.6
  197.7 61.5 %all-to-all-start.3 = ((bf16[64,16,512]{2,1,0:T(8,128)(2,1)}), bf16[64,16,512]{2,1,0:T(8,128)(2,1)}, u32[]{:S(2)}, u32[]{:S(2)}) async-start(bf16[64,16,512]{2,1,0:T(8,128)(2,1)} %copy-done.16), calls=%async_computation.3 | async-start | bytes 2097152 | tf_op jit(solution)/shard_map/all_to_all | solution.py:20
  203.3 1.6 copy-start.7
  208.9 12.1 %collective-permute-start.4 = (bf16[4,64,512]{2,1,0:T(8,128)(2,1)}, bf16[4,64,512]{2,1,0:T(8,128)(2,1)S(1)}, u32[]{:S(2)}, u32[]{:S(2)}) collective-permute-start(bf16[4,64,512]{2,1,0:T(8,128)(2,1)} %get-tuple-element.41), channel_id=1, source_target_pairs={{0,1},{1,0},{2,3},{3,2},{4,5},{5,4},{6,7},{7,6},{8,9},{9,8},{10,11... | collective-permute-start | bytes 786440 | tf_op jit(solution)/shard_map/ppermute | solution.py:32
  221.9 37.3 %copy-start.15 = (bf16[8,128,512]{2,1,0:T(8,128)(2,1)S(1)}, bf16[8,128,512]{2,1,0:T(8,128)(2,1)}, u32[]{:S(2)}) copy-start(bf16[8,128,512]{2,1,0:T(8,128)(2,1)} %copy-done.14) | copy-start | bytes 3145732
  222.7 11.3 %collective-permute-start.5 = (f32[2,64,512]{2,1,0:T(8,128)}, f32[2,64,512]{2,1,0:T(8,128)}, u32[]{:S(2)}, u32[]{:S(2)}) collective-permute-start(f32[2,64,512]{2,1,0:T(8,128)} %slice_select_fusion), channel_id=1, source_target_pairs={{0,4},{2,6},{4,0},{6,2},{1,5},{3,7},{5,1},{7,3},{8,12},{10,14},{12... | collective-permute-start | bytes 786440 | tf_op jit(solution)/shard_map/ppermute | solution.py:32
  235.2 6.9 %collective-permute-start.6 = (f32[64,512]{1,0:T(8,128)S(1)}, f32[64,512]{1,0:T(8,128)S(1)}, u32[]{:S(2)}, u32[]{:S(2)}) collective-permute-start(f32[64,512]{1,0:T(8,128)S(1)} %get-tuple-element.56), channel_id=1, source_target_pairs={{0,2},{2,0},{4,6},{6,4},{1,3},{3,1},{5,7},{7,5},{8,10},{10,8},{12,... | collective-permute-start | bytes 393224 | tf_op jit(solution)/shard_map/ppermute | solution.py:32
  263.3 67.0 %all-to-all-start.4 = ((bf16[64,16,512]{2,1,0:T(8,128)(2,1)}), bf16[64,16,512]{2,1,0:T(8,128)(2,1)S(1)}, u32[]{:S(2)}, u32[]{:S(2)}) async-start(bf16[64,16,512]{2,1,0:T(8,128)(2,1)} %copy-done.1), calls=%async_computation.4 | async-start | bytes 2097152 | tf_op jit(solution)/shard_map/all_to_all | solution.py:20
  272.7 3.4 collective-permute-start.7
  277.8 8.5 %collective-permute-start.8 = (f32[16,8,64]{2,1,0:T(8,128)}, f32[16,8,64]{2,1,0:T(8,128)}, u32[]{:S(2)}, u32[]{:S(2)}) collective-permute-start(f32[16,8,64]{2,1,0:T(8,128)} %select_bitcast_fusion.3), channel_id=1, source_target_pairs={{0,16},{16,0},{1,17},{17,1},{2,18},{18,2},{3,19},{19,3},{4,20},{20... | collective-permute-start | bytes 98312 | tf_op jit(solution)/shard_map/ppermute | solution.py:32
  287.8 39.8 %collective-permute-start.9 = (f32[8,8,64]{2,1,0:T(8,128)S(1)}, f32[8,8,64]{2,1,0:T(8,128)S(1)}, u32[]{:S(2)}, u32[]{:S(2)}) collective-permute-start(f32[8,8,64]{2,1,0:T(8,128)S(1)} %slice_select_fusion.1), channel_id=1, source_target_pairs={{0,256},{32,288},{64,320},{96,352},{128,384},{160,416},{192,448},{... | collective-permute-start | bytes 49160 | tf_op jit(solution)/shard_map/ppermute | solution.py:32
  328.4 9.5 %collective-permute-start.10 = (f32[4,8,64]{2,1,0:T(8,128)S(1)}, f32[4,8,64]{2,1,0:T(8,128)S(1)}, u32[]{:S(2)}, u32[]{:S(2)}) collective-permute-start(f32[4,8,64]{2,1,0:T(8,128)S(1)} %get-tuple-element.58), channel_id=1, source_target_pairs={{0,128},{32,160},{64,192},{96,224},{128,0},{160,32},{192,64},{224,... | collective-permute-start | bytes 24584 | tf_op jit(solution)/shard_map/ppermute | solution.py:32
  337.9 19.9 %all-to-all-start.5 = ((bf16[8,160,512]{2,1,0:T(8,128)(2,1)}), bf16[8,160,512]{2,1,0:T(8,128)(2,1)S(1)}, u32[]{:S(2)}, u32[]{:S(2)}) async-start(bf16[8,160,512]{2,1,0:T(8,128)(2,1)} %copy-done.8), calls=%async_computation.5 | async-start | bytes 2621440 | tf_op jit(solution)/shard_map/all_to_all | solution.py:20
  341.5 6.4 %collective-permute-start.11 = (f32[2,8,64]{2,1,0:T(8,128)S(1)}, f32[2,8,64]{2,1,0:T(8,128)S(1)}, u32[]{:S(2)}, u32[]{:S(2)}) collective-permute-start(f32[2,8,64]{2,1,0:T(8,128)S(1)} %slice_select_fusion.4), channel_id=1, source_target_pairs={{0,64},{32,96},{64,0},{96,32},{128,192},{160,224},{192,128},{224,1... | collective-permute-start | bytes 12296 | tf_op jit(solution)/shard_map/ppermute | solution.py:32
  348.0 6.1 %collective-permute-start.12 = (f32[1,8,64]{2,1,0:T(8,128)S(1)}, f32[1,8,64]{2,1,0:T(8,128)S(1)}, u32[]{:S(2)}, u32[]{:S(2)}) collective-permute-start(f32[1,8,64]{2,1,0:T(8,128)S(1)} %slice_select_fusion.5), channel_id=1, source_target_pairs={{0,32},{32,0},{64,96},{96,64},{128,160},{160,128},{192,224},{224,1... | collective-permute-start | bytes 6152 | tf_op jit(solution)/shard_map/ppermute | solution.py:32
  (20 other events, 19.2 us)

commit v5 on v4

--- a/solution.py
+++ b/solution.py
@@ -32,7 +32,7 @@
     return lax.ppermute(x, axis, [(i, i ^ bits) for i in range(n)])
 
 
-def local(body, out_shape, operands, in_specs=None, flops=0, scratch=()):
+def local(body, out_shape, operands, in_specs=None, out_specs=None, flops=0, scratch=(), alias=None):
     outs = jax.tree.leaves(out_shape)
     moved = sum(a.size * a.dtype.itemsize for a in list(operands) + outs)
     return pl.pallas_call(
@@ -40,7 +40,8 @@
         grid=(1,),
         out_shape=out_shape,
         in_specs=in_specs or [VMEM] * len(operands),
-        out_specs=jax.tree.map(lambda _: VMEM, out_shape),
+        out_specs=out_specs or jax.tree.map(lambda _: VMEM, out_shape),
+        input_output_aliases=alias or {},
         scratch_shapes=list(scratch),
         cost_estimate=pl.CostEstimate(flops=flops, bytes_accessed=moved, transcendentals=0),
         compiler_params=pltpu.CompilerParams(vmem_limit_bytes=28 << 20),
@@ -49,24 +50,6 @@
 
 def shape(dims, dtype):
     return jax.ShapeDtypeStruct(dims, dtype)
-
-
-def order_kernel(me_ref, low_ref, high_ref, after_ref, out_ref):
-    del after_ref
-    n = low_ref.shape[0]
-    for k in range(n):
-        out_ref[me_ref[0] ^ k] = low_ref[k]
-        out_ref[me_ref[0] ^ (n + k)] = high_ref[k]
-
-
-def double(x, axis):
-    low, bit = x[None], 1
-    while True:
-        high = swap(low, axis, bit)
-        bit *= 2
-        if bit == lax.axis_size(axis):
-            return low, high
-        low = jnp.concatenate([low, high])
 
 
 def halve(x, axis, bit):
@@ -161,7 +144,8 @@
         tmp_ref[k, rows] = value[:, k * LANES : (k + 1) * LANES]
 
 
-def forward_kernel(second_ref, one_ref, two_ref, by_ref, tmp_ref, res_ref):
+def forward_kernel(second_ref, one_ref, grad_ref, two_ref, by_ref, tmp_ref, res_ref):
+    del grad_ref
     unfold(one_ref, tmp_ref)
     cols = by_ref.shape[0]
     for j in range(cols):
@@ -205,8 +189,7 @@
     give_ref[...] = sum_ref[1 - me_ref[0]].astype(BF16)
 
 
-def turn_kernel(keep_ref, got_ref, after_ref, out_ref):
-    del after_ref
+def turn_kernel(keep_ref, got_ref, out_ref):
     near, far, nz, crows, cpart = out_ref.shape
     whole = (keep_ref[...] + got_ref[...]).T.reshape(nz, far, near, crows, cpart)
     for k in range(near):
@@ -265,41 +248,51 @@
     both_rows = blocks * part + tail
     by_second = pl.BlockSpec((nd, tail, width), lambda i: (0, blocks * part // tail, 0))
 
+    whole = shape((ns, 2 * blocks * cols, width), BF16)
+    half = [
+        pl.BlockSpec(piece.shape, functools.partial(lambda k, i: (0, k, 0), k)) for k in range(2)
+    ]
+
+    gate_part = exchange(jnp.broadcast_to(gate_weight[None], (nz, crows, cpart)), "z")
     weights = local(
         weights_kernel, shape((nd, both_rows, width), BF16), [first_factor, second_factor]
     )
+    weights, gate_part = lax.optimization_barrier((weights, gate_part))
     weights = exchange(weights, DP)
     one = local(functools.partial(rows_kernel, cols), piece, [weights, x], flops=wide)
-    one, gate_weight = lax.optimization_barrier((one, gate_weight))
-    gate_low, gate_high = double(gate_weight, "z")
+    one, gate_part = lax.optimization_barrier((one, gate_part))
     col_one = exchange(one, SEQ)
-    col_one, gate_low, gate_high = lax.optimization_barrier((col_one, gate_low, gate_high))
-    col_two, by_col = local(
-        forward_kernel,
-        (piece, shape((cols, size2, width), BF16)),
-        [weights, col_one],
-        [by_second, VMEM],
-        flops=wide // 4,
-        scratch=[cells, cells],
-    )
-    two = exchange(col_two, SEQ)
-
-    gate_part = local(
-        order_kernel,
-        shape((nz, crows, cpart), BF16),
-        [lax.axis_index("z")[None], gate_low, gate_high, col_two],
-        [SMEM, VMEM, VMEM, ANY],
-    )
+
     gate_part = gather(gate_part, SEQ[1:]).transpose(1, 0, 2, 3).reshape(width, cpart)
     gate_full = gather(gate_part, DP).transpose(1, 0, 2).reshape(width, width)
     mixed_grad, slope = local(
         functools.partial(gate_kernel, cols),
-        (piece, shape(x.shape, F32)),
+        (whole, shape(x.shape, F32)),
         [x, gate_full, cot],
+        out_specs=(half[0], VMEM),
         flops=wide,
     )
-    two, mixed_grad = lax.optimization_barrier((two, mixed_grad))
-    col_grad = exchange(mixed_grad, SEQ)
+    both, by_col = local(
+        forward_kernel,
+        (whole, shape((cols, size2, width), BF16)),
+        [weights, col_one, mixed_grad],
+        [by_second, VMEM, ANY],
+        (half[1], VMEM),
+        flops=wide // 4,
+        scratch=[cells, cells],
+        alias={2: 0},
+    )
+    both = exchange(both, SEQ)
+    col_back, spart = local(
+        backward_kernel,
+        (piece, shape((nd, tail, width), BF16)),
+        [weights, both, by_col],
+        [by_second, half[0], VMEM],
+        flops=wide // 2,
+        scratch=[cells, cells],
+    )
+    both, col_back = lax.optimization_barrier((both, col_back))
+    back = exchange(col_back, SEQ)
 
     gate_input, keep, give = local(
         functools.partial(delta_kernel, cols),
@@ -308,30 +301,18 @@
             shape((ny, cpart, width), F32),
             shape((ny, cpart, width), BF16),
         ),
-        [lax.axis_index("xl")[None], two, slope, x, gate_full],
-        [SMEM] + [VMEM] * 4,
+        [lax.axis_index("xl")[None], both, slope, x, gate_full],
+        [SMEM, half[1]] + [VMEM] * 3,
         flops=2 * wide,
         scratch=[pltpu.VMEM(x.shape, BF16), pltpu.VMEM((2, ny, cpart, width), F32)],
     )
     gsum = keep + swap(give, "xl", 1).astype(F32)
     keep, got = halve(gsum.reshape(2, ny // 2, cpart, width), "y", 2)
     keep, got = halve(keep + got, "y", 1)
-    col_grad, keep, got = lax.optimization_barrier((col_grad, keep, got))
-
-    col_back, spart = local(
-        backward_kernel,
-        (piece, shape((nd, tail, width), BF16)),
-        [weights, col_grad, by_col],
-        [by_second, VMEM, VMEM],
-        flops=wide // 2,
-        scratch=[cells, cells],
-    )
-    back = exchange(col_back, SEQ)
     gsum = local(
         turn_kernel,
         shape((2, 2, nz, crows, cpart), F32),
-        [keep, got, col_back],
-        [VMEM, VMEM, ANY],
+        [keep, got],
     )
     keep, got = halve(gsum, "co", 1)
     keep, got = halve(keep + got, "xh", 1)
@@ -346,7 +327,7 @@
         [back, x, spart],
         flops=wide,
     )
-    keep, got, parts = lax.optimization_barrier((keep, got, parts))
+    keep, parts = lax.optimization_barrier((keep, parts))
     parts = exchange(parts, DP)
     while bit > 1:
         bit //= 2

time: 360 us -> 337 us (0.936)
  the two profiles are of different devices: /device:TPU:4 before, /device:TPU:1 now
where the time goes in v5:
time: 337 us; the launch traced here: 332 us
  blocking collectives  150 us (45%)
  starting transfers between devices  79.4 us (24%)
  waiting for transfers between devices  64 us (19%)
  local copies, waits for them, and re-layouts  22.1 us (7%)
  Pallas kernels  12.6 us (4%)
    all_to_all x2, blocking collectives, exchange(): return lax.all_to_all(x, axis, split_axis=0, concat_axis=0, tiled=True)  127 us
    ppermute x9, starting transfers between devices, swap(): return lax.ppermute(x, axis, [(i, i ^ bits) for i in range(n)])  42.6 us
    all_to_all x4, starting transfers between devices, exchange(): return lax.all_to_all(x, axis, split_axis=0, concat_axis=0, tiled=True)  36.9 us
    all_to_all x4, waiting for transfers between devices, exchange(): return lax.all_to_all(x, axis, split_axis=0, concat_axis=0, tiled=True)  33.8 us
    ppermute x9, waiting for transfers between devices, swap(): return lax.ppermute(x, axis, [(i, i ^ bits) for i in range(n)])  30.2 us
    all_gather x4, blocking collectives, gather(): out = lax.all_gather(out, axis, axis=0, tiled=True)  23.4 us
    unnamed x45, local copies, waits for them, and re-layouts  21 us
    pallas_call x10, Pallas kernels, local(): pl.pallas_call(body, grid=(1,), out_shape=out_shape, in_specs=in_specs or...  12.6 us
  transfers between devices with their start and end apart: 13, of which 10 were waited for; matrix products, arithmetic and copies ran while one was open for 1% of the time, Pallas kernels for 1%

profile of v5, /device:TPU:1, one launch (start us, length us, event | category | flops | bytes accessed | tf_op | source)
XLA Modules:
  0.0 332.5 jit_solution(203912163093825380)
XLA Ops:
  2.0 15.9 %all-to-all-start = ((bf16[16,2,256]{2,1,0:T(2,128)(2,1)}), bf16[16,2,256]{2,1,0:T(2,128)(2,1)S(1)}, u32[]{:S(2)}, u32[]{:S(2)}) async-start(bf16[16,2,256]{2,1,0:T(2,128)(2,1)} %reshape.67), calls=%async_computation | async-start | bytes 32768 | tf_op jit(solution)/shard_map/all_to_all | solution.py:20
  20.8 8.5 %all-to-all-done = bf16[16,2,256]{2,1,0:T(2,128)(2,1)S(1)} async-done(((bf16[16,2,256]{2,1,0:T(2,128)(2,1)}), bf16[16,2,256]{2,1,0:T(2,128)(2,1)S(1)}, u32[]{:S(2)}, u32[]{:S(2)}) %all-to-all-start) | async-done | bytes 16416 | tf_op jit(solution)/shard_map/all_to_all | solution.py:20
  29.4 21.4 %all_to_all.30.weights_ref.second_ref = bf16[8,160,512]{2,1,0:T(8,128)(2,1)S(1)} all-to-all(bf16[8,160,512]{2,1,0:T(8,128)(2,1)} %copy-done.5), channel_id=1, replica_groups=mesh['z'=16,'xh'=2,'co'=2,'y'=4,'xl'=2] {'y','xl'}, dimensions={0} | all-to-all | bytes 2621440 | tf_op jit(solution)/shard_map/all_to_all | solution.py:20
  52.5 9.2 %all-to-all-start.2 = ((bf16[64,16,512]{2,1,0:T(8,128)(2,1)}), bf16[64,16,512]{2,1,0:T(8,128)(2,1)}, u32[]{:S(2)}, u32[]{:S(2)}) async-start(bf16[64,16,512]{2,1,0:T(8,128)(2,1)} %shard_map.85), calls=%async_computation.2 | async-start | bytes 2097152 | tf_op jit(solution)/shard_map/all_to_all | solution.py:20
  63.8 5.7 %all_gather.13 = bf16[4,16,8,64]{3,2,1,0:T(8,128)(2,1)S(1)} all-gather(bf16[2,16,8,64]{3,2,1,0:T(8,128)(2,1)S(1)} %bitcast.33), channel_id=1, replica_groups=mesh['z'=16,'xh'=2,'co'=2,'y'=4,'xl'=2] {'xh'}, dimensions={0}, use_global_device_ids=true | all-gather | bytes 98304 | tf_op jit(solution)/shard_map/all_gather | solution.py:26
  69.6 4.6 %all_gather.14 = bf16[2,512,64]{1,2,0:T(8,128)(2,1)S(1)} all-gather(bf16[1,512,64]{1,2,0:T(8,128)(2,1)S(1)} %copy.15), channel_id=1, replica_groups=mesh['z'=16,'xh'=2,'co'=2,'y'=4,'xl'=2] {'xl'}, dimensions={0}, use_global_device_ids=true | all-gather | bytes 196608 | tf_op jit(solution)/shard_map/all_gather | solution.py:26
  74.2 11.1 %all_gather.15 = bf16[8,512,64]{1,2,0:T(8,128)(2,1)S(1)} all-gather(bf16[2,512,64]{1,2,0:T(8,128)(2,1)S(1)} %all_gather.14), channel_id=1, replica_groups=mesh['z'=16,'xh'=2,'co'=2,'y'=4,'xl'=2] {'y'}, dimensions={0}, use_global_device_ids=true | all-gather | bytes 655360 | tf_op jit(solution)/shard_map/all_gather | solution.py:26
  90.4 25.3 %all-to-all-done.2.one_ref = bf16[64,16,512]{2,1,0:T(8,128)(2,1)} async-done(((bf16[64,16,512]{2,1,0:T(8,128)(2,1)}), bf16[64,16,512]{2,1,0:T(8,128)(2,1)}, u32[]{:S(2)}, u32[]{:S(2)}) %all-to-all-start.2) | async-done | bytes 1048608 | tf_op jit(solution)/shard_map/all_to_all | solution.py:20
  117.3 2.4 shard_map.87
  119.7 105.5 %all_to_all.31.grad_ref.two_ref = bf16[64,32,512]{2,1,0:T(8,128)(2,1)S(1)} all-to-all(bf16[64,32,512]{2,1,0:T(8,128)(2,1)S(1)} %get-tuple-element.30), channel_id=1, replica_groups=mesh['z'=16,'xh'=2,'co'=2,'y'=4,'xl'=2] {'z','xh','co'}, dimensions={0} | all-to-all | bytes 4194304 | tf_op jit(solution)/shard_map/all_to_all | solution.py:20
  228.1 8.2 %all-to-all-start.4 = ((bf16[64,16,512]{2,1,0:T(8,128)(2,1)}), bf16[64,16,512]{2,1,0:T(8,128)(2,1)}, u32[]{:S(2)}, u32[]{:S(2)}) async-start(bf16[64,16,512]{2,1,0:T(8,128)(2,1)} %copy-done.16), calls=%async_computation.4 | async-start | bytes 2097152 | tf_op jit(solution)/shard_map/all_to_all | solution.py:20
  245.7 9.0 %collective-permute-done = bf16[4,64,512]{2,1,0:T(8,128)(2,1)S(1)} collective-permute-done((bf16[4,64,512]{2,1,0:T(8,128)(2,1)}, bf16[4,64,512]{2,1,0:T(8,128)(2,1)S(1)}, u32[]{:S(2)}, u32[]{:S(2)}) %collective-permute-start) | collective-permute-done | bytes 262176 | tf_op jit(solution)/shard_map/ppermute | solution.py:32
  255.9 2.9 collective-permute-start.1
  258.9 7.2 %collective-permute-done.1 = f32[2,64,512]{2,1,0:T(8,128)} collective-permute-done((f32[2,64,512]{2,1,0:T(8,128)S(1)}, f32[2,64,512]{2,1,0:T(8,128)}, u32[]{:S(2)}, u32[]{:S(2)}) %collective-permute-start.1) | collective-permute-done | bytes 262176 | tf_op jit(solution)/shard_map/ppermute | solution.py:32
  269.1 4.2 %collective-permute-done.2.got_ref = f32[64,512]{1,0:T(8,128)S(1)} collective-permute-done((f32[64,512]{1,0:T(8,128)S(1)}, f32[64,512]{1,0:T(8,128)S(1)}, u32[]{:S(2)}, u32[]{:S(2)}) %collective-permute-start.2) | collective-permute-done | bytes 131104 | tf_op jit(solution)/shard_map/ppermute | solution.py:32
  273.4 4.9 %collective-permute-start.3 = (f32[2,16,8,64]{3,2,1,0:T(8,128)S(1)}, f32[2,16,8,64]{3,2,1,0:T(8,128)S(1)}, u32[]{:S(2)}, u32[]{:S(2)}) collective-permute-start(f32[2,16,8,64]{3,2,1,0:T(8,128)S(1)} %select_bitcast_fusion), channel_id=1, source_target_pairs={{0,8},{8,0},{1,9},{9,1},{2,10},{10,2},{3,11},{11,3},{4,12},{12,4},... | collective-permute-start | bytes 196616 | tf_op jit(solution)/shard_map/ppermute | solution.py:32
  279.3 5.6 %collective-permute-start.4 = (f32[16,8,64]{2,1,0:T(8,128)S(1)}, f32[16,8,64]{2,1,0:T(8,128)S(1)}, u32[]{:S(2)}, u32[]{:S(2)}) collective-permute-start(f32[16,8,64]{2,1,0:T(8,128)S(1)} %select_bitcast_fusion.3), channel_id=1, source_target_pairs={{0,16},{16,0},{1,17},{17,1},{2,18},{18,2},{3,19},{19,3},{4,20},{20... | collective-permute-start | bytes 98312 | tf_op jit(solution)/shard_map/ppermute | solution.py:32
  284.9 2.6 collective-permute-done.4
  287.4 10.5 %collective-permute-start.5 = (f32[8,8,64]{2,1,0:T(8,128)S(1)}, f32[8,8,64]{2,1,0:T(8,128)S(1)}, u32[]{:S(2)}, u32[]{:S(2)}) collective-permute-start(f32[8,8,64]{2,1,0:T(8,128)S(1)} %slice_select_fusion.1), channel_id=1, source_target_pairs={{0,256},{32,288},{64,320},{96,352},{128,384},{160,416},{192,448},{... | collective-permute-start | bytes 49160 | tf_op jit(solution)/shard_map/ppermute | solution.py:32
  298.0 2.9 collective-permute-done.5
  305.0 3.6 %all-to-all-start.5 = ((bf16[8,160,512]{2,1,0:T(8,128)(2,1)}), bf16[8,160,512]{2,1,0:T(8,128)(2,1)S(1)}, u32[]{:S(2)}, u32[]{:S(2)}) async-start(bf16[8,160,512]{2,1,0:T(8,128)(2,1)} %copy-done.10), calls=%async_computation.5 | async-start | bytes 2621440 | tf_op jit(solution)/shard_map/all_to_all | solution.py:20
  308.5 6.8 %collective-permute-start.6 = (f32[4,8,64]{2,1,0:T(8,128)S(1)}, f32[4,8,64]{2,1,0:T(8,128)S(1)}, u32[]{:S(2)}, u32[]{:S(2)}) collective-permute-start(f32[4,8,64]{2,1,0:T(8,128)S(1)} %get-tuple-element.48), channel_id=1, source_target_pairs={{0,128},{32,160},{64,192},{96,224},{128,0},{160,32},{192,64},{224,... | collective-permute-start | bytes 24584 | tf_op jit(solution)/shard_map/ppermute | solution.py:32
  316.9 3.8 %collective-permute-start.7 = (f32[2,8,64]{2,1,0:T(8,128)S(1)}, f32[2,8,64]{2,1,0:T(8,128)S(1)}, u32[]{:S(2)}, u32[]{:S(2)}) collective-permute-start(f32[2,8,64]{2,1,0:T(8,128)S(1)} %slice_select_fusion.4), channel_id=1, source_target_pairs={{0,64},{32,96},{64,0},{96,32},{128,192},{160,224},{192,128},{224,1... | collective-permute-start | bytes 12296 | tf_op jit(solution)/shard_map/ppermute | solution.py:32
  322.5 4.3 %collective-permute-start.8 = (f32[1,8,64]{2,1,0:T(8,128)S(1)}, f32[1,8,64]{2,1,0:T(8,128)S(1)}, u32[]{:S(2)}, u32[]{:S(2)}) collective-permute-start(f32[1,8,64]{2,1,0:T(8,128)S(1)} %slice_select_fusion.5), channel_id=1, source_target_pairs={{0,32},{32,0},{64,96},{96,64},{128,160},{160,128},{192,224},{224,1... | collective-permute-start | bytes 6152 | tf_op jit(solution)/shard_map/ppermute | solution.py:32
  (84 shorter events, 45.4 us)
Async XLA Ops:
  2.0 48.8 %copy-start = (bf16[1,1024,512]{2,1,0:T(8,128)(2,1)S(1)}, bf16[1,1024,512]{2,1,0:T(8,128)(2,1)}, u32[]{:S(2)}) copy-start(bf16[1,1024,512]{2,1,0:T(8,128)(2,1)} %param.5) | copy-start | bytes 3145732
  2.0 27.3 %all-to-all-start = ((bf16[16,2,256]{2,1,0:T(2,128)(2,1)}), bf16[16,2,256]{2,1,0:T(2,128)(2,1)S(1)}, u32[]{:S(2)}, u32[]{:S(2)}) async-start(bf16[16,2,256]{2,1,0:T(2,128)(2,1)} %reshape.67), calls=%async_computation | async-start | bytes 32768 | tf_op jit(solution)/shard_map/all_to_all | solution.py:20
  52.5 63.2 %all-to-all-start.2 = ((bf16[64,16,512]{2,1,0:T(8,128)(2,1)}), bf16[64,16,512]{2,1,0:T(8,128)(2,1)}, u32[]{:S(2)}, u32[]{:S(2)}) async-start(bf16[64,16,512]{2,1,0:T(8,128)(2,1)} %shard_map.85), calls=%async_computation.2 | async-start | bytes 2097152 | tf_op jit(solution)/shard_map/all_to_all | solution.py:20
  85.5 34.2 %copy-start.6 = (bf16[512,512]{1,0:T(8,128)(2,1)}, bf16[512,512]{1,0:T(8,128)(2,1)S(1)}, u32[]{:S(2)}) copy-start(bf16[512,512]{1,0:T(8,128)(2,1)S(1)} %copy.16.weight_ref) | copy-start | bytes 1572868
  85.5 1.4 copy-start.15
  87.7 1.3 copy-start.3
  89.0 1.3 copy-start.8
  115.7 1.6 copy-start.4
  228.1 72.7 %all-to-all-start.4 = ((bf16[64,16,512]{2,1,0:T(8,128)(2,1)}), bf16[64,16,512]{2,1,0:T(8,128)(2,1)}, u32[]{:S(2)}, u32[]{:S(2)}) async-start(bf16[64,16,512]{2,1,0:T(8,128)(2,1)} %copy-done.16), calls=%async_computation.4 | async-start | bytes 2097152 | tf_op jit(solution)/shard_map/all_to_all | solution.py:20
  236.3 1.2 copy-start.1
  238.6 1.6 copy-start.9
  243.8 10.9 %collective-permute-start = (bf16[4,64,512]{2,1,0:T(8,128)(2,1)}, bf16[4,64,512]{2,1,0:T(8,128)(2,1)S(1)}, u32[]{:S(2)}, u32[]{:S(2)}) collective-permute-start(bf16[4,64,512]{2,1,0:T(8,128)(2,1)} %get-tuple-element.40), channel_id=1, source_target_pairs={{0,1},{1,0},{2,3},{3,2},{4,5},{5,4},{6,7},{7,6},{8,9},{9,8},{10,11... | collective-permute-start | bytes 786440 | tf_op jit(solution)/shard_map/ppermute | solution.py:32
  255.9 44.9 %copy-start.2 = (bf16[1,1024,512]{2,1,0:T(8,128)(2,1)S(1)}, bf16[1,1024,512]{2,1,0:T(8,128)(2,1)}, u32[]{:S(2)}) copy-start(bf16[1,1024,512]{2,1,0:T(8,128)(2,1)} %param.5) | copy-start | bytes 3145732
  255.9 44.9 %copy-start.19 = (bf16[8,32,512]{2,1,0:T(8,128)(2,1)S(1)}, bf16[8,32,512]{2,1,0:T(8,128)(2,1)}, u32[]{:S(2)}) copy-start(bf16[8,32,512]{2,1,0:T(8,128)(2,1)} %copy-done.18) | copy-start | bytes 786436
  255.9 10.2 %collective-permute-start.1 = (f32[2,64,512]{2,1,0:T(8,128)S(1)}, f32[2,64,512]{2,1,0:T(8,128)}, u32[]{:S(2)}, u32[]{:S(2)}) collective-permute-start(f32[2,64,512]{2,1,0:T(8,128)S(1)} %slice_select_fusion), channel_id=1, source_target_pairs={{0,4},{2,6},{4,0},{6,2},{1,5},{3,7},{5,1},{7,3},{8,12},{10,14},{12... | collective-permute-start | bytes 786440 | tf_op jit(solution)/shard_map/ppermute | solution.py:32
  267.1 6.1 %collective-permute-start.2 = (f32[64,512]{1,0:T(8,128)S(1)}, f32[64,512]{1,0:T(8,128)S(1)}, u32[]{:S(2)}, u32[]{:S(2)}) collective-permute-start(f32[64,512]{1,0:T(8,128)S(1)} %get-tuple-element.46), channel_id=1, source_target_pairs={{0,2},{2,0},{4,6},{6,4},{1,3},{3,1},{5,7},{7,5},{8,10},{10,8},{12,... | collective-permute-start | bytes 393224 | tf_op jit(solution)/shard_map/ppermute | solution.py:32
  273.4 5.8 %collective-permute-start.3 = (f32[2,16,8,64]{3,2,1,0:T(8,128)S(1)}, f32[2,16,8,64]{3,2,1,0:T(8,128)S(1)}, u32[]{:S(2)}, u32[]{:S(2)}) collective-permute-start(f32[2,16,8,64]{3,2,1,0:T(8,128)S(1)} %select_bitcast_fusion), channel_id=1, source_target_pairs={{0,8},{8,0},{1,9},{9,1},{2,10},{10,2},{3,11},{11,3},{4,12},{12,4},... | collective-permute-start | bytes 196616 | tf_op jit(solution)/shard_map/ppermute | solution.py:32
  279.3 8.1 %collective-permute-start.4 = (f32[16,8,64]{2,1,0:T(8,128)S(1)}, f32[16,8,64]{2,1,0:T(8,128)S(1)}, u32[]{:S(2)}, u32[]{:S(2)}) collective-permute-start(f32[16,8,64]{2,1,0:T(8,128)S(1)} %select_bitcast_fusion.3), channel_id=1, source_target_pairs={{0,16},{16,0},{1,17},{17,1},{2,18},{18,2},{3,19},{19,3},{4,20},{20... | collective-permute-start | bytes 98312 | tf_op jit(solution)/shard_map/ppermute | solution.py:32
  287.4 13.4 %collective-permute-start.5 = (f32[8,8,64]{2,1,0:T(8,128)S(1)}, f32[8,8,64]{2,1,0:T(8,128)S(1)}, u32[]{:S(2)}, u32[]{:S(2)}) collective-permute-start(f32[8,8,64]{2,1,0:T(8,128)S(1)} %slice_select_fusion.1), channel_id=1, source_target_pairs={{0,256},{32,288},{64,320},{96,352},{128,384},{160,416},{192,448},{... | collective-permute-start | bytes 49160 | tf_op jit(solution)/shard_map/ppermute | solution.py:32
  305.0 26.7 %all-to-all-start.5 = ((bf16[8,160,512]{2,1,0:T(8,128)(2,1)}), bf16[8,160,512]{2,1,0:T(8,128)(2,1)S(1)}, u32[]{:S(2)}, u32[]{:S(2)}) async-start(bf16[8,160,512]{2,1,0:T(8,128)(2,1)} %copy-done.10), calls=%async_computation.5 | async-start | bytes 2621440 | tf_op jit(solution)/shard_map/all_to_all | solution.py:20
  308.5 8.4 %collective-permute-start.6 = (f32[4,8,64]{2,1,0:T(8,128)S(1)}, f32[4,8,64]{2,1,0:T(8,128)S(1)}, u32[]{:S(2)}, u32[]{:S(2)}) collective-permute-start(f32[4,8,64]{2,1,0:T(8,128)S(1)} %get-tuple-element.48), channel_id=1, source_target_pairs={{0,128},{32,160},{64,192},{96,224},{128,0},{160,32},{192,64},{224,... | collective-permute-start | bytes 24584 | tf_op jit(solution)/shard_map/ppermute | solution.py:32
  316.9 5.6 %collective-permute-start.7 = (f32[2,8,64]{2,1,0:T(8,128)S(1)}, f32[2,8,64]{2,1,0:T(8,128)S(1)}, u32[]{:S(2)}, u32[]{:S(2)}) collective-permute-start(f32[2,8,64]{2,1,0:T(8,128)S(1)} %slice_select_fusion.4), channel_id=1, source_target_pairs={{0,64},{32,96},{64,0},{96,32},{128,192},{160,224},{192,128},{224,1... | collective-permute-start | bytes 12296 | tf_op jit(solution)/shard_map/ppermute | solution.py:32
  322.5 8.5 %collective-permute-start.8 = (f32[1,8,64]{2,1,0:T(8,128)S(1)}, f32[1,8,64]{2,1,0:T(8,128)S(1)}, u32[]{:S(2)}, u32[]{:S(2)}) collective-permute-start(f32[1,8,64]{2,1,0:T(8,128)S(1)} %slice_select_fusion.5), channel_id=1, source_target_pairs={{0,32},{32,0},{64,96},{96,64},{128,160},{160,128},{192,224},{224,1... | collective-permute-start | bytes 6152 | tf_op jit(solution)/shard_map/ppermute | solution.py:32
  326.8 1.2 copy-start.12
  (11 other events, 10.6 us)

commit v6 on v4

--- a/solution.py
+++ b/solution.py
@@ -32,7 +32,7 @@
     return lax.ppermute(x, axis, [(i, i ^ bits) for i in range(n)])
 
 
-def local(body, out_shape, operands, in_specs=None, flops=0, scratch=()):
+def local(body, out_shape, operands, in_specs=None, out_specs=None, flops=0, scratch=(), alias=None):
     outs = jax.tree.leaves(out_shape)
     moved = sum(a.size * a.dtype.itemsize for a in list(operands) + outs)
     return pl.pallas_call(
@@ -40,7 +40,8 @@
         grid=(1,),
         out_shape=out_shape,
         in_specs=in_specs or [VMEM] * len(operands),
-        out_specs=jax.tree.map(lambda _: VMEM, out_shape),
+        out_specs=out_specs or jax.tree.map(lambda _: VMEM, out_shape),
+        input_output_aliases=alias or {},
         scratch_shapes=list(scratch),
         cost_estimate=pl.CostEstimate(flops=flops, bytes_accessed=moved, transcendentals=0),
         compiler_params=pltpu.CompilerParams(vmem_limit_bytes=28 << 20),
@@ -49,24 +50,6 @@
 
 def shape(dims, dtype):
     return jax.ShapeDtypeStruct(dims, dtype)
-
-
-def order_kernel(me_ref, low_ref, high_ref, after_ref, out_ref):
-    del after_ref
-    n = low_ref.shape[0]
-    for k in range(n):
-        out_ref[me_ref[0] ^ k] = low_ref[k]
-        out_ref[me_ref[0] ^ (n + k)] = high_ref[k]
-
-
-def double(x, axis):
-    low, bit = x[None], 1
-    while True:
-        high = swap(low, axis, bit)
-        bit *= 2
-        if bit == lax.axis_size(axis):
-            return low, high
-        low = jnp.concatenate([low, high])
 
 
 def halve(x, axis, bit):
@@ -84,8 +67,25 @@
 LANES = 128
 
 
-def pack(tops, cols):
-    return jnp.concatenate([t.reshape(-1, cols, t.shape[-1]) for t in tops], axis=1)
+def lanes_of(x, k):
+    return x[:, k * LANES : (k + 1) * LANES]
+
+
+def pack(tops, cols, out_ref, start):
+    tall = len(tops) * cols
+    for k in range(tops[0].shape[1] // LANES):
+        rows = [lanes_of(t, k).reshape(-1, cols, LANES) for t in tops]
+        rows = jnp.concatenate(rows, axis=1).astype(BF16)
+        out_ref[start : start + rows.shape[0], k * tall : (k + 1) * tall] = rows
+
+
+def unpack(piece, cols, blocks, b):
+    tall = blocks * cols
+    rows = [
+        piece[:, k * tall + b * cols : k * tall + (b + 1) * cols].reshape(-1, LANES)
+        for k in range(piece.shape[1] // tall)
+    ]
+    return jnp.concatenate(rows, axis=1)
 
 
 def beside(j, part, width):
@@ -109,16 +109,19 @@
     return second_ref[:, rows, lanes].reshape(LANES, LANES)
 
 
-def rows_kernel(cols, weights_ref, x_ref, out_ref):
-    nd, (blocks, length, _) = weights_ref.shape[0], x_ref.shape
+def rows_kernel(cols, weights_ref, x_ref, gate_ref, out_ref):
+    nd, (blocks, length, width) = weights_ref.shape[0], x_ref.shape
     part = length // nd
     per = STEP * cols // part
+    body = width // LANES * blocks * cols
+    rider = jnp.concatenate([gate_ref[...].astype(F32)] * 2, axis=1).astype(BF16)
     for c in range(out_ref.shape[0] // STEP):
         tops = []
         for b in range(blocks):
             mine = weights_ref[c * per : (c + 1) * per, b * part : (b + 1) * part]
             tops.append(dot(mine.reshape(per * part, length), x_ref[b]))
-        out_ref[c * STEP : (c + 1) * STEP] = pack(tops, cols).astype(BF16)
+        pack(tops, cols, out_ref, c * STEP)
+        out_ref[c * STEP : (c + 1) * STEP, body:] = jnp.broadcast_to(rider[None], (STEP,) + rider.shape)
 
 
 def gate_kernel(cols, x_ref, weight_ref, cot_ref, out_ref, slope_ref):
@@ -131,23 +134,23 @@
             grad = cot_ref[b, rows].astype(F32) * gate
             slope_ref[b, rows] = grad * (1.0 - gate)
             tops.append(grad)
-        out_ref[c * STEP : (c + 1) * STEP] = pack(tops, cols).astype(BF16)
+        pack(tops, cols, out_ref, c * STEP)
 
 
 def unfold(src_ref, tmp_ref):
-    tall = src_ref.shape[1]
+    tall = tmp_ref.shape[1] // src_ref.shape[0]
     for c in range(0, src_ref.shape[0], STEP):
-        piece = src_ref[c : c + STEP].astype(F32).reshape(STEP * tall, src_ref.shape[2])
         for k in range(tmp_ref.shape[0]):
-            tmp_ref[k, pl.ds(c * tall, STEP * tall)] = piece[:, k * LANES : (k + 1) * LANES]
+            piece = src_ref[c : c + STEP, k * tall : (k + 1) * tall].astype(F32)
+            tmp_ref[k, pl.ds(c * tall, STEP * tall)] = piece.reshape(STEP * tall, LANES)
 
 
 def fold(tmp_ref, dst_ref):
-    tall = dst_ref.shape[1]
+    tall = tmp_ref.shape[1] // dst_ref.shape[0]
     for c in range(0, dst_ref.shape[0], STEP):
-        rows = pl.ds(c * tall, STEP * tall)
-        piece = jnp.concatenate([tmp_ref[k, rows] for k in range(tmp_ref.shape[0])], axis=1)
-        dst_ref[c : c + STEP] = piece.reshape(STEP, tall, dst_ref.shape[2]).astype(BF16)
+        for k in range(tmp_ref.shape[0]):
+            piece = tmp_ref[k, pl.ds(c * tall, STEP * tall)].reshape(STEP, tall, LANES)
+            dst_ref[c : c + STEP, k * tall : (k + 1) * tall] = piece.astype(BF16)
 
 
 def column(tmp_ref, j, cols):
@@ -158,7 +161,7 @@
 def set_column(tmp_ref, j, cols, value):
     rows = pl.ds(j, tmp_ref.shape[1] // cols, stride=cols)
     for k in range(tmp_ref.shape[0]):
-        tmp_ref[k, rows] = value[:, k * LANES : (k + 1) * LANES]
+        tmp_ref[k, rows] = lanes_of(value, k)
 
 
 def forward_kernel(second_ref, one_ref, two_ref, by_ref, tmp_ref, res_ref):
@@ -171,7 +174,7 @@
     fold(res_ref, two_ref)
 
 
-def backward_kernel(second_ref, grad_ref, by_ref, back_ref, part_ref, tmp_ref, res_ref):
+def backward_kernel(second_ref, grad_ref, by_ref, keep_ref, got_ref, back_ref, part_ref, tmp_ref, res_ref):
     unfold(grad_ref, tmp_ref)
     cols = by_ref.shape[0]
     nd, _, width = part_ref.shape
@@ -182,6 +185,12 @@
         part = dot(mine, by_ref[j], 1, 1).reshape(nd, LANES // nd, LANES)
         part_ref[:, rows, lanes] = part.astype(BF16)
     fold(res_ref, back_ref)
+    body = grad_ref.shape[1]
+    total = (keep_ref[...] + got_ref[...]).T
+    coarse = total.astype(BF16).astype(F32)
+    rider = jnp.concatenate([coarse, total - coarse], axis=1)
+    rider = rider.reshape(back_ref.shape[0], back_ref.shape[1] - body, LANES)
+    back_ref[:, body:] = rider.astype(BF16)
 
 
 def delta_kernel(
@@ -193,7 +202,7 @@
         two = two_ref[c * STEP : (c + 1) * STEP].astype(F32)
         for b in range(blocks):
             rows = pl.ds(c * n, n)
-            mine = two[:, b * cols : (b + 1) * cols].reshape(n, two.shape[2])
+            mine = unpack(two, cols, blocks, b)
             delta_ref[b, rows] = (mine * slope_ref[b, rows]).astype(BF16)
     pairs, cpart, width = keep_ref.shape
     for b in range(blocks):
@@ -205,25 +214,22 @@
     give_ref[...] = sum_ref[1 - me_ref[0]].astype(BF16)
 
 
-def turn_kernel(keep_ref, got_ref, after_ref, out_ref):
-    del after_ref
-    near, far, nz, crows, cpart = out_ref.shape
-    whole = (keep_ref[...] + got_ref[...]).T.reshape(nz, far, near, crows, cpart)
-    for k in range(near):
-        for h in range(far):
-            out_ref[k, h] = whole[:, h, k]
-
-
 def outer_kernel(cols, back_ref, x_ref, second_ref, part_ref, by_ref):
     blocks, length, _ = x_ref.shape
     nd, rows, width = part_ref.shape
     part = length // nd
+    piece = back_ref[...].astype(F32)
     for b in range(blocks):
-        piece = back_ref[...].astype(F32)[:, b * cols : (b + 1) * cols]
-        by_ref[b] = piece.reshape(length, width).astype(BF16)
+        by_ref[b] = unpack(piece, cols, blocks, b).astype(BF16)
         add = dot(by_ref[b], x_ref[b], 1, 1).astype(BF16)
         part_ref[:, b * part : (b + 1) * part] = add.reshape(nd, part, width)
     part_ref[:, blocks * part :] = second_ref[...]
+
+
+def gate_sum_kernel(riders_ref, out_ref):
+    total = jnp.sum(riders_ref[...].astype(F32), axis=0)
+    half = out_ref.shape[1]
+    out_ref[...] = total[:, :half] + total[:, half:]
 
 
 def inputs_kernel(weights_ref, by_ref, input_ref, out_ref):
@@ -251,46 +257,43 @@
     nd = lax.axis_size(DP)
     ns = lax.axis_size(SEQ)
     ny = lax.axis_size("y")
-    nz = lax.axis_size("z")
     _, rows, width = inputs.shape
     blocks, part, length = first_factor.shape
     cols, part2, size2 = second_factor.shape
     crows, cpart = gate_weight.shape
     x = inputs.reshape(blocks, length, width)
     cot = out_grad.reshape(blocks, length, width)
-    piece = shape((ns, blocks * cols, width), BF16)
+    body = width // LANES * blocks * cols
+    piece = shape((ns, body, LANES), BF16)
+    longer = shape((ns, body + crows, LANES), BF16)
     wide = 2 * rows * width * width
     cells = pltpu.VMEM((width // LANES, rows, LANES), F32)
     tail = cols * part2 * size2 // width
     both_rows = blocks * part + tail
     by_second = pl.BlockSpec((nd, tail, width), lambda i: (0, blocks * part // tail, 0))
+    by_body = pl.BlockSpec(piece.shape, lambda i: (0, 0, 0))
+    by_rider = pl.BlockSpec((ns, crows, LANES), lambda i: (0, body // crows, 0))
 
     weights = local(
         weights_kernel, shape((nd, both_rows, width), BF16), [first_factor, second_factor]
     )
     weights = exchange(weights, DP)
-    one = local(functools.partial(rows_kernel, cols), piece, [weights, x], flops=wide)
-    one, gate_weight = lax.optimization_barrier((one, gate_weight))
-    gate_low, gate_high = double(gate_weight, "z")
+    one = local(
+        functools.partial(rows_kernel, cols), longer, [weights, x, gate_weight], flops=wide
+    )
     col_one = exchange(one, SEQ)
-    col_one, gate_low, gate_high = lax.optimization_barrier((col_one, gate_low, gate_high))
     col_two, by_col = local(
         forward_kernel,
         (piece, shape((cols, size2, width), BF16)),
         [weights, col_one],
-        [by_second, VMEM],
+        [by_second, by_body],
         flops=wide // 4,
         scratch=[cells, cells],
     )
+    col_one, col_two = lax.optimization_barrier((col_one, col_two))
     two = exchange(col_two, SEQ)
 
-    gate_part = local(
-        order_kernel,
-        shape((nz, crows, cpart), BF16),
-        [lax.axis_index("z")[None], gate_low, gate_high, col_two],
-        [SMEM, VMEM, VMEM, ANY],
-    )
-    gate_part = gather(gate_part, SEQ[1:]).transpose(1, 0, 2, 3).reshape(width, cpart)
+    gate_part = col_one[:, body:, :cpart].reshape(width, cpart)
     gate_full = gather(gate_part, DP).transpose(1, 0, 2).reshape(width, width)
     mixed_grad, slope = local(
         functools.partial(gate_kernel, cols),
@@ -320,38 +323,24 @@
 
     col_back, spart = local(
         backward_kernel,
-        (piece, shape((nd, tail, width), BF16)),
-        [weights, col_grad, by_col],
-        [by_second, VMEM, VMEM],
+        (longer, shape((nd, tail, width), BF16)),
+        [weights, col_grad, by_col, keep, got],
+        [by_second] + [VMEM] * 4,
         flops=wide // 2,
         scratch=[cells, cells],
     )
     back = exchange(col_back, SEQ)
-    gsum = local(
-        turn_kernel,
-        shape((2, 2, nz, crows, cpart), F32),
-        [keep, got, col_back],
-        [VMEM, VMEM, ANY],
-    )
-    keep, got = halve(gsum, "co", 1)
-    keep, got = halve(keep + got, "xh", 1)
-    bit = nz
-    while bit > 4:
-        bit //= 2
-        keep, got = halve((keep + got).reshape(2, bit, crows, cpart), "z", bit)
 
     parts, by_row = local(
         functools.partial(outer_kernel, cols),
         (shape(weights.shape, BF16), shape(x.shape, BF16)),
         [back, x, spart],
+        [by_body, VMEM, VMEM],
         flops=wide,
     )
-    keep, got, parts = lax.optimization_barrier((keep, got, parts))
+    back, parts = lax.optimization_barrier((back, parts))
     parts = exchange(parts, DP)
-    while bit > 1:
-        bit //= 2
-        keep, got = halve((keep + got).reshape(2, bit, crows, cpart), "z", bit)
-    grad_gate = (keep + got).reshape(crows, cpart)
+    grad_gate = local(gate_sum_kernel, shape(gate_weight.shape, F32), [back], [by_rider])
     grad_inputs = local(inputs_kernel, shape(x.shape, BF16), [weights, by_row, gate_input], flops=wide)
     grad_first, grad_second = local(
         total_kernel, (shape(first_factor.shape, F32), shape(second_factor.shape, F32)), [parts]

time: 360 us -> 332 us (0.922)
  the two profiles are of different devices: /device:TPU:4 before, /device:TPU:1 now
where the time goes in v6:
time: 332 us; the launch traced here: 328 us
  blocking collectives  185 us (56%)
  waiting for transfers between devices  83.4 us (25%)
  starting transfers between devices  26.4 us (8%)
  local copies, waits for them, and re-layouts  16.5 us (5%)
  Pallas kernels  14 us (4%)
    all_to_all x3, blocking collectives, exchange(): return lax.all_to_all(x, axis, split_axis=0, concat_axis=0, tiled=True)  169 us
    all_to_all x3, waiting for transfers between devices, exchange(): return lax.all_to_all(x, axis, split_axis=0, concat_axis=0, tiled=True)  62.5 us
    ppermute x3, waiting for transfers between devices, swap(): return lax.ppermute(x, axis, [(i, i ^ bits) for i in range(n)])  20.9 us
    all_to_all x3, starting transfers between devices, exchange(): return lax.all_to_all(x, axis, split_axis=0, concat_axis=0, tiled=True)  19.6 us
    all_gather x2, blocking collectives, gather(): out = lax.all_gather(out, axis, axis=0, tiled=True)  15.3 us
    unnamed x38, local copies, waits for them, and re-layouts  14.7 us
    pallas_call x10, Pallas kernels, local(): pl.pallas_call(body, grid=(1,), out_shape=out_shape, in_specs=in_specs or...  14 us
    ppermute x3, starting transfers between devices, swap(): return lax.ppermute(x, axis, [(i, i ^ bits) for i in range(n)])  6.74 us
  transfers between devices with their start and end apart: 6, of which 6 were waited for; matrix products, arithmetic and copies ran while one was open for 1% of the time, Pallas kernels for 2%

profile of v6, /device:TPU:1, one launch (start us, length us, event | category | flops | bytes accessed | tf_op | source)
XLA Modules:
  0.0 328.0 jit_solution(1944433183663991164)
XLA Ops:
  2.4 20.7 %all_to_all.30.weights_ref.second_ref = bf16[8,160,512]{2,1,0:T(8,128)(2,1)S(1)} all-to-all(bf16[8,160,512]{2,1,0:T(8,128)(2,1)S(1)} %shard_map.84), channel_id=1, replica_groups=mesh['z'=16,'xh'=2,'co'=2,'y'=4,'xl'=2] {'y','xl'}, dimensions={0} | all-to-all | bytes 2621440 | tf_op jit(solution)/shard_map/all_to_all | solution.py:20
  23.8 82.0 %all_to_all.31.one_ref = bf16[64,72,128]{2,1,0:T(8,128)(2,1)S(1)} all-to-all(bf16[64,72,128]{2,1,0:T(8,128)(2,1)S(1)} %shard_map.85), channel_id=1, replica_groups=mesh['z'=16,'xh'=2,'co'=2,'y'=4,'xl'=2] {'z','xh','co'}, dimensions={0} | all-to-all | bytes 2359296 | tf_op jit(solution)/shard_map/all_to_all | solution.py:20
  105.8 1.3 shard_map.86
  109.1 7.7 %all-to-all-start.2 = ((bf16[64,64,128]{2,1,0:T(8,128)(2,1)}), bf16[64,64,128]{2,1,0:T(8,128)(2,1)}, u32[]{:S(2)}, u32[]{:S(2)}) async-start(bf16[64,64,128]{2,1,0:T(8,128)(2,1)} %copy-done.12), calls=%async_computation.2 | async-start | bytes 2097152 | tf_op jit(solution)/shard_map/all_to_all | solution.py:20
  118.5 4.2 %all_gather.6 = bf16[2,512,64]{1,2,0:T(8,128)(2,1)S(1)} all-gather(bf16[1,512,64]{1,2,0:T(8,128)(2,1)S(1)} %copy.13), channel_id=1, replica_groups=mesh['z'=16,'xh'=2,'co'=2,'y'=4,'xl'=2] {'xl'}, dimensions={0}, use_global_device_ids=true | all-gather | bytes 196608 | tf_op jit(solution)/shard_map/all_gather | solution.py:26
  122.7 11.1 %all_gather.7 = bf16[8,512,64]{1,2,0:T(8,128)(2,1)S(1)} all-gather(bf16[2,512,64]{1,2,0:T(8,128)(2,1)S(1)} %all_gather.6), channel_id=1, replica_groups=mesh['z'=16,'xh'=2,'co'=2,'y'=4,'xl'=2] {'y'}, dimensions={0}, use_global_device_ids=true | all-gather | bytes 655360 | tf_op jit(solution)/shard_map/all_gather | solution.py:26
  136.0 1.3 copy-done.1
  138.4 32.4 %all-to-all-done.2.two_ref = bf16[64,64,128]{2,1,0:T(8,128)(2,1)} async-done(((bf16[64,64,128]{2,1,0:T(8,128)(2,1)}), bf16[64,64,128]{2,1,0:T(8,128)(2,1)}, u32[]{:S(2)}, u32[]{:S(2)}) %all-to-all-start.2) | async-done | bytes 1048608 | tf_op jit(solution)/shard_map/all_to_all | solution.py:20
  170.8 7.6 %all-to-all-start.3 = ((bf16[64,64,128]{2,1,0:T(8,128)(2,1)}), bf16[64,64,128]{2,1,0:T(8,128)(2,1)}, u32[]{:S(2)}, u32[]{:S(2)}) async-start(bf16[64,64,128]{2,1,0:T(8,128)(2,1)} %copy-done.11), calls=%async_computation.3 | async-start | bytes 2097152 | tf_op jit(solution)/shard_map/all_to_all | solution.py:20
  178.4 1.6 copy-done.2
  180.0 3.1 shard_map.88
  184.1 1.9 collective-permute-start
  186.1 9.4 %collective-permute-done = bf16[4,64,512]{2,1,0:T(8,128)(2,1)S(1)} collective-permute-done((bf16[4,64,512]{2,1,0:T(8,128)(2,1)}, bf16[4,64,512]{2,1,0:T(8,128)(2,1)S(1)}, u32[]{:S(2)}, u32[]{:S(2)}) %collective-permute-start) | collective-permute-done | bytes 262176 | tf_op jit(solution)/shard_map/ppermute | solution.py:32
  197.1 2.9 collective-permute-start.1
  200.0 7.3 %collective-permute-done.1 = f32[2,64,512]{2,1,0:T(8,128)} collective-permute-done((f32[2,64,512]{2,1,0:T(8,128)}, f32[2,64,512]{2,1,0:T(8,128)}, u32[]{:S(2)}, u32[]{:S(2)}) %collective-permute-start.1) | collective-permute-done | bytes 262176 | tf_op jit(solution)/shard_map/ppermute | solution.py:32
  208.6 1.9 collective-permute-start.2
  210.5 4.2 %collective-permute-done.2.got_ref = f32[64,512]{1,0:T(8,128)S(1)} collective-permute-done((f32[64,512]{1,0:T(8,128)S(1)}, f32[64,512]{1,0:T(8,128)S(1)}, u32[]{:S(2)}, u32[]{:S(2)}) %collective-permute-start.2) | collective-permute-done | bytes 131104 | tf_op jit(solution)/shard_map/ppermute | solution.py:32
  215.3 17.0 %all-to-all-done.3.grad_ref = bf16[64,64,128]{2,1,0:T(8,128)(2,1)} async-done(((bf16[64,64,128]{2,1,0:T(8,128)(2,1)}), bf16[64,64,128]{2,1,0:T(8,128)(2,1)}, u32[]{:S(2)}, u32[]{:S(2)}) %all-to-all-start.3) | async-done | bytes 1048608 | tf_op jit(solution)/shard_map/all_to_all | solution.py:20
  233.2 2.4 shard_map.89
  235.7 66.7 %all_to_all.32.back_ref.riders_ref = bf16[64,72,128]{2,1,0:T(8,128)(2,1)S(1)} all-to-all(bf16[64,72,128]{2,1,0:T(8,128)(2,1)S(1)} %get-tuple-element.39), channel_id=1, replica_groups=mesh['z'=16,'xh'=2,'co'=2,'y'=4,'xl'=2] {'z','xh','co'}, dimensions={0} | all-to-all | bytes 2359296 | tf_op jit(solution)/shard_map/all_to_all | solution.py:20
  305.4 4.4 %all-to-all-start.5 = ((bf16[8,160,512]{2,1,0:T(8,128)(2,1)}), bf16[8,160,512]{2,1,0:T(8,128)(2,1)}, u32[]{:S(2)}, u32[]{:S(2)}) async-start(bf16[8,160,512]{2,1,0:T(8,128)(2,1)} %copy-done.3), calls=%async_computation.5 | async-start | bytes 2621440 | tf_op jit(solution)/shard_map/all_to_all | solution.py:20
  311.0 1.7 shard_map.91
  312.7 13.1 %all-to-all-done.5.parts_ref = bf16[8,160,512]{2,1,0:T(8,128)(2,1)} async-done(((bf16[8,160,512]{2,1,0:T(8,128)(2,1)}), bf16[8,160,512]{2,1,0:T(8,128)(2,1)}, u32[]{:S(2)}, u32[]{:S(2)}) %all-to-all-start.5) | async-done | bytes 1310752 | tf_op jit(solution)/shard_map/all_to_all | solution.py:20
  325.8 2.2 shard_map.92
  (48 shorter events, 18.9 us)
Async XLA Ops:
  0.6 0.9 copy-start.13
  1.5 0.8 copy-start.16
  2.4 20.7 %copy-start = (bf16[1,1024,512]{2,1,0:T(8,128)(2,1)S(1)}, bf16[1,1024,512]{2,1,0:T(8,128)(2,1)}, u32[]{:S(2)}) copy-start(bf16[1,1024,512]{2,1,0:T(8,128)(2,1)} %param.5) | copy-start | bytes 3145732
  2.4 20.7 %copy-start.17 = (bf16[8,64]{1,0:T(8,128)(2,1)S(1)}, bf16[8,64]{1,0:T(8,128)(2,1)}, u32[]{:S(2)}) copy-start(bf16[8,64]{1,0:T(8,128)(2,1)} %gate_ref.1) | copy-start | bytes 3076
  107.1 1.0 copy-start.4
  108.1 1.0 copy-start.12
  109.1 61.7 %all-to-all-start.2 = ((bf16[64,64,128]{2,1,0:T(8,128)(2,1)}), bf16[64,64,128]{2,1,0:T(8,128)(2,1)}, u32[]{:S(2)}, u32[]{:S(2)}) async-start(bf16[64,64,128]{2,1,0:T(8,128)(2,1)} %copy-done.12), calls=%async_computation.2 | async-start | bytes 2097152 | tf_op jit(solution)/shard_map/all_to_all | solution.py:20
  134.0 1.2 copy-start.10
  136.0 1.4 copy-start.1
  137.4 1.0 copy-start.11
  170.8 61.5 %all-to-all-start.3 = ((bf16[64,64,128]{2,1,0:T(8,128)(2,1)}), bf16[64,64,128]{2,1,0:T(8,128)(2,1)}, u32[]{:S(2)}, u32[]{:S(2)}) async-start(bf16[64,64,128]{2,1,0:T(8,128)(2,1)} %copy-done.11), calls=%async_computation.3 | async-start | bytes 2097152 | tf_op jit(solution)/shard_map/all_to_all | solution.py:20
  178.4 1.6 copy-start.2
  183.1 1.0 copy-start.6
  184.1 11.3 %collective-permute-start = (bf16[4,64,512]{2,1,0:T(8,128)(2,1)}, bf16[4,64,512]{2,1,0:T(8,128)(2,1)S(1)}, u32[]{:S(2)}, u32[]{:S(2)}) collective-permute-start(bf16[4,64,512]{2,1,0:T(8,128)(2,1)} %get-tuple-element.34), channel_id=1, source_target_pairs={{0,1},{1,0},{2,3},{3,2},{4,5},{5,4},{6,7},{7,6},{8,9},{9,8},{10,11... | collective-permute-start | bytes 786440 | tf_op jit(solution)/shard_map/ppermute | solution.py:32
  195.6 0.8 copy-start.18
  196.3 36.0 %copy-start.5 = (bf16[8,128,512]{2,1,0:T(8,128)(2,1)S(1)}, bf16[8,128,512]{2,1,0:T(8,128)(2,1)}, u32[]{:S(2)}) copy-start(bf16[8,128,512]{2,1,0:T(8,128)(2,1)} %copy-done.4) | copy-start | bytes 3145732
  197.1 10.3 %collective-permute-start.1 = (f32[2,64,512]{2,1,0:T(8,128)}, f32[2,64,512]{2,1,0:T(8,128)}, u32[]{:S(2)}, u32[]{:S(2)}) collective-permute-start(f32[2,64,512]{2,1,0:T(8,128)} %slice_select_fusion), channel_id=1, source_target_pairs={{0,4},{2,6},{4,0},{6,2},{1,5},{3,7},{5,1},{7,3},{8,12},{10,14},{12... | collective-permute-start | bytes 786440 | tf_op jit(solution)/shard_map/ppermute | solution.py:32
  208.6 6.1 %collective-permute-start.2 = (f32[64,512]{1,0:T(8,128)S(1)}, f32[64,512]{1,0:T(8,128)S(1)}, u32[]{:S(2)}, u32[]{:S(2)}) collective-permute-start(f32[64,512]{1,0:T(8,128)S(1)} %get-tuple-element.48), channel_id=1, source_target_pairs={{0,2},{2,0},{4,6},{6,4},{1,3},{3,1},{5,7},{7,5},{8,10},{10,8},{12,... | collective-permute-start | bytes 393224 | tf_op jit(solution)/shard_map/ppermute | solution.py:32
  232.3 0.9 copy-start.15
  303.3 1.1 copy-start.3
  304.4 1.0 copy-start.8
  305.4 5.2 %copy-start.7 = (bf16[2,512,512]{2,1,0:T(8,128)(2,1)S(1)}, bf16[2,512,512]{2,1,0:T(8,128)(2,1)}, u32[]{:S(2)}) copy-start(bf16[2,512,512]{2,1,0:T(8,128)(2,1)} %copy-done.6) | copy-start | bytes 3145732
  305.4 20.4 %all-to-all-start.5 = ((bf16[8,160,512]{2,1,0:T(8,128)(2,1)}), bf16[8,160,512]{2,1,0:T(8,128)(2,1)}, u32[]{:S(2)}, u32[]{:S(2)}) async-start(bf16[8,160,512]{2,1,0:T(8,128)(2,1)} %copy-done.3), calls=%async_computation.5 | async-start | bytes 2621440 | tf_op jit(solution)/shard_map/all_to_all | solution.py:20
  309.8 1.2 copy-start.9
  (1 other events, 0.7 us)

commit v7 on v6

--- a/solution.py
+++ b/solution.py
@@ -10,6 +10,7 @@
 BF16 = jnp.bfloat16
 F32 = jnp.float32
 SEQ = ("z", "xh", "co")
+SENT = SEQ[::-1]
 DP = ("y", "xl")
 VMEM = pl.BlockSpec(memory_space=pltpu.VMEM)
 ANY = pl.BlockSpec(memory_space=pl.ANY)
@@ -71,16 +72,27 @@
     return x[:, k * LANES : (k + 1) * LANES]
 
 
+def lanes_of(x, k):
+    return x[:, k * LANES : (k + 1) * LANES]
+
+
+def slot(owner):
+    return lambda n: (owner % 2) * (n // 2) + (owner // 2 % 2) * (n // 4) + owner // 4
+
+
 def pack(tops, cols, out_ref, start):
     tall = len(tops) * cols
     for k in range(tops[0].shape[1] // LANES):
         rows = [lanes_of(t, k).reshape(-1, cols, LANES) for t in tops]
         rows = jnp.concatenate(rows, axis=1).astype(BF16)
-        out_ref[start : start + rows.shape[0], k * tall : (k + 1) * tall] = rows
-
-
-def unpack(piece, cols, blocks, b):
+        for i in range(rows.shape[0]):
+            out_ref[slot(start + i)(out_ref.shape[0]), k * tall : (k + 1) * tall] = rows[i]
+
+
+def unpack(src_ref, start, count, cols, blocks, b):
     tall = blocks * cols
+    piece = jnp.stack([src_ref[slot(s)(src_ref.shape[0])] for s in range(start, start + count)])
+    piece = piece.astype(F32)
     rows = [
         piece[:, k * tall + b * cols : k * tall + (b + 1) * cols].reshape(-1, LANES)
         for k in range(piece.shape[1] // tall)
@@ -138,19 +150,21 @@
 
 
 def unfold(src_ref, tmp_ref):
-    tall = tmp_ref.shape[1] // src_ref.shape[0]
-    for c in range(0, src_ref.shape[0], STEP):
+    n = src_ref.shape[0]
+    tall = tmp_ref.shape[1] // n
+    for s in range(n):
         for k in range(tmp_ref.shape[0]):
-            piece = src_ref[c : c + STEP, k * tall : (k + 1) * tall].astype(F32)
-            tmp_ref[k, pl.ds(c * tall, STEP * tall)] = piece.reshape(STEP * tall, LANES)
+            piece = src_ref[slot(s)(n), k * tall : (k + 1) * tall]
+            tmp_ref[k, pl.ds(s * tall, tall)] = piece.astype(F32)
 
 
 def fold(tmp_ref, dst_ref):
-    tall = tmp_ref.shape[1] // dst_ref.shape[0]
-    for c in range(0, dst_ref.shape[0], STEP):
+    n = dst_ref.shape[0]
+    tall = tmp_ref.shape[1] // n
+    for s in range(n):
         for k in range(tmp_ref.shape[0]):
-            piece = tmp_ref[k, pl.ds(c * tall, STEP * tall)].reshape(STEP, tall, LANES)
-            dst_ref[c : c + STEP, k * tall : (k + 1) * tall] = piece.astype(BF16)
+            piece = tmp_ref[k, pl.ds(s * tall, tall)].astype(BF16)
+            dst_ref[slot(s)(n), k * tall : (k + 1) * tall] = piece
 
 
 def column(tmp_ref, j, cols):
@@ -164,12 +178,16 @@
         tmp_ref[k, rows] = lanes_of(value, k)
 
 
-def forward_kernel(second_ref, one_ref, two_ref, by_ref, tmp_ref, res_ref):
+def columns_kernel(one_ref, by_ref, tmp_ref):
     unfold(one_ref, tmp_ref)
-    cols = by_ref.shape[0]
+    for j in range(by_ref.shape[0]):
+        by_ref[j] = column(tmp_ref, j, by_ref.shape[0]).astype(BF16)
+
+
+def forward_kernel(cols, second_ref, one_ref, two_ref, tmp_ref, res_ref):
+    unfold(one_ref, tmp_ref)
     for j in range(cols):
         mine = column(tmp_ref, j, cols).astype(BF16)
-        by_ref[j] = mine
         set_column(res_ref, j, cols, dot(second_of(second_ref, j), mine))
     fold(res_ref, two_ref)
 
@@ -189,8 +207,10 @@
     total = (keep_ref[...] + got_ref[...]).T
     coarse = total.astype(BF16).astype(F32)
     rider = jnp.concatenate([coarse, total - coarse], axis=1)
-    rider = rider.reshape(back_ref.shape[0], back_ref.shape[1] - body, LANES)
-    back_ref[:, body:] = rider.astype(BF16)
+    n = back_ref.shape[0]
+    rider = rider.reshape(n, back_ref.shape[1] - body, LANES).astype(BF16)
+    for s in range(n):
+        back_ref[slot(s)(n), body:] = rider[s]
 
 
 def delta_kernel(
@@ -199,10 +219,9 @@
     blocks, length, _ = x_ref.shape
     n = STEP * cols
     for c in range(two_ref.shape[0] // STEP):
-        two = two_ref[c * STEP : (c + 1) * STEP].astype(F32)
         for b in range(blocks):
             rows = pl.ds(c * n, n)
-            mine = unpack(two, cols, blocks, b)
+            mine = unpack(two_ref, c * STEP, STEP, cols, blocks, b)
             delta_ref[b, rows] = (mine * slope_ref[b, rows]).astype(BF16)
     pairs, cpart, width = keep_ref.shape
     for b in range(blocks):
@@ -214,14 +233,13 @@
     give_ref[...] = sum_ref[1 - me_ref[0]].astype(BF16)
 
 
-def outer_kernel(cols, back_ref, x_ref, second_ref, part_ref, by_ref):
+def outer_kernel(cols, back_ref, x_ref, second_ref, part_ref):
     blocks, length, _ = x_ref.shape
     nd, rows, width = part_ref.shape
     part = length // nd
-    piece = back_ref[...].astype(F32)
     for b in range(blocks):
-        by_ref[b] = unpack(piece, cols, blocks, b).astype(BF16)
-        add = dot(by_ref[b], x_ref[b], 1, 1).astype(BF16)
+        mine = unpack(back_ref, 0, back_ref.shape[0], cols, blocks, b).astype(BF16)
+        add = dot(mine, x_ref[b], 1, 1).astype(BF16)
         part_ref[:, b * part : (b + 1) * part] = add.reshape(nd, part, width)
     part_ref[:, blocks * part :] = second_ref[...]
 
@@ -232,12 +250,13 @@
     out_ref[...] = total[:, :half] + total[:, half:]
 
 
-def inputs_kernel(weights_ref, by_ref, input_ref, out_ref):
-    nd, (blocks, length, _) = weights_ref.shape[0], by_ref.shape
+def inputs_kernel(cols, weights_ref, back_ref, input_ref, out_ref):
+    nd, (blocks, length, _) = weights_ref.shape[0], out_ref.shape
     part = length // nd
     for b in range(blocks):
         mine = weights_ref[:, b * part : (b + 1) * part].reshape(length, length)
-        through = dot(mine, by_ref[b], 0, 0)
+        back = unpack(back_ref, 0, back_ref.shape[0], cols, blocks, b).astype(BF16)
+        through = dot(mine, back, 0, 0)
         out_ref[b] = (through + input_ref[b].astype(F32)).astype(BF16)
 
 
@@ -281,19 +300,23 @@
     one = local(
         functools.partial(rows_kernel, cols), longer, [weights, x, gate_weight], flops=wide
     )
-    col_one = exchange(one, SEQ)
-    col_two, by_col = local(
-        forward_kernel,
-        (piece, shape((cols, size2, width), BF16)),
+    col_one = exchange(one, SENT)
+    col_two = local(
+        functools.partial(forward_kernel, cols),
+        piece,
         [weights, col_one],
         [by_second, by_body],
         flops=wide // 4,
         scratch=[cells, cells],
     )
     col_one, col_two = lax.optimization_barrier((col_one, col_two))
-    two = exchange(col_two, SEQ)
-
-    gate_part = col_one[:, body:, :cpart].reshape(width, cpart)
+    two = exchange(col_two, SENT)
+    by_col = local(
+        columns_kernel, shape((cols, size2, width), BF16), [col_one], [by_body], scratch=[cells]
+    )
+
+    gate_part = col_one[:, body:, :cpart].reshape(2, 2, ns // 4, crows, cpart)
+    gate_part = gate_part.transpose(2, 1, 0, 3, 4).reshape(width, cpart)
     gate_full = gather(gate_part, DP).transpose(1, 0, 2).reshape(width, width)
     mixed_grad, slope = local(
         functools.partial(gate_kernel, cols),
@@ -302,7 +325,7 @@
         flops=wide,
     )
     two, mixed_grad = lax.optimization_barrier((two, mixed_grad))
-    col_grad = exchange(mixed_grad, SEQ)
+    col_grad = exchange(mixed_grad, SENT)
 
     gate_input, keep, give = local(
         functools.partial(delta_kernel, cols),
@@ -329,11 +352,11 @@
         flops=wide // 2,
         scratch=[cells, cells],
     )
-    back = exchange(col_back, SEQ)
-
-    parts, by_row = local(
+    back = exchange(col_back, SENT)
+
+    parts = local(
         functools.partial(outer_kernel, cols),
-        (shape(weights.shape, BF16), shape(x.shape, BF16)),
+        shape(weights.shape, BF16),
         [back, x, spart],
         [by_body, VMEM, VMEM],
         flops=wide,
@@ -341,7 +364,13 @@
     back, parts = lax.optimization_barrier((back, parts))
     parts = exchange(parts, DP)
     grad_gate = local(gate_sum_kernel, shape(gate_weight.shape, F32), [back], [by_rider])
-    grad_inputs = local(inputs_kernel, shape(x.shape, BF16), [weights, by_row, gate_input], flops=wide)
+    grad_inputs = local(
+        functools.partial(inputs_kernel, cols),
+        shape(x.shape, BF16),
+        [weights, back, gate_input],
+        [VMEM, by_body, VMEM],
+        flops=wide,
+    )
     grad_first, grad_second = local(
         total_kernel, (shape(first_factor.shape, F32), shape(second_factor.shape, F32)), [parts]
     )

time: 332 us -> 332 us (level)
  waiting for transfers between devices: 83.4 us -> 74.6 us
  local copies, waits for them, and re-layouts: 16.5 us -> 22.6 us
    all_to_all x3, waiting for transfers between devices: 62.5 us -> 54.4 us  [exchange(): return lax.all_to_all(x, axis, split_axis=0, concat_axis=0, tiled=True)]
    unnamed x38 -> x42, local copies, waits for them, and re-layouts: 14.7 us -> 18.2 us
    pallas_call x10 -> x11, Pallas kernels: 14 us -> 14.5 us  [local(): pl.pallas_call(body, grid=(1,), out_shape=out_shape, in_specs=in_specs or...]
  transfers between devices with their start and end apart: 6 -> 6, of which waited for: 6 -> 6; matrix products, arithmetic and copies ran while one was open for 1% -> 2% of each run, Pallas kernels for 2% -> 2%
where the time goes in v7:
time: 332 us; the launch traced here: 331 us
  blocking collectives  188 us (57%)
  waiting for transfers between devices  74.6 us (22%)
  starting transfers between devices  27.3 us (8%)
  local copies, waits for them, and re-layouts  22.6 us (7%)
  Pallas kernels  14.5 us (4%)
  other arithmetic  3.76 us (1%)
    all_to_all x3, blocking collectives, exchange(): return lax.all_to_all(x, axis, split_axis=0, concat_axis=0, tiled=True)  172 us
    all_to_all x3, waiting for transfers between devices, exchange(): return lax.all_to_all(x, axis, split_axis=0, concat_axis=0, tiled=True)  54.4 us
    all_to_all x3, starting transfers between devices, exchange(): return lax.all_to_all(x, axis, split_axis=0, concat_axis=0, tiled=True)  20.8 us
    ppermute x3, waiting for transfers between devices, swap(): return lax.ppermute(x, axis, [(i, i ^ bits) for i in range(n)])  20.2 us
    unnamed x42, local copies, waits for them, and re-layouts  18.2 us
    all_gather x2, blocking collectives, gather(): out = lax.all_gather(out, axis, axis=0, tiled=True)  16 us
    pallas_call x11, Pallas kernels, local(): pl.pallas_call(body, grid=(1,), out_shape=out_shape, in_specs=in_specs or...  14.5 us
  transfers between devices with their start and end apart: 6, of which 6 were waited for; matrix products, arithmetic and copies ran while one was open for 2% of the time, Pallas kernels for 2%

profile of v7, /device:TPU:1, one launch (start us, length us, event | category | flops | bytes accessed | tf_op | source)
XLA Modules:
  0.0 331.1 jit_solution(7091827980999942982)
XLA Ops:
  2.4 20.7 %all_to_all.30.weights_ref.second_ref = bf16[8,160,512]{2,1,0:T(8,128)(2,1)S(1)} all-to-all(bf16[8,160,512]{2,1,0:T(8,128)(2,1)S(1)} %shard_map.84), channel_id=1, replica_groups=mesh['z'=16,'xh'=2,'co'=2,'y'=4,'xl'=2] {'y','xl'}, dimensions={0} | all-to-all | bytes 2621440 | tf_op jit(solution)/shard_map/all_to_all | solution.py:21
  23.8 82.4 %all_to_all.31.one_ref = bf16[64,72,128]{2,1,0:T(8,128)(2,1)S(1)} all-to-all(bf16[64,72,128]{2,1,0:T(8,128)(2,1)S(1)} %shard_map.85), channel_id=1, replica_groups=mesh['z'=16,'xh'=2,'co'=2,'y'=4,'xl'=2] {'co','xh','z'}, dimensions={0} | all-to-all | bytes 2359296 | tf_op jit(solution)/shard_map/all_to_all | solution.py:21
  108.5 7.5 %all-to-all-start.2 = ((bf16[64,64,128]{2,1,0:T(8,128)(2,1)}), bf16[64,64,128]{2,1,0:T(8,128)(2,1)}, u32[]{:S(2)}, u32[]{:S(2)}) async-start(bf16[64,64,128]{2,1,0:T(8,128)(2,1)} %copy-done.4), calls=%async_computation.2 | async-start | bytes 2097152 | tf_op jit(solution)/shard_map/all_to_all | solution.py:21
  116.7 1.6 copy.14
  118.3 4.5 %all_gather.6 = bf16[2,512,64]{1,2,0:T(8,128)(2,1)S(1)} all-gather(bf16[1,512,64]{1,2,0:T(8,128)(2,1)} %copy.14), channel_id=1, replica_groups=mesh['z'=16,'xh'=2,'co'=2,'y'=4,'xl'=2] {'xl'}, dimensions={0}, use_global_device_ids=true | all-gather | bytes 196608 | tf_op jit(solution)/shard_map/all_gather | solution.py:27
  122.8 11.5 %all_gather.7 = bf16[8,512,64]{1,2,0:T(8,128)(2,1)} all-gather(bf16[2,512,64]{1,2,0:T(8,128)(2,1)S(1)} %all_gather.6), channel_id=1, replica_groups=mesh['z'=16,'xh'=2,'co'=2,'y'=4,'xl'=2] {'y'}, dimensions={0}, use_global_device_ids=true | all-gather | bytes 655360 | tf_op jit(solution)/shard_map/all_gather | solution.py:27
  134.3 2.1 copy.15.weight_ref
  141.8 27.0 %all-to-all-done.2.two_ref = bf16[64,64,128]{2,1,0:T(8,128)(2,1)} async-done(((bf16[64,64,128]{2,1,0:T(8,128)(2,1)}), bf16[64,64,128]{2,1,0:T(8,128)(2,1)}, u32[]{:S(2)}, u32[]{:S(2)}) %all-to-all-start.2) | async-done | bytes 1048608 | tf_op jit(solution)/shard_map/all_to_all | solution.py:21
  168.8 8.9 %all-to-all-start.3 = ((bf16[64,64,128]{2,1,0:T(8,128)(2,1)}), bf16[64,64,128]{2,1,0:T(8,128)(2,1)}, u32[]{:S(2)}, u32[]{:S(2)}) async-start(bf16[64,64,128]{2,1,0:T(8,128)(2,1)} %copy-done.10), calls=%async_computation.3 | async-start | bytes 2097152 | tf_op jit(solution)/shard_map/all_to_all | solution.py:21
  178.8 1.6 copy-done.8
  180.4 3.0 shard_map.88
  185.2 1.9 collective-permute-start
  187.1 9.7 %collective-permute-done = bf16[4,64,512]{2,1,0:T(8,128)(2,1)} collective-permute-done((bf16[4,64,512]{2,1,0:T(8,128)(2,1)}, bf16[4,64,512]{2,1,0:T(8,128)(2,1)}, u32[]{:S(2)}, u32[]{:S(2)}) %collective-permute-start) | collective-permute-done | bytes 262176 | tf_op jit(solution)/shard_map/ppermute | solution.py:33
  199.5 2.6 collective-permute-start.1
  202.1 8.0 %collective-permute-done.1 = f32[2,64,512]{2,1,0:T(8,128)} collective-permute-done((f32[2,64,512]{2,1,0:T(8,128)}, f32[2,64,512]{2,1,0:T(8,128)}, u32[]{:S(2)}, u32[]{:S(2)}) %collective-permute-start.1) | collective-permute-done | bytes 262176 | tf_op jit(solution)/shard_map/ppermute | solution.py:33
  212.0 1.9 collective-permute-start.2
  215.6 2.5 collective-permute-done.2.got_ref
  218.7 11.7 %all-to-all-done.3.grad_ref = bf16[64,64,128]{2,1,0:T(8,128)(2,1)} async-done(((bf16[64,64,128]{2,1,0:T(8,128)(2,1)}), bf16[64,64,128]{2,1,0:T(8,128)(2,1)}, u32[]{:S(2)}, u32[]{:S(2)}) %all-to-all-start.3) | async-done | bytes 1048608 | tf_op jit(solution)/shard_map/all_to_all | solution.py:21
  233.5 2.5 shard_map.90
  236.0 68.4 %all_to_all.32.back_ref.riders_ref = bf16[64,72,128]{2,1,0:T(8,128)(2,1)S(1)} all-to-all(bf16[64,72,128]{2,1,0:T(8,128)(2,1)S(1)} %get-tuple-element.33), channel_id=1, replica_groups=mesh['z'=16,'xh'=2,'co'=2,'y'=4,'xl'=2] {'co','xh','z'}, dimensions={0} | all-to-all | bytes 2359296 | tf_op jit(solution)/shard_map/all_to_all | solution.py:21
  306.3 4.4 %all-to-all-start.5 = ((bf16[8,160,512]{2,1,0:T(8,128)(2,1)}), bf16[8,160,512]{2,1,0:T(8,128)(2,1)}, u32[]{:S(2)}, u32[]{:S(2)}) async-start(bf16[8,160,512]{2,1,0:T(8,128)(2,1)} %copy-done.1), calls=%async_computation.5 | async-start | bytes 2621440 | tf_op jit(solution)/shard_map/all_to_all | solution.py:21
  311.4 1.8 shard_map.92
  313.2 15.7 %all-to-all-done.5.parts_ref = bf16[8,160,512]{2,1,0:T(8,128)(2,1)} async-done(((bf16[8,160,512]{2,1,0:T(8,128)(2,1)}), bf16[8,160,512]{2,1,0:T(8,128)(2,1)}, u32[]{:S(2)}, u32[]{:S(2)}) %all-to-all-start.5) | async-done | bytes 1310752 | tf_op jit(solution)/shard_map/all_to_all | solution.py:21
  328.9 2.2 shard_map.93
  (54 shorter events, 26.0 us)
Async XLA Ops:
  0.6 0.9 copy-start.15
  2.4 20.7 %copy-start = (bf16[1,1024,512]{2,1,0:T(8,128)(2,1)S(1)}, bf16[1,1024,512]{2,1,0:T(8,128)(2,1)}, u32[]{:S(2)}) copy-start(bf16[1,1024,512]{2,1,0:T(8,128)(2,1)} %param.5) | copy-start | bytes 3145732
  2.4 20.7 %copy-start.19 = (bf16[8,64]{1,0:T(8,128)(2,1)S(1)}, bf16[8,64]{1,0:T(8,128)(2,1)}, u32[]{:S(2)}) copy-start(bf16[8,64]{1,0:T(8,128)(2,1)} %gate_ref.1) | copy-start | bytes 3076
  107.5 1.0 copy-start.4
  108.5 60.3 %all-to-all-start.2 = ((bf16[64,64,128]{2,1,0:T(8,128)(2,1)}), bf16[64,64,128]{2,1,0:T(8,128)(2,1)}, u32[]{:S(2)}, u32[]{:S(2)}) async-start(bf16[64,64,128]{2,1,0:T(8,128)(2,1)} %copy-done.4), calls=%async_computation.2 | async-start | bytes 2097152 | tf_op jit(solution)/shard_map/all_to_all | solution.py:21
  136.4 1.0 copy-start.2
  137.5 1.2 copy-start.9
  139.5 1.4 copy-start.7
  140.8 1.0 copy-start.10
  168.8 61.7 %all-to-all-start.3 = ((bf16[64,64,128]{2,1,0:T(8,128)(2,1)}), bf16[64,64,128]{2,1,0:T(8,128)(2,1)}, u32[]{:S(2)}, u32[]{:S(2)}) async-start(bf16[64,64,128]{2,1,0:T(8,128)(2,1)} %copy-done.10), calls=%async_computation.3 | async-start | bytes 2097152 | tf_op jit(solution)/shard_map/all_to_all | solution.py:21
  177.7 1.0 copy-start.3
  178.8 1.6 copy-start.8
  183.4 1.0 copy-start.11
  185.2 11.6 %collective-permute-start = (bf16[4,64,512]{2,1,0:T(8,128)(2,1)}, bf16[4,64,512]{2,1,0:T(8,128)(2,1)}, u32[]{:S(2)}, u32[]{:S(2)}) collective-permute-start(bf16[4,64,512]{2,1,0:T(8,128)(2,1)} %get-tuple-element.29), channel_id=1, source_target_pairs={{0,1},{1,0},{2,3},{3,2},{4,5},{5,4},{6,7},{7,6},{8,9},{9,8},{10,11... | collective-permute-start | bytes 786440 | tf_op jit(solution)/shard_map/ppermute | solution.py:33
  198.0 0.8 copy-start.20
  199.5 10.6 %collective-permute-start.1 = (f32[2,64,512]{2,1,0:T(8,128)}, f32[2,64,512]{2,1,0:T(8,128)}, u32[]{:S(2)}, u32[]{:S(2)}) collective-permute-start(f32[2,64,512]{2,1,0:T(8,128)} %slice_select_fusion), channel_id=1, source_target_pairs={{0,4},{2,6},{4,0},{6,2},{1,5},{3,7},{5,1},{7,3},{8,12},{10,14},{12... | collective-permute-start | bytes 786440 | tf_op jit(solution)/shard_map/ppermute | solution.py:33
  212.0 6.1 %collective-permute-start.2 = (f32[64,512]{1,0:T(8,128)S(1)}, f32[64,512]{1,0:T(8,128)S(1)}, u32[]{:S(2)}, u32[]{:S(2)}) collective-permute-start(f32[64,512]{1,0:T(8,128)S(1)} %get-tuple-element.40), channel_id=1, source_target_pairs={{0,2},{2,0},{4,6},{6,4},{1,3},{3,1},{5,7},{7,5},{8,10},{10,8},{12,... | collective-permute-start | bytes 393224 | tf_op jit(solution)/shard_map/ppermute | solution.py:33
  214.6 1.0 copy-start.5
  230.5 1.2 copy-start.6
  231.7 0.9 copy-start.13
  232.6 0.9 copy-start.17
  305.2 1.1 copy-start.1
  306.3 5.2 %copy-start.12 = (bf16[2,512,512]{2,1,0:T(8,128)(2,1)S(1)}, bf16[2,512,512]{2,1,0:T(8,128)(2,1)}, u32[]{:S(2)}) copy-start(bf16[2,512,512]{2,1,0:T(8,128)(2,1)} %copy-done.11) | copy-start | bytes 3145732
  306.3 22.6 %all-to-all-start.5 = ((bf16[8,160,512]{2,1,0:T(8,128)(2,1)}), bf16[8,160,512]{2,1,0:T(8,128)(2,1)}, u32[]{:S(2)}, u32[]{:S(2)}) async-start(bf16[8,160,512]{2,1,0:T(8,128)(2,1)} %copy-done.1), calls=%async_computation.5 | async-start | bytes 2621440 | tf_op jit(solution)/shard_map/all_to_all | solution.py:21
  (3 other events, 2.2 us)

commit v8 on v7

--- a/solution.py
+++ b/solution.py
@@ -10,10 +10,9 @@
 BF16 = jnp.bfloat16
 F32 = jnp.float32
 SEQ = ("z", "xh", "co")
-SENT = SEQ[::-1]
 DP = ("y", "xl")
 VMEM = pl.BlockSpec(memory_space=pltpu.VMEM)
-ANY = pl.BlockSpec(memory_space=pl.ANY)
+HBM = pl.BlockSpec(memory_space=pltpu.HBM)
 SMEM = pl.BlockSpec(memory_space=pltpu.SMEM)
 
 
@@ -33,7 +32,7 @@
     return lax.ppermute(x, axis, [(i, i ^ bits) for i in range(n)])
 
 
-def local(body, out_shape, operands, in_specs=None, out_specs=None, flops=0, scratch=(), alias=None):
+def local(body, out_shape, operands, in_specs=None, out_specs=None, flops=0, scratch=(), room=60):
     outs = jax.tree.leaves(out_shape)
     moved = sum(a.size * a.dtype.itemsize for a in list(operands) + outs)
     return pl.pallas_call(
@@ -42,10 +41,9 @@
         out_shape=out_shape,
         in_specs=in_specs or [VMEM] * len(operands),
         out_specs=out_specs or jax.tree.map(lambda _: VMEM, out_shape),
-        input_output_aliases=alias or {},
         scratch_shapes=list(scratch),
         cost_estimate=pl.CostEstimate(flops=flops, bytes_accessed=moved, transcendentals=0),
-        compiler_params=pltpu.CompilerParams(vmem_limit_bytes=28 << 20),
+        compiler_params=pltpu.CompilerParams(vmem_limit_bytes=room << 20),
     )(*operands)
 
 
@@ -76,23 +74,17 @@
     return x[:, k * LANES : (k + 1) * LANES]
 
 
-def slot(owner):
-    return lambda n: (owner % 2) * (n // 2) + (owner // 2 % 2) * (n // 4) + owner // 4
-
-
 def pack(tops, cols, out_ref, start):
     tall = len(tops) * cols
     for k in range(tops[0].shape[1] // LANES):
         rows = [lanes_of(t, k).reshape(-1, cols, LANES) for t in tops]
         rows = jnp.concatenate(rows, axis=1).astype(BF16)
-        for i in range(rows.shape[0]):
-            out_ref[slot(start + i)(out_ref.shape[0]), k * tall : (k + 1) * tall] = rows[i]
+        out_ref[start : start + rows.shape[0], k * tall : (k + 1) * tall] = rows
 
 
 def unpack(src_ref, start, count, cols, blocks, b):
     tall = blocks * cols
-    piece = jnp.stack([src_ref[slot(s)(src_ref.shape[0])] for s in range(start, start + count)])
-    piece = piece.astype(F32)
+    piece = src_ref[start : start + count].astype(F32)
     rows = [
         piece[:, k * tall + b * cols : k * tall + (b + 1) * cols].reshape(-1, LANES)
         for k in range(piece.shape[1] // tall)
@@ -150,21 +142,18 @@
 
 
 def unfold(src_ref, tmp_ref):
-    n = src_ref.shape[0]
-    tall = tmp_ref.shape[1] // n
-    for s in range(n):
+    tall = tmp_ref.shape[1] // src_ref.shape[0]
+    for c in range(0, src_ref.shape[0], STEP):
         for k in range(tmp_ref.shape[0]):
-            piece = src_ref[slot(s)(n), k * tall : (k + 1) * tall]
-            tmp_ref[k, pl.ds(s * tall, tall)] = piece.astype(F32)
-
-
-def fold(tmp_ref, dst_ref):
-    n = dst_ref.shape[0]
-    tall = tmp_ref.shape[1] // n
-    for s in range(n):
-        for k in range(tmp_ref.shape[0]):
-            piece = tmp_ref[k, pl.ds(s * tall, tall)].astype(BF16)
-            dst_ref[slot(s)(n), k * tall : (k + 1) * tall] = piece
+            piece = src_ref[c : c + STEP, k * tall : (k + 1) * tall].astype(F32)
+            tmp_ref[k, pl.ds(c * tall, STEP * tall)] = piece.reshape(STEP * tall, LANES)
+
+
+def fold(tmp_ref, dst_ref, start):
+    tall = tmp_ref.shape[1] // dst_ref.shape[0]
+    for k in range(tmp_ref.shape[0]):
+        piece = tmp_ref[k, pl.ds(start * tall, STEP * tall)].reshape(STEP, tall, LANES)
+        dst_ref[start : start + STEP, k * tall : (k + 1) * tall] = piece.astype(BF16)
 
 
 def column(tmp_ref, j, cols):
@@ -184,33 +173,54 @@
         by_ref[j] = column(tmp_ref, j, by_ref.shape[0]).astype(BF16)
 
 
-def forward_kernel(cols, second_ref, one_ref, two_ref, tmp_ref, res_ref):
+def forward_kernel(cols, second_ref, one_ref, two_ref, tmp_ref, res_ref, done_ref, sems):
     unfold(one_ref, tmp_ref)
     for j in range(cols):
         mine = column(tmp_ref, j, cols).astype(BF16)
         set_column(res_ref, j, cols, dot(second_of(second_ref, j), mine))
-    fold(res_ref, two_ref)
-
-
-def backward_kernel(second_ref, grad_ref, by_ref, keep_ref, got_ref, back_ref, part_ref, tmp_ref, res_ref):
+    copies = []
+    for i, c in enumerate(range(0, done_ref.shape[0], STEP)):
+        fold(res_ref, done_ref, c)
+        here = pl.ds(c, STEP)
+        copies.append(pltpu.make_async_copy(done_ref.at[here], two_ref.at[here], sems.at[i]))
+        copies[-1].start()
+    for copy in copies:
+        copy.wait()
+
+
+def backward_kernel(
+    second_ref, grad_ref, by_ref, keep_ref, got_ref, back_ref, part_ref,
+    tmp_ref, res_ref, mine_ref, sums_ref, sems,
+):
+    copies = [
+        pltpu.make_async_copy(by_ref, mine_ref, sems.at[0]),
+        pltpu.make_async_copy(keep_ref, sums_ref.at[0], sems.at[1]),
+        pltpu.make_async_copy(got_ref, sums_ref.at[1], sems.at[2]),
+    ]
+    for copy in copies:
+        copy.start()
     unfold(grad_ref, tmp_ref)
-    cols = by_ref.shape[0]
+    for copy in copies:
+        copy.wait()
+    cols = mine_ref.shape[0]
     nd, _, width = part_ref.shape
     for j in range(cols):
         mine = column(tmp_ref, j, cols).astype(BF16)
         set_column(res_ref, j, cols, dot(second_of(second_ref, j), mine, 0, 0))
         rows, lanes = beside(j, LANES // nd, width)
-        part = dot(mine, by_ref[j], 1, 1).reshape(nd, LANES // nd, LANES)
+        part = dot(mine, mine_ref[j], 1, 1).reshape(nd, LANES // nd, LANES)
         part_ref[:, rows, lanes] = part.astype(BF16)
-    fold(res_ref, back_ref)
     body = grad_ref.shape[1]
-    total = (keep_ref[...] + got_ref[...]).T
+    for c in range(0, grad_ref.shape[0], STEP):
+        tall = tmp_ref.shape[1] // grad_ref.shape[0]
+        for k in range(tmp_ref.shape[0]):
+            piece = res_ref[k, pl.ds(c * tall, STEP * tall)].reshape(STEP, tall, LANES)
+            back_ref[c : c + STEP, k * tall : (k + 1) * tall] = piece.astype(BF16)
+    total = (sums_ref[0] + sums_ref[1]).T
     coarse = total.astype(BF16).astype(F32)
     rider = jnp.concatenate([coarse, total - coarse], axis=1)
-    n = back_ref.shape[0]
-    rider = rider.reshape(n, back_ref.shape[1] - body, LANES).astype(BF16)
-    for s in range(n):
-        back_ref[slot(s)(n), body:] = rider[s]
+    rider = rider.reshape(back_ref.shape[0], back_ref.shape[1] - body, LANES)
+    back_ref[:, body:] = rider.astype(BF16)
 
 
 def delta_kernel(
@@ -233,15 +243,21 @@
     give_ref[...] = sum_ref[1 - me_ref[0]].astype(BF16)
 
 
-def outer_kernel(cols, back_ref, x_ref, second_ref, part_ref):
+def outer_kernel(cols, back_ref, x_ref, second_ref, out_ref, part_ref, sems):
     blocks, length, _ = x_ref.shape
     nd, rows, width = part_ref.shape
     part = length // nd
+    copies = [pltpu.make_async_copy(second_ref, out_ref.at[:, pl.ds(rows, second_ref.shape[1])], sems.at[0])]
+    copies[0].start()
     for b in range(blocks):
         mine = unpack(back_ref, 0, back_ref.shape[0], cols, blocks, b).astype(BF16)
         add = dot(mine, x_ref[b], 1, 1).astype(BF16)
-        part_ref[:, b * part : (b + 1) * part] = add.reshape(nd, part, width)
-    part_ref[:, blocks * part :] = second_ref[...]
+        here = pl.ds(b * part, part)
+        part_ref[:, here] = add.reshape(nd, part, width)
+        copies.append(pltpu.make_async_copy(part_ref.at[:, here], out_ref.at[:, here], sems.at[b + 1]))
+        copies[-1].start()
+    for copy in copies:
+        copy.wait()
 
 
 def gate_sum_kernel(riders_ref, out_ref):
@@ -300,23 +316,23 @@
     one = local(
         functools.partial(rows_kernel, cols), longer, [weights, x, gate_weight], flops=wide
     )
-    col_one = exchange(one, SENT)
+    col_one = exchange(one, SEQ)
     col_two = local(
         functools.partial(forward_kernel, cols),
         piece,
         [weights, col_one],
         [by_second, by_body],
+        HBM,
         flops=wide // 4,
-        scratch=[cells, cells],
+        scratch=[cells, cells, pltpu.VMEM(piece.shape, BF16), pltpu.SemaphoreType.DMA((ns // STEP,))],
     )
     col_one, col_two = lax.optimization_barrier((col_one, col_two))
-    two = exchange(col_two, SENT)
+    two = exchange(col_two, SEQ)
     by_col = local(
         columns_kernel, shape((cols, size2, width), BF16), [col_one], [by_body], scratch=[cells]
     )
 
-    gate_part = col_one[:, body:, :cpart].reshape(2, 2, ns // 4, crows, cpart)
-    gate_part = gate_part.transpose(2, 1, 0, 3, 4).reshape(width, cpart)
+    gate_part = col_one[:, body:, :cpart].reshape(width, cpart)
     gate_full = gather(gate_part, DP).transpose(1, 0, 2).reshape(width, width)
     mixed_grad, slope = local(
         functools.partial(gate_kernel, cols),
@@ -325,7 +341,7 @@
         flops=wide,
     )
     two, mixed_grad = lax.optimization_barrier((two, mixed_grad))
-    col_grad = exchange(mixed_grad, SENT)
+    col_grad = exchange(mixed_grad, SEQ)
 
     gate_input, keep, give = local(
         functools.partial(delta_kernel, cols),
@@ -338,6 +354,7 @@
         [SMEM] + [VMEM] * 4,
         flops=2 * wide,
         scratch=[pltpu.VMEM(x.shape, BF16), pltpu.VMEM((2, ny, cpart, width), F32)],
+        room=28,
     )
     gsum = keep + swap(give, "xl", 1).astype(F32)
     keep, got = halve(gsum.reshape(2, ny // 2, cpart, width), "y", 2)
@@ -348,18 +365,29 @@
         backward_kernel,
         (longer, shape((nd, tail, width), BF16)),
         [weights, col_grad, by_col, keep, got],
-        [by_second] + [VMEM] * 4,
+        [by_second, VMEM, HBM, HBM, HBM],
         flops=wide // 2,
-        scratch=[cells, cells],
-    )
-    back = exchange(col_back, SENT)
+        scratch=[
+            cells,
+            cells,
+            pltpu.VMEM((cols, size2, width), BF16),
+            pltpu.VMEM((2, cpart, width), F32),
+            pltpu.SemaphoreType.DMA((3,)),
+        ],
+    )
+    back = exchange(col_back, SEQ)
 
     parts = local(
         functools.partial(outer_kernel, cols),
         shape(weights.shape, BF16),
         [back, x, spart],
-        [by_body, VMEM, VMEM],
+        [by_body, VMEM, HBM],
+        HBM,
         flops=wide,
+        scratch=[
+            pltpu.VMEM((nd, blocks * part, width), BF16),
+            pltpu.SemaphoreType.DMA((blocks + 1,)),
+        ],
     )
     back, parts = lax.optimization_barrier((back, parts))
     parts = exchange(parts, DP)
@@ -372,7 +400,7 @@
         flops=wide,
     )
     grad_first, grad_second = local(
-        total_kernel, (shape(first_factor.shape, F32), shape(second_factor.shape, F32)), [parts]
+        total_kernel, (shape(first_factor.shape, F32), shape(second_factor.shape, F32)), [parts], room=28
     )
     return (grad_inputs.reshape(inputs.shape), grad_first, grad_second, grad_gate)
 

time: 332 us -> 343 us (1.033); the launches traced: 331 us -> 338 us
  Pallas kernels: 14.5 us -> 38.9 us
  local copies, waits for them, and re-layouts: 22.6 us -> 4.58 us
  waiting for transfers between devices: 74.6 us -> 83.3 us
    pallas_call x11, Pallas kernels: 14.5 us -> 38.9 us  [local(): pl.pallas_call(body, grid=(1,), out_shape=out_shape, in_specs=in_specs or...]
    unnamed x42 -> x10, local copies, waits for them, and re-layouts: 18.2 us -> 2.55 us
    all_to_all x3, waiting for transfers between devices: 54.4 us -> 65.3 us  [exchange(): return lax.all_to_all(x, axis, split_axis=0, concat_axis=0, tiled=True)]
  transfers between devices with their start and end apart: 6 -> 6, of which waited for: 6 -> 6; matrix products, arithmetic and copies ran while one was open for 2% -> 1% of each run, Pallas kernels for 2% -> 4%
where the time goes in v8:
time: 343 us; the launch traced here: 338 us
  blocking collectives  185 us (54%)
  waiting for transfers between devices  83.3 us (24%)
  Pallas kernels  38.9 us (11%)
  starting transfers between devices  24.9 us (7%)
  local copies, waits for them, and re-layouts  4.58 us (1%)
    all_to_all x3, blocking collectives, exchange(): return lax.all_to_all(x, axis, split_axis=0, concat_axis=0, tiled=True)  170 us
    all_to_all x3, waiting for transfers between devices, exchange(): return lax.all_to_all(x, axis, split_axis=0, concat_axis=0, tiled=True)  65.3 us
    pallas_call x11, Pallas kernels, local(): pl.pallas_call(body, grid=(1,), out_shape=out_shape, in_specs=in_specs or...  38.9 us
    all_to_all x3, starting transfers between devices, exchange(): return lax.all_to_all(x, axis, split_axis=0, concat_axis=0, tiled=True)  18.7 us
    ppermute x3, waiting for transfers between devices, swap(): return lax.ppermute(x, axis, [(i, i ^ bits) for i in range(n)])  18 us
    all_gather x2, blocking collectives, gather(): out = lax.all_gather(out, axis, axis=0, tiled=True)  14.9 us
  transfers between devices with their start and end apart: 6, of which 6 were waited for; matrix products, arithmetic and copies ran while one was open for 1% of the time, Pallas kernels for 4%

profile of v8, /device:TPU:1, one launch (start us, length us, event | category | flops | bytes accessed | tf_op | source)
XLA Modules:
  0.0 338.2 jit_solution(16615106529832608763)
XLA Ops:
  0.6 2.1 shard_map.84
  2.7 19.5 %all_to_all.30.weights_ref.second_ref = bf16[8,160,512]{2,1,0:T(8,128)(2,1)} all-to-all(bf16[8,160,512]{2,1,0:T(8,128)(2,1)} %shard_map.84), channel_id=1, replica_groups=mesh['z'=16,'xh'=2,'co'=2,'y'=4,'xl'=2] {'y','xl'}, dimensions={0} | all-to-all | bytes 2621440 | tf_op jit(solution)/shard_map/all_to_all | solution.py:20
  22.2 3.4 shard_map.85
  25.6 83.6 %all_to_all.31.one_ref = bf16[64,72,128]{2,1,0:T(8,128)(2,1)} all-to-all(bf16[64,72,128]{2,1,0:T(8,128)(2,1)} %shard_map.85), channel_id=1, replica_groups=mesh['z'=16,'xh'=2,'co'=2,'y'=4,'xl'=2] {'z','xh','co'}, dimensions={0} | all-to-all | bytes 2359296 | tf_op jit(solution)/shard_map/all_to_all | solution.py:20
  109.3 3.4 %shard_map.86 = bf16[64,64,128]{2,1,0:T(8,128)(2,1)} custom-call(bf16[8,160,512]{2,1,0:T(8,128)(2,1)} %all_to_all.30.weights_ref.second_ref, bf16[64,72,128]{2,1,0:T(8,128)(2,1)} %all_to_all.31.one_ref), custom_call_target="tpu_custom_call" | custom-call | flops 134217728 | bytes 3538944 | tf_op jit(solution)/shard_map/pallas_call | solution.py:38
  112.7 7.5 %all-to-all-start.2 = ((bf16[64,64,128]{2,1,0:T(8,128)(2,1)}), bf16[64,64,128]{2,1,0:T(8,128)(2,1)S(1)}, u32[]{:S(2)}, u32[]{:S(2)}) async-start(bf16[64,64,128]{2,1,0:T(8,128)(2,1)} %shard_map.86), calls=%async_computation.2 | async-start | bytes 2097152 | tf_op jit(solution)/shard_map/all_to_all | solution.py:20
  121.2 4.1 %all_gather.6 = bf16[2,512,64]{1,2,0:T(8,128)(2,1)S(1)} all-gather(bf16[1,512,64]{1,2,0:T(8,128)(2,1)S(1)} %copy.13), channel_id=1, replica_groups=mesh['z'=16,'xh'=2,'co'=2,'y'=4,'xl'=2] {'xl'}, dimensions={0}, use_global_device_ids=true | all-gather | bytes 196608 | tf_op jit(solution)/shard_map/all_gather | solution.py:26
  125.4 10.8 %all_gather.7 = bf16[8,512,64]{1,2,0:T(8,128)(2,1)S(1)} all-gather(bf16[2,512,64]{1,2,0:T(8,128)(2,1)S(1)} %all_gather.6), channel_id=1, replica_groups=mesh['z'=16,'xh'=2,'co'=2,'y'=4,'xl'=2] {'y'}, dimensions={0}, use_global_device_ids=true | all-gather | bytes 655360 | tf_op jit(solution)/shard_map/all_gather | solution.py:26
  137.1 4.2 %shard_map.87 = (bf16[64,64,128]{2,1,0:T(8,128)(2,1)}, f32[2,512,512]{2,1,0:T(8,128)}) custom-call(bf16[2,512,512]{2,1,0:T(8,128)(2,1)} %bitcast.14, bf16[512,512]{1,0:T(8,128)(2,1)} %copy.14.weight_ref, bf16[2,512,512]{2,1,0:T(8,128)(2,1)} %bitcast.18), custom_call_target="tpu_custom_call" | custom-call | flops 536870912 | bytes 5767168 | tf_op jit(solution)/shard_map/pallas_call | solution.py:38
  141.4 32.9 %all-to-all-done.2.two_ref = bf16[64,64,128]{2,1,0:T(8,128)(2,1)S(1)} async-done(((bf16[64,64,128]{2,1,0:T(8,128)(2,1)}), bf16[64,64,128]{2,1,0:T(8,128)(2,1)S(1)}, u32[]{:S(2)}, u32[]{:S(2)}) %all-to-all-start.2) | async-done | bytes 1048608 | tf_op jit(solution)/shard_map/all_to_all | solution.py:20
  174.3 7.6 %all-to-all-start.3 = ((bf16[64,64,128]{2,1,0:T(8,128)(2,1)}), bf16[64,64,128]{2,1,0:T(8,128)(2,1)}, u32[]{:S(2)}, u32[]{:S(2)}) async-start(bf16[64,64,128]{2,1,0:T(8,128)(2,1)} %get-tuple-element.25), calls=%async_computation.3 | async-start | bytes 2097152 | tf_op jit(solution)/shard_map/all_to_all | solution.py:20
  185.8 1.9 collective-permute-start
  187.7 9.0 %collective-permute-done = bf16[4,64,512]{2,1,0:T(8,128)(2,1)S(1)} collective-permute-done((bf16[4,64,512]{2,1,0:T(8,128)(2,1)S(1)}, bf16[4,64,512]{2,1,0:T(8,128)(2,1)S(1)}, u32[]{:S(2)}, u32[]{:S(2)}) %collective-permute-start) | collective-permute-done | bytes 262176 | tf_op jit(solution)/shard_map/ppermute | solution.py:32
  196.8 2.3 collective-permute-start.1
  199.1 7.8 %collective-permute-done.1 = f32[2,64,512]{2,1,0:T(8,128)S(1)} collective-permute-done((f32[2,64,512]{2,1,0:T(8,128)S(1)}, f32[2,64,512]{2,1,0:T(8,128)S(1)}, u32[]{:S(2)}, u32[]{:S(2)}) %collective-permute-start.1) | collective-permute-done | bytes 262176 | tf_op jit(solution)/shard_map/ppermute | solution.py:32
  207.7 2.0 collective-permute-start.2
  209.7 2.8 shard_map.89.by_ref
  213.8 22.0 %all-to-all-done.3.grad_ref = bf16[64,64,128]{2,1,0:T(8,128)(2,1)} async-done(((bf16[64,64,128]{2,1,0:T(8,128)(2,1)}), bf16[64,64,128]{2,1,0:T(8,128)(2,1)}, u32[]{:S(2)}, u32[]{:S(2)}) %all-to-all-start.3) | async-done | bytes 1048608 | tf_op jit(solution)/shard_map/all_to_all | solution.py:20
  235.8 4.8 %shard_map.90 = (bf16[64,72,128]{2,1,0:T(8,128)(2,1)}, bf16[8,32,512]{2,1,0:T(8,128)(2,1)}) custom-call(bf16[8,160,512]{2,1,0:T(8,128)(2,1)} %all_to_all.30.weights_ref.second_ref, bf16[64,64,128]{2,1,0:T(8,128)(2,1)} %all-to-all-done.3.grad_ref, bf16[8,128,512]{2,1,0:T(8,128)(2,1)} %shard_map.89.by_ref, f32[64,512]{1,0:T(8,128)} %get-tuple-element.31.keep_ref, ...), custom_call_target="tpu_custom_call" | custom-call | flops 268435456 | bytes 5111808 | tf_op jit(solution)/shard_map/pallas_call | solution.py:38
  240.6 66.9 %all_to_all.32.back_ref.riders_ref = bf16[64,72,128]{2,1,0:T(8,128)(2,1)} all-to-all(bf16[64,72,128]{2,1,0:T(8,128)(2,1)} %get-tuple-element.33), channel_id=1, replica_groups=mesh['z'=16,'xh'=2,'co'=2,'y'=4,'xl'=2] {'z','xh','co'}, dimensions={0} | all-to-all | bytes 2359296 | tf_op jit(solution)/shard_map/all_to_all | solution.py:20
  307.5 10.6 %shard_map.91 = bf16[8,160,512]{2,1,0:T(8,128)(2,1)} custom-call(bf16[64,72,128]{2,1,0:T(8,128)(2,1)} %all_to_all.32.back_ref.riders_ref, bf16[2,512,512]{2,1,0:T(8,128)(2,1)} %bitcast.15, bf16[8,32,512]{2,1,0:T(8,128)(2,1)} %get-tuple-element.34.second_ref), custom_call_target="tpu_custom_call" | custom-call | flops 536870912 | bytes 3801088 | tf_op jit(solution)/shard_map/pallas_call | solution.py:38
  318.1 3.6 %all-to-all-start.5 = ((bf16[8,160,512]{2,1,0:T(8,128)(2,1)}), bf16[8,160,512]{2,1,0:T(8,128)(2,1)S(1)}, u32[]{:S(2)}, u32[]{:S(2)}) async-start(bf16[8,160,512]{2,1,0:T(8,128)(2,1)} %shard_map.91), calls=%async_computation.5 | async-start | bytes 2621440 | tf_op jit(solution)/shard_map/all_to_all | solution.py:20
  323.3 3.6 %shard_map.92 = bf16[2,512,512]{2,1,0:T(8,128)(2,1)} custom-call(bf16[8,160,512]{2,1,0:T(8,128)(2,1)} %all_to_all.30.weights_ref.second_ref, bf16[64,72,128]{2,1,0:T(8,128)(2,1)} %all_to_all.32.back_ref.riders_ref, bf16[2,512,512]{2,1,0:T(8,128)(2,1)} %copy-done.3), custom_call_target="tpu_custom_call" | custom-call | flops 536870912 | bytes 4587520 | tf_op jit(solution)/shard_map/pallas_call | solution.py:38
  327.0 10.4 %all-to-all-done.5.parts_ref = bf16[8,160,512]{2,1,0:T(8,128)(2,1)S(1)} async-done(((bf16[8,160,512]{2,1,0:T(8,128)(2,1)}), bf16[8,160,512]{2,1,0:T(8,128)(2,1)S(1)}, u32[]{:S(2)}, u32[]{:S(2)}) %all-to-all-start.5) | async-done | bytes 1310752 | tf_op jit(solution)/shard_map/all_to_all | solution.py:20
  (21 shorter events, 10.5 us)
Async XLA Ops:
  112.7 61.6 %all-to-all-start.2 = ((bf16[64,64,128]{2,1,0:T(8,128)(2,1)}), bf16[64,64,128]{2,1,0:T(8,128)(2,1)S(1)}, u32[]{:S(2)}, u32[]{:S(2)}) async-start(bf16[64,64,128]{2,1,0:T(8,128)(2,1)} %shard_map.86), calls=%async_computation.2 | async-start | bytes 2097152 | tf_op jit(solution)/shard_map/all_to_all | solution.py:20
  141.4 40.5 %copy-start = (bf16[1,1024,512]{2,1,0:T(8,128)(2,1)S(1)}, bf16[1,1024,512]{2,1,0:T(8,128)(2,1)}, u32[]{:S(2)}) copy-start(bf16[1,1024,512]{2,1,0:T(8,128)(2,1)} %param.5) | copy-start | bytes 3145732
  141.4 40.5 %copy-start.1 = (bf16[512,512]{1,0:T(8,128)(2,1)S(1)}, bf16[512,512]{1,0:T(8,128)(2,1)}, u32[]{:S(2)}) copy-start(bf16[512,512]{1,0:T(8,128)(2,1)} %copy.14.weight_ref) | copy-start | bytes 1572868
  174.3 61.5 %all-to-all-start.3 = ((bf16[64,64,128]{2,1,0:T(8,128)(2,1)}), bf16[64,64,128]{2,1,0:T(8,128)(2,1)}, u32[]{:S(2)}, u32[]{:S(2)}) async-start(bf16[64,64,128]{2,1,0:T(8,128)(2,1)} %get-tuple-element.25), calls=%async_computation.3 | async-start | bytes 2097152 | tf_op jit(solution)/shard_map/all_to_all | solution.py:20
  181.9 1.6 copy-start.2
  184.8 1.0 copy-start.3
  185.8 10.9 %collective-permute-start = (bf16[4,64,512]{2,1,0:T(8,128)(2,1)S(1)}, bf16[4,64,512]{2,1,0:T(8,128)(2,1)S(1)}, u32[]{:S(2)}, u32[]{:S(2)}) collective-permute-start(bf16[4,64,512]{2,1,0:T(8,128)(2,1)S(1)} %get-tuple-element.29), channel_id=1, source_target_pairs={{0,1},{1,0},{2,3},{3,2},{4,5},{5,4},{6,7},{7,6},{8,9},{9,8},{10,11... | collective-permute-start | bytes 786440 | tf_op jit(solution)/shard_map/ppermute | solution.py:32
  196.8 10.1 %collective-permute-start.1 = (f32[2,64,512]{2,1,0:T(8,128)S(1)}, f32[2,64,512]{2,1,0:T(8,128)S(1)}, u32[]{:S(2)}, u32[]{:S(2)}) collective-permute-start(f32[2,64,512]{2,1,0:T(8,128)S(1)} %slice_select_fusion), channel_id=1, source_target_pairs={{0,4},{2,6},{4,0},{6,2},{1,5},{3,7},{5,1},{7,3},{8,12},{10,14},{12... | collective-permute-start | bytes 786440 | tf_op jit(solution)/shard_map/ppermute | solution.py:32
  207.7 6.1 %collective-permute-start.2 = (f32[64,512]{1,0:T(8,128)S(1)}, f32[64,512]{1,0:T(8,128)S(1)}, u32[]{:S(2)}, u32[]{:S(2)}) collective-permute-start(f32[64,512]{1,0:T(8,128)S(1)} %get-tuple-element.40), channel_id=1, source_target_pairs={{0,2},{2,0},{4,6},{6,4},{1,3},{3,1},{5,7},{7,5},{8,10},{10,8},{12,... | collective-permute-start | bytes 393224 | tf_op jit(solution)/shard_map/ppermute | solution.py:32
  213.8 22.0 %copy-start.4 = (f32[64,512]{1,0:T(8,128)}, f32[64,512]{1,0:T(8,128)S(1)}, u32[]{:S(2)}) copy-start(f32[64,512]{1,0:T(8,128)S(1)} %collective-permute-done.2.got_ref) | copy-start | bytes 393220
  318.1 19.3 %all-to-all-start.5 = ((bf16[8,160,512]{2,1,0:T(8,128)(2,1)}), bf16[8,160,512]{2,1,0:T(8,128)(2,1)S(1)}, u32[]{:S(2)}, u32[]{:S(2)}) async-start(bf16[8,160,512]{2,1,0:T(8,128)(2,1)} %shard_map.91), calls=%async_computation.5 | async-start | bytes 2621440 | tf_op jit(solution)/shard_map/all_to_all | solution.py:20

commit v9 on v6

--- a/solution.py
+++ b/solution.py
@@ -214,14 +214,14 @@
     give_ref[...] = sum_ref[1 - me_ref[0]].astype(BF16)
 
 
-def outer_kernel(cols, back_ref, x_ref, second_ref, part_ref, by_ref):
+def outer_kernel(cols, back_ref, x_ref, second_ref, part_ref):
     blocks, length, _ = x_ref.shape
     nd, rows, width = part_ref.shape
     part = length // nd
     piece = back_ref[...].astype(F32)
     for b in range(blocks):
-        by_ref[b] = unpack(piece, cols, blocks, b).astype(BF16)
-        add = dot(by_ref[b], x_ref[b], 1, 1).astype(BF16)
+        mine = unpack(piece, cols, blocks, b).astype(BF16)
+        add = dot(mine, x_ref[b], 1, 1).astype(BF16)
         part_ref[:, b * part : (b + 1) * part] = add.reshape(nd, part, width)
     part_ref[:, blocks * part :] = second_ref[...]
 
@@ -232,12 +232,13 @@
     out_ref[...] = total[:, :half] + total[:, half:]
 
 
-def inputs_kernel(weights_ref, by_ref, input_ref, out_ref):
-    nd, (blocks, length, _) = weights_ref.shape[0], by_ref.shape
+def inputs_kernel(cols, weights_ref, back_ref, input_ref, out_ref):
+    nd, (blocks, length, _) = weights_ref.shape[0], out_ref.shape
     part = length // nd
+    piece = back_ref[...].astype(F32)
     for b in range(blocks):
         mine = weights_ref[:, b * part : (b + 1) * part].reshape(length, length)
-        through = dot(mine, by_ref[b], 0, 0)
+        through = dot(mine, unpack(piece, cols, blocks, b).astype(BF16), 0, 0)
         out_ref[b] = (through + input_ref[b].astype(F32)).astype(BF16)
 
 
@@ -331,9 +332,9 @@
     )
     back = exchange(col_back, SEQ)
 
-    parts, by_row = local(
+    parts = local(
         functools.partial(outer_kernel, cols),
-        (shape(weights.shape, BF16), shape(x.shape, BF16)),
+        shape(weights.shape, BF16),
         [back, x, spart],
         [by_body, VMEM, VMEM],
         flops=wide,
@@ -341,7 +342,13 @@
     back, parts = lax.optimization_barrier((back, parts))
     parts = exchange(parts, DP)
     grad_gate = local(gate_sum_kernel, shape(gate_weight.shape, F32), [back], [by_rider])
-    grad_inputs = local(inputs_kernel, shape(x.shape, BF16), [weights, by_row, gate_input], flops=wide)
+    grad_inputs = local(
+        functools.partial(inputs_kernel, cols),
+        shape(x.shape, BF16),
+        [weights, back, gate_input],
+        [VMEM, by_body, VMEM],
+        flops=wide,
+    )
     grad_first, grad_second = local(
         total_kernel, (shape(first_factor.shape, F32), shape(second_factor.shape, F32)), [parts]
     )

time: 332 us -> 331 us (level)
    unnamed x38 -> x34, local copies, waits for them, and re-layouts: 14.7 us -> 13.2 us
where the time goes in v9:
time: 331 us; the launch traced here: 327 us
  blocking collectives  185 us (56%)
  waiting for transfers between devices  83.9 us (25%)
  starting transfers between devices  26.3 us (8%)
  local copies, waits for them, and re-layouts  15 us (5%)
  Pallas kernels  13.9 us (4%)
    all_to_all x3, blocking collectives, exchange(): return lax.all_to_all(x, axis, split_axis=0, concat_axis=0, tiled=True)  169 us
    all_to_all x3, waiting for transfers between devices, exchange(): return lax.all_to_all(x, axis, split_axis=0, concat_axis=0, tiled=True)  62.9 us
    ppermute x3, waiting for transfers between devices, swap(): return lax.ppermute(x, axis, [(i, i ^ bits) for i in range(n)])  21 us
    all_to_all x3, starting transfers between devices, exchange(): return lax.all_to_all(x, axis, split_axis=0, concat_axis=0, tiled=True)  19.6 us
    all_gather x2, blocking collectives, gather(): out = lax.all_gather(out, axis, axis=0, tiled=True)  15.3 us
    pallas_call x10, Pallas kernels, local(): pl.pallas_call(body, grid=(1,), out_shape=out_shape, in_specs=in_specs or...  13.9 us
    unnamed x34, local copies, waits for them, and re-layouts  13.2 us
    ppermute x3, starting transfers between devices, swap(): return lax.ppermute(x, axis, [(i, i ^ bits) for i in range(n)])  6.7 us
  transfers between devices with their start and end apart: 6, of which 6 were waited for; matrix products, arithmetic and copies ran while one was open for 1% of the time, Pallas kernels for 2%

profile of v9, /device:TPU:1, one launch (start us, length us, event | category | flops | bytes accessed | tf_op | source)
XLA Modules:
  0.0 326.8 jit_solution(17969113311569376864)
XLA Ops:
  2.4 20.7 %all_to_all.30.weights_ref.second_ref = bf16[8,160,512]{2,1,0:T(8,128)(2,1)S(1)} all-to-all(bf16[8,160,512]{2,1,0:T(8,128)(2,1)S(1)} %shard_map.84), channel_id=1, replica_groups=mesh['z'=16,'xh'=2,'co'=2,'y'=4,'xl'=2] {'y','xl'}, dimensions={0} | all-to-all | bytes 2621440 | tf_op jit(solution)/shard_map/all_to_all | solution.py:20
  23.8 82.0 %all_to_all.31.one_ref = bf16[64,72,128]{2,1,0:T(8,128)(2,1)S(1)} all-to-all(bf16[64,72,128]{2,1,0:T(8,128)(2,1)S(1)} %shard_map.85), channel_id=1, replica_groups=mesh['z'=16,'xh'=2,'co'=2,'y'=4,'xl'=2] {'z','xh','co'}, dimensions={0} | all-to-all | bytes 2359296 | tf_op jit(solution)/shard_map/all_to_all | solution.py:20
  105.8 1.3 shard_map.86
  109.1 7.7 %all-to-all-start.2 = ((bf16[64,64,128]{2,1,0:T(8,128)(2,1)}), bf16[64,64,128]{2,1,0:T(8,128)(2,1)}, u32[]{:S(2)}, u32[]{:S(2)}) async-start(bf16[64,64,128]{2,1,0:T(8,128)(2,1)} %copy-done.8), calls=%async_computation.2 | async-start | bytes 2097152 | tf_op jit(solution)/shard_map/all_to_all | solution.py:20
  118.4 4.2 %all_gather.6 = bf16[2,512,64]{1,2,0:T(8,128)(2,1)S(1)} all-gather(bf16[1,512,64]{1,2,0:T(8,128)(2,1)S(1)} %copy.13), channel_id=1, replica_groups=mesh['z'=16,'xh'=2,'co'=2,'y'=4,'xl'=2] {'xl'}, dimensions={0}, use_global_device_ids=true | all-gather | bytes 196608 | tf_op jit(solution)/shard_map/all_gather | solution.py:26
  122.7 11.1 %all_gather.7 = bf16[8,512,64]{1,2,0:T(8,128)(2,1)S(1)} all-gather(bf16[2,512,64]{1,2,0:T(8,128)(2,1)S(1)} %all_gather.6), channel_id=1, replica_groups=mesh['z'=16,'xh'=2,'co'=2,'y'=4,'xl'=2] {'y'}, dimensions={0}, use_global_device_ids=true | all-gather | bytes 655360 | tf_op jit(solution)/shard_map/all_gather | solution.py:26
  136.0 1.3 copy-done.2
  138.3 32.4 %all-to-all-done.2.two_ref = bf16[64,64,128]{2,1,0:T(8,128)(2,1)} async-done(((bf16[64,64,128]{2,1,0:T(8,128)(2,1)}), bf16[64,64,128]{2,1,0:T(8,128)(2,1)}, u32[]{:S(2)}, u32[]{:S(2)}) %all-to-all-start.2) | async-done | bytes 1048608 | tf_op jit(solution)/shard_map/all_to_all | solution.py:20
  170.8 7.6 %all-to-all-start.3 = ((bf16[64,64,128]{2,1,0:T(8,128)(2,1)}), bf16[64,64,128]{2,1,0:T(8,128)(2,1)}, u32[]{:S(2)}, u32[]{:S(2)}) async-start(bf16[64,64,128]{2,1,0:T(8,128)(2,1)} %copy-done.7), calls=%async_computation.3 | async-start | bytes 2097152 | tf_op jit(solution)/shard_map/all_to_all | solution.py:20
  178.3 1.6 copy-done.3
  179.9 3.1 shard_map.88
  184.1 1.9 collective-permute-start
  186.0 9.4 %collective-permute-done = bf16[4,64,512]{2,1,0:T(8,128)(2,1)S(1)} collective-permute-done((bf16[4,64,512]{2,1,0:T(8,128)(2,1)}, bf16[4,64,512]{2,1,0:T(8,128)(2,1)S(1)}, u32[]{:S(2)}, u32[]{:S(2)}) %collective-permute-start) | collective-permute-done | bytes 262176 | tf_op jit(solution)/shard_map/ppermute | solution.py:32
  197.0 2.9 collective-permute-start.1
  199.9 7.4 %collective-permute-done.1 = f32[2,64,512]{2,1,0:T(8,128)} collective-permute-done((f32[2,64,512]{2,1,0:T(8,128)}, f32[2,64,512]{2,1,0:T(8,128)}, u32[]{:S(2)}, u32[]{:S(2)}) %collective-permute-start.1) | collective-permute-done | bytes 262176 | tf_op jit(solution)/shard_map/ppermute | solution.py:32
  208.5 1.9 collective-permute-start.2
  210.4 4.2 %collective-permute-done.2.got_ref = f32[64,512]{1,0:T(8,128)S(1)} collective-permute-done((f32[64,512]{1,0:T(8,128)S(1)}, f32[64,512]{1,0:T(8,128)S(1)}, u32[]{:S(2)}, u32[]{:S(2)}) %collective-permute-start.2) | collective-permute-done | bytes 131104 | tf_op jit(solution)/shard_map/ppermute | solution.py:32
  215.3 17.0 %all-to-all-done.3.grad_ref = bf16[64,64,128]{2,1,0:T(8,128)(2,1)} async-done(((bf16[64,64,128]{2,1,0:T(8,128)(2,1)}), bf16[64,64,128]{2,1,0:T(8,128)(2,1)}, u32[]{:S(2)}, u32[]{:S(2)}) %all-to-all-start.3) | async-done | bytes 1048608 | tf_op jit(solution)/shard_map/all_to_all | solution.py:20
  233.2 2.4 shard_map.89
  235.7 66.7 %all_to_all.32.back_ref.riders_ref = bf16[64,72,128]{2,1,0:T(8,128)(2,1)S(1)} all-to-all(bf16[64,72,128]{2,1,0:T(8,128)(2,1)S(1)} %get-tuple-element.37), channel_id=1, replica_groups=mesh['z'=16,'xh'=2,'co'=2,'y'=4,'xl'=2] {'z','xh','co'}, dimensions={0} | all-to-all | bytes 2359296 | tf_op jit(solution)/shard_map/all_to_all | solution.py:20
  304.2 4.4 %all-to-all-start.5 = ((bf16[8,160,512]{2,1,0:T(8,128)(2,1)}), bf16[8,160,512]{2,1,0:T(8,128)(2,1)}, u32[]{:S(2)}, u32[]{:S(2)}) async-start(bf16[8,160,512]{2,1,0:T(8,128)(2,1)} %copy-done.1), calls=%async_computation.5 | async-start | bytes 2621440 | tf_op jit(solution)/shard_map/all_to_all | solution.py:20
  309.4 1.8 shard_map.91
  311.2 13.5 %all-to-all-done.5.parts_ref = bf16[8,160,512]{2,1,0:T(8,128)(2,1)} async-done(((bf16[8,160,512]{2,1,0:T(8,128)(2,1)}), bf16[8,160,512]{2,1,0:T(8,128)(2,1)}, u32[]{:S(2)}, u32[]{:S(2)}) %all-to-all-start.5) | async-done | bytes 1310752 | tf_op jit(solution)/shard_map/all_to_all | solution.py:20
  324.6 2.2 shard_map.92
  (44 shorter events, 17.2 us)
Async XLA Ops:
  0.6 0.9 copy-start.11
  1.5 0.8 copy-start.14
  2.4 20.7 %copy-start = (bf16[1,1024,512]{2,1,0:T(8,128)(2,1)S(1)}, bf16[1,1024,512]{2,1,0:T(8,128)(2,1)}, u32[]{:S(2)}) copy-start(bf16[1,1024,512]{2,1,0:T(8,128)(2,1)} %param.5) | copy-start | bytes 3145732
  2.4 20.7 %copy-start.15 = (bf16[8,64]{1,0:T(8,128)(2,1)S(1)}, bf16[8,64]{1,0:T(8,128)(2,1)}, u32[]{:S(2)}) copy-start(bf16[8,64]{1,0:T(8,128)(2,1)} %gate_ref.1) | copy-start | bytes 3076
  107.1 1.0 copy-start.4
  108.1 1.0 copy-start.8
  109.1 61.7 %all-to-all-start.2 = ((bf16[64,64,128]{2,1,0:T(8,128)(2,1)}), bf16[64,64,128]{2,1,0:T(8,128)(2,1)}, u32[]{:S(2)}, u32[]{:S(2)}) async-start(bf16[64,64,128]{2,1,0:T(8,128)(2,1)} %copy-done.8), calls=%async_computation.2 | async-start | bytes 2097152 | tf_op jit(solution)/shard_map/all_to_all | solution.py:20
  134.0 1.2 copy-start.6
  136.0 1.3 copy-start.2
  137.3 1.0 copy-start.7
  170.8 61.5 %all-to-all-start.3 = ((bf16[64,64,128]{2,1,0:T(8,128)(2,1)}), bf16[64,64,128]{2,1,0:T(8,128)(2,1)}, u32[]{:S(2)}, u32[]{:S(2)}) async-start(bf16[64,64,128]{2,1,0:T(8,128)(2,1)} %copy-done.7), calls=%async_computation.3 | async-start | bytes 2097152 | tf_op jit(solution)/shard_map/all_to_all | solution.py:20
  178.3 1.6 copy-start.3
  183.1 1.0 copy-start.9
  184.1 11.3 %collective-permute-start = (bf16[4,64,512]{2,1,0:T(8,128)(2,1)}, bf16[4,64,512]{2,1,0:T(8,128)(2,1)S(1)}, u32[]{:S(2)}, u32[]{:S(2)}) collective-permute-start(bf16[4,64,512]{2,1,0:T(8,128)(2,1)} %get-tuple-element.32), channel_id=1, source_target_pairs={{0,1},{1,0},{2,3},{3,2},{4,5},{5,4},{6,7},{7,6},{8,9},{9,8},{10,11... | collective-permute-start | bytes 786440 | tf_op jit(solution)/shard_map/ppermute | solution.py:32
  195.5 0.8 copy-start.16
  196.3 36.0 %copy-start.5 = (bf16[8,128,512]{2,1,0:T(8,128)(2,1)S(1)}, bf16[8,128,512]{2,1,0:T(8,128)(2,1)}, u32[]{:S(2)}) copy-start(bf16[8,128,512]{2,1,0:T(8,128)(2,1)} %copy-done.4) | copy-start | bytes 3145732
  197.0 10.3 %collective-permute-start.1 = (f32[2,64,512]{2,1,0:T(8,128)}, f32[2,64,512]{2,1,0:T(8,128)}, u32[]{:S(2)}, u32[]{:S(2)}) collective-permute-start(f32[2,64,512]{2,1,0:T(8,128)} %slice_select_fusion), channel_id=1, source_target_pairs={{0,4},{2,6},{4,0},{6,2},{1,5},{3,7},{5,1},{7,3},{8,12},{10,14},{12... | collective-permute-start | bytes 786440 | tf_op jit(solution)/shard_map/ppermute | solution.py:32
  208.5 6.1 %collective-permute-start.2 = (f32[64,512]{1,0:T(8,128)S(1)}, f32[64,512]{1,0:T(8,128)S(1)}, u32[]{:S(2)}, u32[]{:S(2)}) collective-permute-start(f32[64,512]{1,0:T(8,128)S(1)} %get-tuple-element.44), channel_id=1, source_target_pairs={{0,2},{2,0},{4,6},{6,4},{1,3},{3,1},{5,7},{7,5},{8,10},{10,8},{12,... | collective-permute-start | bytes 393224 | tf_op jit(solution)/shard_map/ppermute | solution.py:32
  214.6 0.7 copy-start.12
  232.3 0.9 copy-start.13
  303.2 1.1 copy-start.1
  304.2 5.2 %copy-start.10 = (bf16[2,512,512]{2,1,0:T(8,128)(2,1)S(1)}, bf16[2,512,512]{2,1,0:T(8,128)(2,1)}, u32[]{:S(2)}) copy-start(bf16[2,512,512]{2,1,0:T(8,128)(2,1)} %copy-done.9) | copy-start | bytes 3145732
  304.2 20.4 %all-to-all-start.5 = ((bf16[8,160,512]{2,1,0:T(8,128)(2,1)}), bf16[8,160,512]{2,1,0:T(8,128)(2,1)}, u32[]{:S(2)}, u32[]{:S(2)}) async-start(bf16[8,160,512]{2,1,0:T(8,128)(2,1)} %copy-done.1), calls=%async_computation.5 | async-start | bytes 2621440 | tf_op jit(solution)/shard_map/all_to_all | solution.py:20
